TPU v7x, 32 devices: a whole 2x2x4 slice. The times are simulated.
32 devices in a mesh: dp: 2 (over y), expert: 16 (over z, x, core).
Axes of the slice: x: 2, y: 2, z: 4, core: 2. Of those that a mesh axis runs over, the one named last changes fastest.
Arguments:
- tokens: bfloat16 [1024, 2048], P(('dp', 'expert')), may hold values from -6 to 6
- cotangent: bfloat16 [1024, 2048], P(('dp', 'expert')), may hold values from -0.29882812 to 0.29882812
- routes: int32 [1024, 8], P(('dp', 'expert')), may hold values from 0 to 15, all different within a row; in each aligned block of 32 rows (0 to 31, 32 to 63, ...) at most 32 rows name the same one
- combine: float32 [1024, 8], P(('dp', 'expert')), may hold values from 0.05 to 0.5
- w_in: bfloat16 [16, 2, 512, 2048], P('expert', None, 'dp'), may hold values from -0.125 to 0.125
- w_out: bfloat16 [16, 512, 2048], P('expert', 'dp'), may hold values from -0.25 to 0.25
- v_in: bfloat16 [16, 2, 512, 2048], P('expert', None, 'dp'), may hold values from -0.125 to 0.125
Outputs:
- hvp: float32 [16, 2, 512, 2048], P('expert', None, 'dp')
Inputs may be any that keep to these rules, and one draw needn't show every extreme that they name: `routes`: each token names 8 different experts. Among the tokens of one device no expert is named more than 32 times, and on some device an expert is named exactly 32 times.
All inputs are finite; a program needn't handle non-finite values.
Results may differ from a plain program's by a relative error of at most 0.015.
Values may be sent and summed in bfloat16 or wider, within the bound.
No kernel may reach another device: no remote copies, remote signals or barrier semaphores. Data moves between devices by JAX's collectives and lax.ppermute only.
A program may use at most 128 MiB of HBM per device.

v0:
```python
import jax
import jax.numpy as jnp
from jax import lax
from jax.sharding import PartitionSpec as P


def expert_terms(slot_rows, slot_grads, w_pair, v_pair, w_down):
    hidden_width = w_pair.shape[1]
    model_dim = w_pair.shape[2]
    stacked = jnp.concatenate([w_pair, v_pair], axis=0).reshape(4 * hidden_width, model_dim)
    projected = lax.dot_general(
        slot_rows, stacked, (((1,), (1,)), ((), ())), preferred_element_type=jnp.float32
    )
    pre_gate = projected[:, :hidden_width]
    pre_up = projected[:, hidden_width : 2 * hidden_width]
    tan_gate = projected[:, 2 * hidden_width : 3 * hidden_width]
    tan_up = projected[:, 3 * hidden_width :]
    back_grad = lax.dot_general(
        slot_grads, w_down, (((1,), (1,)), ((), ())), preferred_element_type=jnp.float32
    )
    gate_sig = jax.nn.sigmoid(pre_gate)
    first_deriv = gate_sig * (1.0 + pre_gate * (1.0 - gate_sig))
    second_deriv = gate_sig * (1.0 - gate_sig) * (2.0 + pre_gate * (1.0 - 2.0 * gate_sig))
    gate_dir = (back_grad * (tan_up * first_deriv + pre_up * second_deriv * tan_gate)).astype(
        jnp.bfloat16
    )
    up_dir = (back_grad * first_deriv * tan_gate).astype(jnp.bfloat16)
    gate_term = lax.dot_general(
        gate_dir, slot_rows, (((0,), (0,)), ((), ())), preferred_element_type=jnp.float32
    )
    up_term = lax.dot_general(
        up_dir, slot_rows, (((0,), (0,)), ((), ())), preferred_element_type=jnp.float32
    )
    return jnp.stack([gate_term, up_term], axis=0)


def local(tokens, cotangent, routes, combine, w_in, w_out, v_in):
    n_expert = lax.axis_size("expert")
    exp_dev = w_in.shape[0]
    experts = n_expert * exp_dev
    tok_dev, top_k = routes.shape
    model_dim = tokens.shape[1]
    capacity = 2 * tok_dev * top_k // experts
    pair_count = tok_dev * top_k
    slot_count = n_expert * capacity
    flat_routes = routes.reshape(pair_count)
    onehot = (flat_routes[:, None] == jnp.arange(experts, dtype=jnp.int32)[None, :]).astype(
        jnp.int32
    )
    earlier = jnp.cumsum(onehot, axis=0) - onehot
    slot_rank = jnp.sum(earlier * onehot, axis=1)
    position = flat_routes * capacity + slot_rank
    slot_table = jnp.full((experts * capacity,), pair_count, jnp.int32)
    slot_table = slot_table.at[position].set(jnp.arange(pair_count, dtype=jnp.int32))
    token_index = slot_table // top_k
    padded_tokens = jnp.concatenate([tokens, jnp.zeros((1, model_dim), jnp.bfloat16)], axis=0)
    scaled = (combine[:, :, None] * cotangent[:, None, :].astype(jnp.float32)).astype(jnp.bfloat16)
    padded_scaled = jnp.concatenate(
        [scaled.reshape(pair_count, model_dim), jnp.zeros((1, model_dim), jnp.bfloat16)], axis=0
    )
    send_rows = padded_tokens[token_index].reshape(n_expert, exp_dev * capacity, model_dim)
    send_grads = padded_scaled[slot_table].reshape(n_expert, exp_dev * capacity, model_dim)
    recv_rows = lax.all_to_all(send_rows, "expert", split_axis=0, concat_axis=0, tiled=True)
    recv_grads = lax.all_to_all(send_grads, "expert", split_axis=0, concat_axis=0, tiled=True)

    def regroup(received):
        shaped = received.reshape(n_expert, exp_dev, capacity, model_dim)
        return jnp.transpose(shaped, (1, 0, 2, 3)).reshape(exp_dev, slot_count, model_dim)

    local_rows = regroup(recv_rows)
    local_grads = regroup(recv_grads)
    batched_terms = jax.vmap(expert_terms)
    pair_piece, probe_piece, down_piece = lax.all_gather(
        (w_in, v_in, w_out[:, None]), "dp", axis=2, tiled=True
    )
    partials = batched_terms(local_rows, local_grads, pair_piece, probe_piece, down_piece[:, 0])
    return lax.psum_scatter(
        partials.astype(jnp.bfloat16), "dp", scatter_dimension=2, tiled=True
    ).astype(jnp.float32)


def solution(mesh):
    in_specs = (
        P(("dp", "expert"), None),
        P(("dp", "expert"), None),
        P(("dp", "expert"), None),
        P(("dp", "expert"), None),
        P("expert", None, "dp", None),
        P("expert", "dp", None),
        P("expert", None, "dp", None),
    )
    out_specs = P("expert", None, "dp", None)
    return jax.shard_map(local, mesh=mesh, in_specs=in_specs, out_specs=out_specs, check_vma=False)
```

profile of v0, /device:TPU:0, one launch (start us, length us, event | category | flops | bytes accessed | tf_op | source)
XLA Modules:
  0.0 250.7 jit_solution(13350500371979342378)
XLA Ops:
  6.5 0.0 copy-start.2
  6.5 0.0 copy-start.3
  6.5 0.0 copy-start
  6.5 0.0 all-gather.9.cloned.1.call-start
  6.5 0.7 all-gather.9.cloned.1.call-update
  7.3 0.0 all-gather.5.cloned.1.call-start
  7.3 0.7 all-gather.5.cloned.1.call-update
  8.0 0.0 copy-done.2
  8.0 0.1 copy.10
  8.1 0.1 eq.29
  8.2 0.1 eq.25
  8.3 0.1 copy.9
  8.4 0.1 mul.80
  8.5 0.6 reduce-window.6
  9.1 0.2 slice_reduce_fusion
  9.3 0.0 copy-done.3
  9.3 0.1 copy.8
  9.4 0.1 mul.73
  9.5 0.0 copy-done
  9.5 0.2 fusion.4
  9.7 0.1 concatenate.9
  9.8 0.1 fusion.23
  9.9 1.4 scatter_custom_fusion
  11.3 3.3 %gather_fusion = bf16[512,2048]{1,0:T(8,128)(2,1)} fusion(bf16[257,2048]{1,0:T(8,128)(2,1)S(1)} %concatenate.9, s32[1024]{0:T(1024)S(1)} %get-tuple-element.8), kind=kCustom, calls=%fused_computation | custom fusion | bytes 4196352 | tf_op jit(solution)/shard_map/gather | solution.py:62
  14.6 7.4 %all-to-all-start = ((bf16[16,32,2048]{2,1,0:T(8,128)(2,1)}), bf16[16,32,2048]{2,1,0:T(8,128)(2,1)S(1)}, u32[]{:S(2)}, u32[]{:S(2)}) async-start(bf16[16,32,2048]{2,1,0:T(8,128)(2,1)} %bitcast.4), calls=%async_computation | async-start | bytes 4194304 | tf_op jit(solution)/shard_map/all_to_all | solution.py:64
  22.0 0.0 copy-start.1
  22.0 0.0 all-gather.7.cloned.1.call-start
  22.0 0.7 all-gather.7.cloned.1.call-update
  22.7 0.2 copy-done.1
  22.9 3.3 %gather_fusion.1 = bf16[512,2048]{1,0:T(8,128)(2,1)} fusion(bf16[33,2048]{1,0:T(8,128)(2,1)S(1)} %concatenate.10, s32[1024]{0:T(1024)S(1)} %get-tuple-element.7), kind=kCustom, calls=%fused_computation.1 | custom fusion | bytes 4196352 | tf_op jit(solution)/shard_map/gather | solution.py:61
  26.2 36.9 %all-to-all-done = bf16[16,32,2048]{2,1,0:T(8,128)(2,1)S(1)} async-done(((bf16[16,32,2048]{2,1,0:T(8,128)(2,1)}), bf16[16,32,2048]{2,1,0:T(8,128)(2,1)S(1)}, u32[]{:S(2)}, u32[]{:S(2)}) %all-to-all-start) | async-done | bytes 2097184 | tf_op jit(solution)/shard_map/all_to_all | solution.py:64
  63.1 11.3 %all-to-all-start.1 = ((bf16[16,32,2048]{2,1,0:T(8,128)(2,1)}), bf16[16,32,2048]{2,1,0:T(8,128)(2,1)}, u32[]{:S(2)}, u32[]{:S(2)}) async-start(bf16[16,32,2048]{2,1,0:T(8,128)(2,1)} %bitcast.8), calls=%async_computation.1 | async-start | bytes 4194304 | tf_op jit(solution)/shard_map/all_to_all | solution.py:63
  74.3 0.0 reduce-scatter.2.cloned.1.call-start
  74.4 0.0 all-gather.9.cloned.1.call-done
  74.4 2.9 %fusion.5 = f32[1,512,512]{2,1,0:T(8,128)S(1)} fusion(bf16[512,2048]{1,0:T(8,128)(2,1)S(1)} %bitcast.58, bf16[1,512,2048]{2,1,0:T(8,128)(2,1)} %all-gather.9.cloned.1.call-done), kind=kOutput, calls=%fused_computation.16 | convolution fusion | flops 1073741824 | bytes 5242880 | tf_op jit(solution)/shard_map/vmap()/dot_general | solution.py:18
  77.3 25.8 %all-gather.5.cloned.1.call-done = bf16[1,2,512,2048]{3,2,1,0:T(8,128)(2,1)} async-done(((bf16[1,2,256,2048]{3,2,1,0:T(8,128)(2,1)}), bf16[1,2,512,2048]{3,2,1,0:T(8,128)(2,1)}) %all-gather.5.cloned.1.call-update) | async-done | bytes 4194320 | tf_op jit(solution)/shard_map/all_gather | solution.py:73
  103.1 58.3 %all-gather.7.cloned.1.call-done = bf16[1,2,512,2048]{3,2,1,0:T(8,128)(2,1)} async-done(((bf16[1,2,256,2048]{3,2,1,0:T(8,128)(2,1)}), bf16[1,2,512,2048]{3,2,1,0:T(8,128)(2,1)}) %all-gather.7.cloned.1.call-update) | async-done | bytes 4194320 | tf_op jit(solution)/shard_map/all_gather | solution.py:73
  161.4 7.4 %pad_maximum_fusion = bf16[1,4,512,2048]{3,2,1,0:T(8,128)(2,1)} fusion(bf16[1,2,512,2048]{3,2,1,0:T(8,128)(2,1)} %all-gather.7.cloned.1.call-done, bf16[1,2,512,2048]{3,2,1,0:T(8,128)(2,1)} %all-gather.5.cloned.1.call-done), kind=kLoop, calls=%fused_computation.3 | loop fusion | flops 4194304 | bytes 16777216 | tf_op jit(solution)/shard_map/vmap()/concatenate | solution.py:10
  168.8 0.0 all-to-all-done.1
  168.8 7.6 %convolution_bitcast_fusion = f32[1,512,2048]{2,1,0:T(8,128)S(1)} fusion(bf16[512,2048]{1,0:T(8,128)(2,1)} %bitcast.9, bf16[2048,2048]{1,0:T(8,128)(2,1)} %bitcast.57), kind=kOutput, calls=%fused_computation.5 | convolution fusion | flops 4294967296 | bytes 14680064 | tf_op jit(solution)/shard_map/vmap()/dot_general | solution.py:11
  176.5 3.5 %fusion = bf16[1,1,512,2048]{3,2,1,0:T(8,128)(2,1)S(1)} fusion(bf16[512,2048]{1,0:T(8,128)(2,1)} %bitcast.9, f32[1,512,512]{2,1,0:T(8,128)S(1)} %fusion.5, f32[1,512,2048]{2,1,0:T(8,128)S(1)} %convolution_bitcast_fusion), kind=kOutput, calls=%fused_computation.8 | convolution fusion | flops 1079771136 | bytes 9437184 | tf_op jit(solution)/shard_map/vmap()/dot_general | solution.py:28
  180.0 3.1 %fusion.1 = bf16[1,1,512,2048]{3,2,1,0:T(8,128)(2,1)S(1)} fusion(bf16[512,2048]{1,0:T(8,128)(2,1)} %bitcast.9, f32[1,512,2048]{2,1,0:T(8,128)S(1)} %convolution_bitcast_fusion, f32[1,512,512]{2,1,0:T(8,128)S(1)} %fusion.5), kind=kOutput, calls=%fused_computation.9 | convolution fusion | flops 1077411840 | bytes 7340032 | tf_op jit(solution)/shard_map/vmap()/dot_general | solution.py:31
  183.1 2.4 maximum_bitcast_fusion
  185.5 0.0 reduce-scatter.2.cloned.1.call-update
  185.5 54.4 %reduce-scatter.2.cloned.1.call-done = bf16[1,2,256,2048]{3,2,1,0:T(8,128)(2,1)} async-done(((bf16[1,2,512,2048]{3,2,1,0:T(8,128)(2,1)}), bf16[1,2,256,2048]{3,2,1,0:T(8,128)(2,1)}) %reduce-scatter.2.cloned.1.call-update) | async-done | bytes 2097168 | tf_op jit(solution)/shard_map/reduce_scatter | solution.py:77
  240.0 4.1 %convert_element_type.43 = f32[1,2,256,2048]{3,2,1,0:T(8,128)} convert(bf16[1,2,256,2048]{3,2,1,0:T(8,128)(2,1)} %reduce-scatter.2.cloned.1.call-done) | non-fusion elementwise | flops 1048576 | bytes 6291456 | tf_op jit(solution)/shard_map/convert_element_type | solution.py:79
  (10 shorter events, 0.1 us)
Async XLA Ops:
  6.5 1.5 copy-start.2
  6.5 2.8 %copy-start.3 = (f32[32,8]{0,1:T(8,128)S(1)}, f32[32,8]{0,1:T(8,128)}, u32[]{:S(2)}) copy-start(f32[32,8]{0,1:T(8,128)} %param.10) | copy-start | bytes 3076
  6.5 2.9 %copy-start = (bf16[32,2048]{1,0:T(8,128)(2,1)S(1)}, bf16[32,2048]{1,0:T(8,128)(2,1)}, u32[]{:S(2)}) copy-start(bf16[32,2048]{1,0:T(8,128)(2,1)} %param.8) | copy-start | bytes 393220
  6.5 67.9 %all-gather.9.cloned.1.call-start = ((), (), s32[]{:S(2)}) async-start(), calls=%async_computation.6 | async-start | bytes 3145728 | tf_op jit(solution)/shard_map/all_gather | solution.py:73
  7.3 95.8 %all-gather.5.cloned.1.call-start = ((), (), s32[]{:S(2)}) async-start(), calls=%async_computation.3 | async-start | bytes 6291456 | tf_op jit(solution)/shard_map/all_gather | solution.py:73
  14.6 48.5 %all-to-all-start = ((bf16[16,32,2048]{2,1,0:T(8,128)(2,1)}), bf16[16,32,2048]{2,1,0:T(8,128)(2,1)S(1)}, u32[]{:S(2)}, u32[]{:S(2)}) async-start(bf16[16,32,2048]{2,1,0:T(8,128)(2,1)} %bitcast.4), calls=%async_computation | async-start | bytes 4194304 | tf_op jit(solution)/shard_map/all_to_all | solution.py:64
  22.0 0.9 copy-start.1
  22.0 139.4 %all-gather.7.cloned.1.call-start = ((), (), s32[]{:S(2)}) async-start(), calls=%async_computation.4 | async-start | bytes 6291456 | tf_op jit(solution)/shard_map/all_gather | solution.py:73
  63.1 105.8 %all-to-all-start.1 = ((bf16[16,32,2048]{2,1,0:T(8,128)(2,1)}), bf16[16,32,2048]{2,1,0:T(8,128)(2,1)}, u32[]{:S(2)}, u32[]{:S(2)}) async-start(bf16[16,32,2048]{2,1,0:T(8,128)(2,1)} %bitcast.8), calls=%async_computation.1 | async-start | bytes 4194304 | tf_op jit(solution)/shard_map/all_to_all | solution.py:63
  74.3 165.6 %reduce-scatter.2.cloned.1.call-start = ((), (), s32[]{:S(2)}) async-start(), calls=%async_computation.5 | async-start | bytes 6291456 | tf_op jit(solution)/shard_map/reduce_scatter | solution.py:77
Sparse Core Ops, SparseCore 0:
  8.9 35.8 all-gather.8
  46.3 56.7 all-gather.4
  104.6 56.7 all-gather.6
  185.7 54.2 reduce-scatter.1
where the time goes:
time: 251 us
  waiting for transfers between devices  178 us (71%)
  starting transfers between devices  18.7 us (7%)
  matrix products  17.2 us (7%)
  other arithmetic  14.9 us (6%)
  between operations  13.3 us (5%)
  local copies, waits for them, and re-layouts  9.01 us (4%)
    all_gather x3, waiting for transfers between devices, local(): lax.all_gather((w_in, v_in, w_out[:, None]), 'dp', axis=2, tiled=True)  84.1 us
    reduce_scatter x1, waiting for transfers between devices, local(): lax.psum_scatter(partials.astype(jnp.bfloat16), 'dp', scatter_dimension=2...  54.4 us
    all_to_all x1, waiting for transfers between devices, local(): lax.all_to_all(send_grads, 'expert', split_axis=0, concat_axis=0, tiled=T...  36.9 us
    all_to_all x1, starting transfers between devices, local(): lax.all_to_all(send_rows, 'expert', split_axis=0, concat_axis=0, tiled=True)  11.3 us
    dot_general x1, matrix products, expert_terms(): lax.dot_general(slot_rows, stacked, (((1,), (1,)), ((), ())), preferred_e...  7.63 us
    concatenate x1, other arithmetic, expert_terms(): jnp.concatenate([w_pair, v_pair], axis=0)  7.42 us
    all_to_all x1, starting transfers between devices, local(): lax.all_to_all(send_grads, 'expert', split_axis=0, concat_axis=0, tiled=T...  7.36 us
  transfers between devices with their start and end apart: 6, of which 4 were waited for; matrix products, arithmetic and copies ran while one was open for 8% of the time, Pallas kernels for 0%

commit v1 on v0

--- a/solution.py
+++ b/solution.py
@@ -1,30 +1,25 @@
 import jax
 import jax.numpy as jnp
 from jax import lax
+from jax.experimental import pallas as pl
+from jax.experimental.pallas import tpu as pltpu
 from jax.sharding import PartitionSpec as P
+
+NT = (((1,), (1,)), ((), ()))
+NN = (((1,), (0,)), ((), ()))
 
 
 def expert_terms(slot_rows, slot_grads, w_pair, v_pair, w_down):
     hidden_width = w_pair.shape[1]
     model_dim = w_pair.shape[2]
     stacked = jnp.concatenate([w_pair, v_pair], axis=0).reshape(4 * hidden_width, model_dim)
-    projected = lax.dot_general(
-        slot_rows, stacked, (((1,), (1,)), ((), ())), preferred_element_type=jnp.float32
-    )
+    projected = lax.dot_general(slot_rows, stacked, NT, preferred_element_type=jnp.float32)
     pre_gate = projected[:, :hidden_width]
     pre_up = projected[:, hidden_width : 2 * hidden_width]
     tan_gate = projected[:, 2 * hidden_width : 3 * hidden_width]
     tan_up = projected[:, 3 * hidden_width :]
-    back_grad = lax.dot_general(
-        slot_grads, w_down, (((1,), (1,)), ((), ())), preferred_element_type=jnp.float32
-    )
-    gate_sig = jax.nn.sigmoid(pre_gate)
-    first_deriv = gate_sig * (1.0 + pre_gate * (1.0 - gate_sig))
-    second_deriv = gate_sig * (1.0 - gate_sig) * (2.0 + pre_gate * (1.0 - 2.0 * gate_sig))
-    gate_dir = (back_grad * (tan_up * first_deriv + pre_up * second_deriv * tan_gate)).astype(
-        jnp.bfloat16
-    )
-    up_dir = (back_grad * first_deriv * tan_gate).astype(jnp.bfloat16)
+    back_grad = lax.dot_general(slot_grads, w_down, NT, preferred_element_type=jnp.float32)
+    gate_dir, up_dir = directions(pre_gate, pre_up, tan_gate, tan_up, back_grad)
     gate_term = lax.dot_general(
         gate_dir, slot_rows, (((0,), (0,)), ((), ())), preferred_element_type=jnp.float32
     )
@@ -34,7 +29,16 @@
     return jnp.stack([gate_term, up_term], axis=0)
 
 
-def local(tokens, cotangent, routes, combine, w_in, w_out, v_in):
+def directions(pre_gate, pre_up, tan_gate, tan_up, back_grad):
+    gate_sig = jax.nn.sigmoid(pre_gate)
+    first_deriv = gate_sig * (1.0 + pre_gate * (1.0 - gate_sig))
+    second_deriv = gate_sig * (1.0 - gate_sig) * (2.0 + pre_gate * (1.0 - 2.0 * gate_sig))
+    gate_dir = back_grad * (tan_up * first_deriv + pre_up * second_deriv * tan_gate)
+    up_dir = back_grad * first_deriv * tan_gate
+    return gate_dir.astype(jnp.bfloat16), up_dir.astype(jnp.bfloat16)
+
+
+def dispatched(tokens, cotangent, routes, combine, w_in, w_out, v_in):
     n_expert = lax.axis_size("expert")
     exp_dev = w_in.shape[0]
     experts = n_expert * exp_dev
@@ -79,6 +83,78 @@
     ).astype(jnp.float32)
 
 
+def dense_kernel(x_ref, c_ref, wt_ref, w_ref, v_ref, wo_ref, out_ref):
+    half = w_ref.shape[0] // 2
+    x = x_ref[...]
+    pre = lax.dot_general(w_ref[...], x, NT, preferred_element_type=jnp.float32)
+    tan = lax.dot_general(v_ref[...], x, NT, preferred_element_type=jnp.float32)
+    back = lax.dot_general(wo_ref[...], c_ref[...], NT, preferred_element_type=jnp.float32)
+    back = back * wt_ref[...]
+    gate_dir, up_dir = directions(pre[:half], pre[half:], tan[:half], tan[half:], back)
+    gate = lax.dot_general(gate_dir, x, NN, preferred_element_type=jnp.float32)
+    up = lax.dot_general(up_dir, x, NN, preferred_element_type=jnp.float32)
+
+    @pl.when(pl.program_id(0) == 0)
+    def _():
+        out_ref[0:half, :] = gate
+        out_ref[half:, :] = up
+
+    @pl.when(pl.program_id(0) != 0)
+    def _():
+        out_ref[0:half, :] += gate
+        out_ref[half:, :] += up
+
+
+def dense(tokens, cotangent, routes, combine, w_in, w_out, v_in):
+    axes = ("dp", "expert")
+    experts = lax.axis_size("expert")
+    model_dim = tokens.shape[1]
+    half = w_in.shape[2]
+    named = routes[:, :, None] == jnp.arange(experts, dtype=jnp.int32)[None, None, :]
+    weights = jnp.sum(jnp.where(named, combine[:, :, None], 0.0), axis=1)
+    weights = lax.all_gather(weights, axes, axis=0, tiled=True)
+    x = lax.all_gather(tokens, axes, axis=0, tiled=True)
+    c = lax.all_gather(cotangent, axes, axis=0, tiled=True)
+    mine = jnp.arange(experts, dtype=jnp.int32)[None, :] == lax.axis_index("expert")
+    column = jnp.sum(jnp.where(mine, weights, 0.0), axis=1)[None, :]
+    rows = x.shape[0]
+    chunk = 256
+    out = pl.pallas_call(
+        dense_kernel,
+        grid=(rows // chunk,),
+        in_specs=[
+            pl.BlockSpec((chunk, model_dim), lambda i: (i, 0)),
+            pl.BlockSpec((chunk, model_dim), lambda i: (i, 0)),
+            pl.BlockSpec((1, chunk), lambda i: (0, i)),
+            pl.BlockSpec((2 * half, model_dim), lambda i: (0, 0)),
+            pl.BlockSpec((2 * half, model_dim), lambda i: (0, 0)),
+            pl.BlockSpec((half, model_dim), lambda i: (0, 0)),
+        ],
+        out_specs=pl.BlockSpec((2 * half, model_dim), lambda i: (0, 0)),
+        out_shape=jax.ShapeDtypeStruct((2 * half, model_dim), jnp.float32),
+        compiler_params=pltpu.CompilerParams(vmem_limit_bytes=48 * 2**20),
+        cost_estimate=pl.CostEstimate(
+            flops=2 * rows * model_dim * 7 * half, bytes_accessed=17 * 2**20, transcendentals=rows * half
+        ),
+    )(
+        x,
+        c,
+        column,
+        w_in.reshape(2 * half, model_dim),
+        v_in.reshape(2 * half, model_dim),
+        w_out.reshape(half, model_dim),
+    )
+    return out.reshape(1, 2, half, model_dim)
+
+
+def local(tokens, cotangent, routes, combine, w_in, w_out, v_in):
+    experts = lax.axis_size("expert") * w_in.shape[0]
+    tok_dev, top_k = routes.shape
+    if w_in.shape[0] == 1 and 2 * tok_dev * top_k // experts >= tok_dev:
+        return dense(tokens, cotangent, routes, combine, w_in, w_out, v_in)
+    return dispatched(tokens, cotangent, routes, combine, w_in, w_out, v_in)
+
+
 def solution(mesh):
     in_specs = (
         P(("dp", "expert"), None),

time: 251 us -> 166 us (0.66)
  waiting for transfers between devices: 178 us -> 86.7 us
  blocking collectives: 0 us -> 44.3 us
  starting transfers between devices: 18.7 us -> 0.04 us
  matrix products: 17.2 us -> 0 us
  Pallas kernels: 0 us -> 16.2 us
  other arithmetic: 14.9 us -> 0.81 us
  local copies, waits for them, and re-layouts: 9.01 us -> 4.63 us
    reduce_scatter x1 -> x0, waiting for transfers between devices: 54.4 us -> none  [local(): lax.psum_scatter(partials.astype(jnp.bfloat16), 'dp', scatter_dimension=2...]
    all_gather x0 -> x1, blocking collectives: none -> 44.3 us  [dense(): weights = lax.all_gather(weights, axes, axis=0, tiled=True)]
    all_to_all x2 -> x0, waiting for transfers between devices: 36.9 us -> none  [the longest x1 36.9 us: local(): lax.all_to_all(send_grads, 'expert', split_axis=0, concat_axis=0, tiled=T...]
    all_to_all x2 -> x0, starting transfers between devices: 18.6 us -> none  [the longest x1 11.3 us: local(): lax.all_to_all(send_rows, 'expert', split_axis=0, concat_axis=0, tiled=True)]
    dot_general x4 -> x0, matrix products: 17.2 us -> none  [the longest x1 7.63 us: expert_terms(): lax.dot_general(slot_rows, stacked, (((1,), (1,)), ((), ())), preferred_e...]
    pallas_call x0 -> x1, Pallas kernels: none -> 16.2 us  [dense(): pl.pallas_call(dense_kernel, grid=(rows // chunk,), in_specs=[pl.BlockSpe...]
    concatenate x1 -> x0, other arithmetic: 7.42 us -> none  [expert_terms(): jnp.concatenate([w_pair, v_pair], axis=0)]
    convert_element_type x5 -> x0, other arithmetic: 6.71 us -> none  [the longest x1 4.13 us: local(): return lax.psum_scatter(partials.astype(jnp.bfloat16), 'dp', scatter_dime...]
  transfers between devices with their start and end apart: 6 -> 2, of which waited for: 4 -> 2; matrix products, arithmetic and copies ran while one was open for 8% -> 1% of each run, Pallas kernels for 0% -> 0%
where the time goes in v1:
time: 166 us
  waiting for transfers between devices  86.7 us (52%)
  blocking collectives  44.3 us (27%)
  Pallas kernels  16.2 us (10%)
  between operations  13.4 us (8%)
  local copies, waits for them, and re-layouts  4.63 us (3%)
    all_gather x1, waiting for transfers between devices, dense(): c = lax.all_gather(cotangent, axes, axis=0, tiled=True)  63.5 us
    all_gather x1, blocking collectives, dense(): weights = lax.all_gather(weights, axes, axis=0, tiled=True)  44.3 us
    all_gather x1, waiting for transfers between devices, dense(): x = lax.all_gather(tokens, axes, axis=0, tiled=True)  21.8 us
    pallas_call x1, Pallas kernels, dense(): pl.pallas_call(dense_kernel, grid=(rows // chunk,), in_specs=[pl.BlockSpe...  16.2 us
    unnamed x7, local copies, waits for them, and re-layouts  4.55 us
  transfers between devices with their start and end apart: 2, of which 2 were waited for; matrix products, arithmetic and copies ran while one was open for 1% of the time, Pallas kernels for 0%

profile of v1, /device:TPU:0, one launch (start us, length us, event | category | flops | bytes accessed | tf_op | source)
XLA Modules:
  0.0 166.1 jit_solution(9997018942427056140)
XLA Ops:
  6.5 0.0 all-gather.4.cloned.1.call-start
  6.5 0.7 all-gather.4.cloned.1.call-update
  7.3 0.0 all-gather.6.cloned.1.call-start
  7.3 0.7 all-gather.6.cloned.1.call-update
  8.0 0.7 select_reduce_fusion.1
  8.7 44.3 %all-gather = f32[32,32,16]{1,2,0:T(8,128)S(1)} all-gather(f32[1,32,16]{1,2,0:T(8,128)S(1)} %bitcast.12), channel_id=1, replica_groups=mesh['dp'=2,'expert'=16] {'dp','expert'}, dimensions={0}, use_global_device_ids=true | all-gather | bytes 67584 | tf_op jit(solution)/shard_map/all_gather | solution.py:115
  53.1 0.1 copy.15
  53.2 0.1 reshape.24
  53.3 0.1 select_reduce_fusion
  53.4 21.8 %all-gather.4.cloned.1.call-done.x_ref = bf16[1024,2048]{1,0:T(8,128)(2,1)} async-done(((bf16[32,2048]{1,0:T(8,128)(2,1)}), bf16[1024,2048]{1,0:T(8,128)(2,1)}) %all-gather.4.cloned.1.call-update) | async-done | bytes 4194320 | tf_op jit(solution)/shard_map/all_gather | solution.py:116
  75.2 63.5 %all-gather.6.cloned.1.call-done.c_ref = bf16[1024,2048]{1,0:T(8,128)(2,1)} async-done(((bf16[32,2048]{1,0:T(8,128)(2,1)}), bf16[1024,2048]{1,0:T(8,128)(2,1)}) %all-gather.6.cloned.1.call-update) | async-done | bytes 4194320 | tf_op jit(solution)/shard_map/all_gather | solution.py:117
  138.7 0.0 copy-start
  138.7 1.6 copy-done
  140.3 0.0 copy-start.1
  140.3 1.6 copy-done.1
  141.9 0.0 copy-start.2
  141.9 1.2 copy-done.2
  143.1 16.2 %shard_map.73 = f32[512,2048]{1,0:T(8,128)} custom-call(bf16[1024,2048]{1,0:T(8,128)(2,1)} %all-gather.4.cloned.1.call-done.x_ref, bf16[1024,2048]{1,0:T(8,128)(2,1)} %all-gather.6.cloned.1.call-done.c_ref, f32[1,1024]{1,0:T(1,128)S(1)} %bitcast.8, bf16[512,2048]{1,0:T(8,128)(2,1)S(1)} %bitcast.9, bf16[512,2048]{1,0:T(8,128)(2,1)S(1)} %bitcast.10, ...), custom_call_target="tpu_custom_call" | custom-call | flops 7516192768 | bytes 17825792 | tf_op jit(solution)/shard_map/pallas_call | solution.py:122
  (1 shorter events, 0.0 us)
Async XLA Ops:
  6.5 68.7 %all-gather.4.cloned.1.call-start = ((), (), s32[]{:S(2)}) async-start(), calls=%async_computation | async-start | bytes 4325376 | tf_op jit(solution)/shard_map/all_gather | solution.py:116
  7.3 131.4 %all-gather.6.cloned.1.call-start = ((), (), s32[]{:S(2)}) async-start(), calls=%async_computation.1 | async-start | bytes 4325376 | tf_op jit(solution)/shard_map/all_gather | solution.py:117
  138.7 1.6 copy-start
  140.3 1.6 copy-start.1
  141.9 1.2 copy-start.2
Sparse Core Ops, SparseCore 0:
  10.2 64.9 all-gather.3
  78.0 60.6 all-gather.5

commit v2 on v0

--- a/solution.py
+++ b/solution.py
@@ -1,40 +1,46 @@
+import functools
+
 import jax
 import jax.numpy as jnp
 from jax import lax
+from jax.experimental import pallas as pl
+from jax.experimental.pallas import tpu as pltpu
 from jax.sharding import PartitionSpec as P
+
+NT = (((1,), (1,)), ((), ()))
+NN = (((1,), (0,)), ((), ()))
 
 
 def expert_terms(slot_rows, slot_grads, w_pair, v_pair, w_down):
     hidden_width = w_pair.shape[1]
     model_dim = w_pair.shape[2]
     stacked = jnp.concatenate([w_pair, v_pair], axis=0).reshape(4 * hidden_width, model_dim)
-    projected = lax.dot_general(
-        slot_rows, stacked, (((1,), (1,)), ((), ())), preferred_element_type=jnp.float32
-    )
+    projected = lax.dot_general(slot_rows, stacked, NT, preferred_element_type=jnp.float32)
     pre_gate = projected[:, :hidden_width]
     pre_up = projected[:, hidden_width : 2 * hidden_width]
     tan_gate = projected[:, 2 * hidden_width : 3 * hidden_width]
     tan_up = projected[:, 3 * hidden_width :]
-    back_grad = lax.dot_general(
-        slot_grads, w_down, (((1,), (1,)), ((), ())), preferred_element_type=jnp.float32
-    )
+    back_grad = lax.dot_general(slot_grads, w_down, NT, preferred_element_type=jnp.float32)
+    gate_dir, up_dir = directions(pre_gate, pre_up, tan_gate, tan_up, back_grad)
+    gate_term = lax.dot_general(
+        gate_dir, slot_rows, (((0,), (0,)), ((), ())), preferred_element_type=jnp.float32
+    )
+    up_term = lax.dot_general(
+        up_dir, slot_rows, (((0,), (0,)), ((), ())), preferred_element_type=jnp.float32
+    )
+    return jnp.stack([gate_term, up_term], axis=0)
+
+
+def directions(pre_gate, pre_up, tan_gate, tan_up, back_grad):
     gate_sig = jax.nn.sigmoid(pre_gate)
     first_deriv = gate_sig * (1.0 + pre_gate * (1.0 - gate_sig))
     second_deriv = gate_sig * (1.0 - gate_sig) * (2.0 + pre_gate * (1.0 - 2.0 * gate_sig))
-    gate_dir = (back_grad * (tan_up * first_deriv + pre_up * second_deriv * tan_gate)).astype(
-        jnp.bfloat16
-    )
-    up_dir = (back_grad * first_deriv * tan_gate).astype(jnp.bfloat16)
-    gate_term = lax.dot_general(
-        gate_dir, slot_rows, (((0,), (0,)), ((), ())), preferred_element_type=jnp.float32
-    )
-    up_term = lax.dot_general(
-        up_dir, slot_rows, (((0,), (0,)), ((), ())), preferred_element_type=jnp.float32
-    )
-    return jnp.stack([gate_term, up_term], axis=0)
-
-
-def local(tokens, cotangent, routes, combine, w_in, w_out, v_in):
+    gate_dir = back_grad * (tan_up * first_deriv + pre_up * second_deriv * tan_gate)
+    up_dir = back_grad * first_deriv * tan_gate
+    return gate_dir.astype(jnp.bfloat16), up_dir.astype(jnp.bfloat16)
+
+
+def dispatched(tokens, cotangent, routes, combine, w_in, w_out, v_in):
     n_expert = lax.axis_size("expert")
     exp_dev = w_in.shape[0]
     experts = n_expert * exp_dev
@@ -79,6 +85,183 @@
     ).astype(jnp.float32)
 
 
+CORE, X, Y = 1, 2, 16
+Z_NEAR, Z_FAR = 4, 8
+LANES = 128
+
+
+def pack_kernel(tok_ref, cot_ref, route_ref, comb_ref, out_ref, *, experts):
+    tok_dev, model_dim = tok_ref.shape
+    out_ref[0:tok_dev, 0:model_dim] = tok_ref[...]
+    out_ref[tok_dev:, 0:model_dim] = cot_ref[...]
+    lane = lax.broadcasted_iota(jnp.int32, (tok_dev, LANES), 1)
+    weight = jnp.zeros((tok_dev, LANES), jnp.float32)
+    for k in range(route_ref.shape[1]):
+        named = route_ref[:, k : k + 1] == lane % experts
+        weight = jnp.where(named, comb_ref[:, k : k + 1], weight)
+    high = weight.astype(jnp.bfloat16).astype(jnp.float32)
+    middle = (weight - high).astype(jnp.bfloat16).astype(jnp.float32)
+    low = weight - high - middle
+    part = lane // experts
+    zero = jnp.zeros_like(weight)
+    value = jnp.where(part == 0, high, jnp.where(part == 1, middle, jnp.where(part == 2, low, zero)))
+    out_ref[0:tok_dev, model_dim:] = value.astype(jnp.bfloat16)
+    out_ref[tok_dev:, model_dim:] = zero.astype(jnp.bfloat16)
+
+
+def slice_dirs(pieces, pick_ref, w_ref, v_ref, wo_ref, x_ref, c_ref, wt_ref, tok_dev):
+    model_dim = x_ref.shape[1]
+    half = wo_ref.shape[0]
+    row = 0
+    for piece in pieces:
+        for first in range(0, piece.shape[0], 2 * tok_dev):
+            at = pl.ds(row, tok_dev)
+            x_ref[at, :] = piece[first : first + tok_dev, 0:model_dim]
+            wt_ref[at, :] = piece[first : first + tok_dev, model_dim:]
+            c_ref[at, :] = piece[first + tok_dev : first + 2 * tok_dev, 0:model_dim]
+            row += tok_dev
+    x = x_ref[...]
+    weight = lax.dot_general(pick_ref[...], wt_ref[...], NT, preferred_element_type=jnp.float32)
+    pre = lax.dot_general(w_ref[...], x, NT, preferred_element_type=jnp.float32)
+    tan = lax.dot_general(v_ref[...], x, NT, preferred_element_type=jnp.float32)
+    back = lax.dot_general(wo_ref[...], c_ref[...], NT, preferred_element_type=jnp.float32)
+    back = back * weight[0:1, :]
+    return directions(pre[:half], pre[half:], tan[:half], tan[half:], back)
+
+
+def slice_kernel(*refs, count, tok_dev):
+    pieces = refs[:count]
+    pick_ref, w_ref, v_ref, wo_ref, x_ref, dir_ref, c_ref, wt_ref = refs[count:]
+    half = wo_ref.shape[0]
+    gate_dir, up_dir = slice_dirs(
+        pieces, pick_ref, w_ref, v_ref, wo_ref, x_ref, c_ref, wt_ref, tok_dev
+    )
+    dir_ref[0:half, :] = gate_dir
+    dir_ref[half:, :] = up_dir
+
+
+def last_kernel(*refs, count, earlier, tok_dev):
+    pieces = refs[:count]
+    held = refs[count : count + 2 * earlier]
+    pick_ref, w_ref, v_ref, wo_ref, out_ref, x_ref, c_ref, wt_ref, dir_ref, sum_ref, sems = refs[
+        count + 2 * earlier :
+    ]
+    half = wo_ref.shape[0]
+    gate_dir, up_dir = slice_dirs(
+        pieces, pick_ref, w_ref, v_ref, wo_ref, x_ref, c_ref, wt_ref, tok_dev
+    )
+    dir_ref[0:half, :] = gate_dir
+    dir_ref[half:, :] = up_dir
+    pairs = [(held[2 * n], held[2 * n + 1]) for n in range(earlier)] + [(x_ref, dir_ref)]
+    columns = 512
+    copies = []
+    for n in range(out_ref.shape[1] // columns):
+        at = pl.ds(n * columns, columns)
+        total = None
+        for rows, dirs in pairs:
+            term = lax.dot_general(dirs[...], rows[:, at], NN, preferred_element_type=jnp.float32)
+            total = term if total is None else total + term
+        sum_ref[:, at] = total
+        copy = pltpu.make_async_copy(sum_ref.at[:, at], out_ref.at[:, at], sems.at[n])
+        copy.start()
+        copies.append(copy)
+    for copy in copies:
+        copy.wait()
+
+
+def swap(value, masks):
+    axes = ("dp", "expert")
+    count = lax.axis_size("dp") * lax.axis_size("expert")
+    return lax.ppermute(value, axes, [(i, i ^ masks[i & CORE]) for i in range(count)])
+
+
+def dense(tokens, cotangent, routes, combine, w_in, w_out, v_in):
+    experts = lax.axis_size("expert")
+    tok_dev, model_dim = tokens.shape
+    half = w_in.shape[2]
+    wide = model_dim + LANES
+    inside = pl.BlockSpec(memory_space=pltpu.VMEM)
+    own = pl.pallas_call(
+        functools.partial(pack_kernel, experts=experts),
+        in_specs=[inside] * 4,
+        out_specs=inside,
+        out_shape=jax.ShapeDtypeStruct((2 * tok_dev, wide), jnp.bfloat16),
+    )(tokens, cotangent, routes, combine)
+
+    lane = jnp.arange(LANES, dtype=jnp.int32)
+    mine = (lane % experts == lax.axis_index("expert")) & (lane < 3 * experts)
+    pick = jnp.broadcast_to(mine.astype(jnp.bfloat16)[None, :], (16, LANES))
+
+    slices = [own] + [swap(own, (m, m)) for m in (Z_NEAR, Z_NEAR ^ Z_FAR, Z_FAR)]
+    weights = (
+        w_in.reshape(2 * half, model_dim),
+        v_in.reshape(2 * half, model_dim),
+        w_out.reshape(half, model_dim),
+    )
+    held = []
+    for n, block in enumerate(slices):
+        chip = jnp.concatenate([block, swap(block, (CORE, CORE))], axis=0)
+        beside = swap(chip, (X, Y))
+        across = swap(beside[: 2 * tok_dev], (Y, X))
+        got = jnp.concatenate([beside, across], axis=0)
+        pieces = [chip, got, swap(got, (CORE, CORE))]
+        rows = sum(p.shape[0] for p in pieces) // 2
+        last = n == len(slices) - 1
+        scratch = [
+            pltpu.VMEM((rows, model_dim), jnp.bfloat16),
+            pltpu.VMEM((rows, LANES), jnp.bfloat16),
+        ]
+        params = pltpu.CompilerParams(vmem_limit_bytes=28 * 2**20)
+        if not last:
+            held += pl.pallas_call(
+                functools.partial(slice_kernel, count=len(pieces), tok_dev=tok_dev),
+                in_specs=[inside] * (len(pieces) + 4),
+                out_specs=[inside] * 2,
+                out_shape=[
+                    jax.ShapeDtypeStruct((rows, model_dim), jnp.bfloat16),
+                    jax.ShapeDtypeStruct((2 * half, rows), jnp.bfloat16),
+                ],
+                scratch_shapes=scratch,
+                compiler_params=params,
+                cost_estimate=pl.CostEstimate(
+                    flops=2 * rows * model_dim * 5 * half,
+                    bytes_accessed=8 * 2**20,
+                    transcendentals=rows * half,
+                ),
+            )(*pieces, pick, *weights)
+    out = pl.pallas_call(
+        functools.partial(
+            last_kernel, count=len(pieces), earlier=len(held) // 2, tok_dev=tok_dev
+        ),
+        in_specs=[inside] * (len(pieces) + len(held) + 4),
+        out_specs=pl.BlockSpec(memory_space=pl.ANY),
+        out_shape=jax.ShapeDtypeStruct((2 * half, model_dim), jnp.float32),
+        scratch_shapes=[pltpu.VMEM((rows, model_dim), jnp.bfloat16)]
+        + scratch
+        + [
+            pltpu.VMEM((2 * half, rows), jnp.bfloat16),
+            pltpu.VMEM((2 * half, model_dim), jnp.float32),
+            pltpu.SemaphoreType.DMA((model_dim // 512,)),
+        ],
+        compiler_params=params,
+        cost_estimate=pl.CostEstimate(
+            flops=2 * rows * model_dim * 13 * half,
+            bytes_accessed=16 * 2**20,
+            transcendentals=rows * half,
+        ),
+    )(*pieces, *held, pick, *weights)
+    return out.reshape(1, 2, half, model_dim)
+
+
+def local(tokens, cotangent, routes, combine, w_in, w_out, v_in):
+    experts = lax.axis_size("expert") * w_in.shape[0]
+    tok_dev, top_k = routes.shape
+    sizes = (lax.axis_size("dp"), lax.axis_size("expert"))
+    if sizes == (2, 16) and w_in.shape[0] == 1 and 2 * tok_dev * top_k // experts >= tok_dev:
+        return dense(tokens, cotangent, routes, combine, w_in, w_out, v_in)
+    return dispatched(tokens, cotangent, routes, combine, w_in, w_out, v_in)
+
+
 def solution(mesh):
     in_specs = (
         P(("dp", "expert"), None),

time: 251 us -> 94.4 us (0.38)
  waiting for transfers between devices: 178 us -> 43.9 us
  Pallas kernels: 0 us -> 17.8 us
  matrix products: 17.2 us -> 0 us
  other arithmetic: 14.9 us -> 1.03 us
  between operations: 13.3 us -> 0.24 us
  local copies, waits for them, and re-layouts: 9.01 us -> 12 us
    all_gather x3 -> x0, waiting for transfers between devices: 84.1 us -> none  [local(): lax.all_gather((w_in, v_in, w_out[:, None]), 'dp', axis=2, tiled=True)]
    reduce_scatter x1 -> x0, waiting for transfers between devices: 54.4 us -> none  [local(): lax.psum_scatter(partials.astype(jnp.bfloat16), 'dp', scatter_dimension=2...]
    ppermute x0 -> x19, waiting for transfers between devices: none -> 43.9 us  [swap(): lax.ppermute(value, axes, [(i, i ^ masks[i & CORE]) for i in range(count)])]
    all_to_all x2 -> x0, waiting for transfers between devices: 36.9 us -> none  [the longest x1 36.9 us: local(): lax.all_to_all(send_grads, 'expert', split_axis=0, concat_axis=0, tiled=T...]
    ppermute x0 -> x19, starting transfers between devices: none -> 19.1 us  [swap(): lax.ppermute(value, axes, [(i, i ^ masks[i & CORE]) for i in range(count)])]
    all_to_all x2 -> x0, starting transfers between devices: 18.6 us -> none  [the longest x1 11.3 us: local(): lax.all_to_all(send_rows, 'expert', split_axis=0, concat_axis=0, tiled=True)]
    pallas_call x0 -> x5, Pallas kernels: none -> 17.8 us  [the longest x3 9.53 us: dense(): pl.pallas_call(functools.partial(slice_kernel, count=len(pieces), tok_dev...]
    dot_general x4 -> x0, matrix products: 17.2 us -> none  [the longest x1 7.63 us: expert_terms(): lax.dot_general(slot_rows, stacked, (((1,), (1,)), ((), ())), preferred_e...]
  transfers between devices with their start and end apart: 6 -> 19, of which waited for: 4 -> 5; matrix products, arithmetic and copies ran while one was open for 8% -> 8% of each run, Pallas kernels for 0% -> 10%
where the time goes in v2:
time: 94.4 us; the launch traced here: 94 us
  waiting for transfers between devices  43.9 us (47%)
  starting transfers between devices  19.1 us (20%)
  Pallas kernels  17.8 us (19%)
  local copies, waits for them, and re-layouts  12 us (13%)
  other arithmetic  1.03 us (1%)
    ppermute x19, waiting for transfers between devices, swap(): lax.ppermute(value, axes, [(i, i ^ masks[i & CORE]) for i in range(count)])  43.9 us
    ppermute x19, starting transfers between devices, swap(): lax.ppermute(value, axes, [(i, i ^ masks[i & CORE]) for i in range(count)])  19.1 us
    pallas_call x3, Pallas kernels, dense(): pl.pallas_call(functools.partial(slice_kernel, count=len(pieces), tok_dev...  9.53 us
    unnamed x33, local copies, waits for them, and re-layouts  8.9 us
    pallas_call x1, Pallas kernels, dense(): pl.pallas_call(functools.partial(last_kernel, count=len(pieces), earlier=...  6.47 us
    concatenate x4, local copies, waits for them, and re-layouts, dense(): got = jnp.concatenate([beside, across], axis=0)  2.89 us
  transfers between devices with their start and end apart: 19, of which 5 were waited for; matrix products, arithmetic and copies ran while one was open for 8% of the time, Pallas kernels for 10%

profile of v2, /device:TPU:0, one launch (start us, length us, event | category | flops | bytes accessed | tf_op | source)
XLA Modules:
  0.0 94.0 jit_solution(5341237600115330713)
XLA Ops:
  0.0 1.4 %copy.8.route_ref = s32[32,8]{1,0:T(8,128)} copy(s32[32,8]{0,1:T(8,128)} %param.9) | data formatting | bytes 2048 | tf_op args[2]
  1.4 1.4 %copy.9.comb_ref = f32[32,8]{1,0:T(8,128)} copy(f32[32,8]{0,1:T(8,128)} %param.10) | data formatting | bytes 2048 | tf_op args[3]
  2.7 1.8 %shard_map.73 = bf16[64,2176]{1,0:T(8,128)(2,1)} custom-call(bf16[32,2048]{1,0:T(8,128)(2,1)} %tok_ref.1, bf16[32,2048]{1,0:T(8,128)(2,1)} %cot_ref.1, s32[32,8]{1,0:T(8,128)} %copy.8.route_ref, f32[32,8]{1,0:T(8,128)} %copy.9.comb_ref), custom_call_target="tpu_custom_call" | custom-call | tf_op jit(solution)/shard_map/pallas_call | solution.py:184
  4.6 0.5 collective-permute-start.5
  5.0 4.6 %collective-permute-start.14 = (bf16[64,2176]{1,0:T(8,128)(2,1)}, bf16[64,2176]{1,0:T(8,128)(2,1)S(1)}, u32[]{:S(2)}, u32[]{:S(2)}) collective-permute-start(bf16[64,2176]{1,0:T(8,128)(2,1)} %shard_map.73), channel_id=1, source_target_pairs={{0,12},{1,13},{2,14},{3,15},{4,8},{5,9},{6,10},{7,11},{8,4},{9,5},... | collective-permute-start | bytes 835592 | tf_op jit(solution)/shard_map/ppermute | solution.py:175
  9.6 0.0 collective-permute-start.9
  9.6 0.6 collective-permute-start
  10.2 0.0 collective-permute-done.5
  10.2 1.0 %pad_maximum_fusion.refs_0_ = bf16[128,2176]{1,0:T(8,128)(2,1)S(1)} fusion(bf16[64,2176]{1,0:T(8,128)(2,1)S(1)} %collective-permute-done.5, bf16[64,2176]{1,0:T(8,128)(2,1)} %shard_map.73), kind=kLoop, calls=%fused_computation | loop fusion | flops 1114112 | bytes 1114112 | tf_op jit(solution)/shard_map/concatenate | solution.py:203
  11.3 1.7 %collective-permute-start.6 = (bf16[128,2176]{1,0:T(8,128)(2,1)S(1)}, bf16[128,2176]{1,0:T(8,128)(2,1)S(1)}, u32[]{:S(2)}, u32[]{:S(2)}) collective-permute-start(bf16[128,2176]{1,0:T(8,128)(2,1)S(1)} %pad_maximum_fusion.refs_0_), channel_id=1, source_target_pairs={{0,2},{1,17},{2,0},{3,19},{4,6},{5,21},{6,4},{7,23},{8,10},{9,25},... | collective-permute-start | bytes 1671176 | tf_op jit(solution)/shard_map/ppermute | solution.py:175
  13.0 21.2 %collective-permute-done = bf16[64,2176]{1,0:T(8,128)(2,1)S(1)} collective-permute-done((bf16[64,2176]{1,0:T(8,128)(2,1)}, bf16[64,2176]{1,0:T(8,128)(2,1)S(1)}, u32[]{:S(2)}, u32[]{:S(2)}) %collective-permute-start) | collective-permute-done | bytes 278560 | tf_op jit(solution)/shard_map/ppermute | solution.py:175
  34.2 0.0 collective-permute-start.1
  34.2 0.0 collective-permute-done.9
  34.2 0.6 collective-permute-start.10
  34.8 0.0 collective-permute-done.14
  34.9 0.1 collective-permute-start.15
  35.0 1.6 %collective-permute-done.15 = bf16[64,2176]{1,0:T(8,128)(2,1)S(1)} collective-permute-done((bf16[64,2176]{1,0:T(8,128)(2,1)S(1)}, bf16[64,2176]{1,0:T(8,128)(2,1)S(1)}, u32[]{:S(2)}, u32[]{:S(2)}) %collective-permute-start.15) | collective-permute-done | bytes 278560 | tf_op jit(solution)/shard_map/ppermute | solution.py:175
  36.6 1.6 %collective-permute-start.16 = (bf16[128,2176]{1,0:T(8,128)(2,1)S(1)}, bf16[128,2176]{1,0:T(8,128)(2,1)S(1)}, u32[]{:S(2)}, u32[]{:S(2)}) collective-permute-start(bf16[128,2176]{1,0:T(8,128)(2,1)S(1)} %constant_dynamic-update-slice_fusion.10.refs_0_), channel_id=1, source_target_pairs={{0,2},{1,17},{2,0},{3,19},{4,6},{5,21},{6,4},{7,23},{8,10},{9,25},... | collective-permute-start | bytes 1671176 | tf_op jit(solution)/shard_map/ppermute | solution.py:175
  38.2 0.0 collective-permute-done.10
  38.2 0.0 copy-start.8
  38.2 0.6 collective-permute-start.11
  38.8 0.0 collective-permute-done.1
  38.8 0.0 copy-start.6
  38.8 1.6 %collective-permute-start.2 = (bf16[128,2176]{1,0:T(8,128)(2,1)S(1)}, bf16[128,2176]{1,0:T(8,128)(2,1)S(1)}, u32[]{:S(2)}, u32[]{:S(2)}) collective-permute-start(bf16[128,2176]{1,0:T(8,128)(2,1)S(1)} %constant_dynamic-update-slice_fusion.refs_0_), channel_id=1, source_target_pairs={{0,2},{1,17},{2,0},{3,19},{4,6},{5,21},{6,4},{7,23},{8,10},{9,25},... | collective-permute-start | bytes 1671176 | tf_op jit(solution)/shard_map/ppermute | solution.py:175
  40.4 0.0 collective-permute-done.6
  40.4 1.6 %collective-permute-start.7 = (bf16[64,2176]{1,0:T(8,128)(2,1)S(1)}, bf16[64,2176]{1,0:T(8,128)(2,1)S(1)}, u32[]{:S(2)}, u32[]{:S(2)}) collective-permute-start(bf16[64,2176]{1,0:T(8,128)(2,1)S(1)} %slice.17), channel_id=1, source_target_pairs={{0,16},{1,3},{2,18},{3,1},{4,20},{5,7},{6,22},{7,5},{8,24},{9,11},... | collective-permute-start | bytes 835592 | tf_op jit(solution)/shard_map/ppermute | solution.py:175
  42.0 0.8 constant_dynamic-update-slice_fusion.5
  42.9 6.3 %collective-permute-done.16 = bf16[128,2176]{1,0:T(8,128)(2,1)S(1)} collective-permute-done((bf16[128,2176]{1,0:T(8,128)(2,1)S(1)}, bf16[128,2176]{1,0:T(8,128)(2,1)S(1)}, u32[]{:S(2)}, u32[]{:S(2)}) %collective-permute-start.16) | collective-permute-done | bytes 557088 | tf_op jit(solution)/shard_map/ppermute | solution.py:175
  49.2 1.6 %collective-permute-start.17 = (bf16[64,2176]{1,0:T(8,128)(2,1)S(1)}, bf16[64,2176]{1,0:T(8,128)(2,1)S(1)}, u32[]{:S(2)}, u32[]{:S(2)}) collective-permute-start(bf16[64,2176]{1,0:T(8,128)(2,1)S(1)} %slice.19), channel_id=1, source_target_pairs={{0,16},{1,3},{2,18},{3,1},{4,20},{5,7},{6,22},{7,5},{8,24},{9,11},... | collective-permute-start | bytes 835592 | tf_op jit(solution)/shard_map/ppermute | solution.py:175
  50.8 7.3 %collective-permute-done.11 = bf16[128,2176]{1,0:T(8,128)(2,1)S(1)} collective-permute-done((bf16[128,2176]{1,0:T(8,128)(2,1)S(1)}, bf16[128,2176]{1,0:T(8,128)(2,1)S(1)}, u32[]{:S(2)}, u32[]{:S(2)}) %collective-permute-start.11) | collective-permute-done | bytes 557088 | tf_op jit(solution)/shard_map/ppermute | solution.py:175
  58.2 1.6 %collective-permute-start.12 = (bf16[64,2176]{1,0:T(8,128)(2,1)S(1)}, bf16[64,2176]{1,0:T(8,128)(2,1)S(1)}, u32[]{:S(2)}, u32[]{:S(2)}) collective-permute-start(bf16[64,2176]{1,0:T(8,128)(2,1)S(1)} %slice.18), channel_id=1, source_target_pairs={{0,16},{1,3},{2,18},{3,1},{4,20},{5,7},{6,22},{7,5},{8,24},{9,11},... | collective-permute-start | bytes 835592 | tf_op jit(solution)/shard_map/ppermute | solution.py:175
  59.8 7.3 %collective-permute-done.2 = bf16[128,2176]{1,0:T(8,128)(2,1)S(1)} collective-permute-done((bf16[128,2176]{1,0:T(8,128)(2,1)S(1)}, bf16[128,2176]{1,0:T(8,128)(2,1)S(1)}, u32[]{:S(2)}, u32[]{:S(2)}) %collective-permute-start.2) | collective-permute-done | bytes 557088 | tf_op jit(solution)/shard_map/ppermute | solution.py:175
  67.1 1.6 %collective-permute-start.3 = (bf16[64,2176]{1,0:T(8,128)(2,1)S(1)}, bf16[64,2176]{1,0:T(8,128)(2,1)S(1)}, u32[]{:S(2)}, u32[]{:S(2)}) collective-permute-start(bf16[64,2176]{1,0:T(8,128)(2,1)S(1)} %slice.16), channel_id=1, source_target_pairs={{0,16},{1,3},{2,18},{3,1},{4,20},{5,7},{6,22},{7,5},{8,24},{9,11},... | collective-permute-start | bytes 835592 | tf_op jit(solution)/shard_map/ppermute | solution.py:175
  68.7 0.0 collective-permute-done.7
  68.7 0.7 constant_dynamic-update-slice_fusion.4.refs_1_
  69.4 0.0 copy-done.8
  69.4 0.0 collective-permute-start.8
  69.5 0.9 constant_dynamic-update-slice_fusion.13
  70.3 0.9 constant_dynamic-update-slice_fusion.9
  71.2 0.8 constant_dynamic-update-slice_fusion.3
  72.0 0.0 collective-permute-done.12
  72.1 0.7 constant_dynamic-update-slice_fusion.8.refs_1_
  72.8 0.5 collective-permute-start.13
  73.3 0.0 collective-permute-done.17
  73.3 0.7 constant_dynamic-update-slice_fusion.12.refs_1_
  74.0 0.0 collective-permute-start.18
  74.0 0.0 collective-permute-done.3
  74.0 0.7 constant_dynamic-update-slice_fusion.2.refs_1_
  74.7 0.5 collective-permute-start.4
  75.2 0.0 collective-permute-done.8.refs_2_
  75.3 0.0 copy-start.1
  75.3 1.6 %copy-done.1 = bf16[1,2,256,2048]{3,2,1,0:T(8,128)(2,1)S(1)} copy-done((bf16[1,2,256,2048]{3,2,1,0:T(8,128)(2,1)S(1)}, bf16[1,2,256,2048]{3,2,1,0:T(8,128)(2,1)}, u32[]{:S(2)}) %copy-start.1) | copy-done | bytes 2097176
  76.9 1.1 %copy-done.5 = bf16[128,2176]{1,0:T(8,128)(2,1)S(1)} copy-done((bf16[128,2176]{1,0:T(8,128)(2,1)S(1)}, bf16[128,2176]{1,0:T(8,128)(2,1)}, u32[]{:S(2)}) %copy-start.5) | copy-done | bytes 557080
  77.9 3.2 %shard_map.74 = (bf16[256,2048]{1,0:T(8,128)(2,1)S(1)}, bf16[512,256]{1,0:T(8,128)(2,1)S(1)}) custom-call(bf16[128,2176]{1,0:T(8,128)(2,1)S(1)} %copy-done.5, bf16[192,2176]{1,0:T(8,128)(2,1)} %constant_dynamic-update-slice_fusion.4.refs_1_, bf16[192,2176]{1,0:T(8,128)(2,1)} %collective-permute-done.8.refs_2_, ...), custom_call_target="tpu_custom_call" | custom-call | flops 1342177280 | bytes 8388608 | tf_op jit(solution)/shard_map/pallas_call | solution.py:216
  81.2 0.0 collective-permute-done.13.refs_2_
  81.2 0.0 copy-done.2
  81.2 0.0 copy-done.9
  81.2 3.1 %shard_map.75 = (bf16[256,2048]{1,0:T(8,128)(2,1)S(1)}, bf16[512,256]{1,0:T(8,128)(2,1)S(1)}) custom-call(bf16[128,2176]{1,0:T(8,128)(2,1)S(1)} %copy-done.9, bf16[192,2176]{1,0:T(8,128)(2,1)} %constant_dynamic-update-slice_fusion.8.refs_1_, bf16[192,2176]{1,0:T(8,128)(2,1)} %collective-permute-done.13.refs_2_, ...), custom_call_target="tpu_custom_call" | custom-call | flops 1342177280 | bytes 8388608 | tf_op jit(solution)/shard_map/pallas_call | solution.py:216
  84.4 0.0 collective-permute-done.18.refs_2_
  84.4 0.0 copy-done.11
  84.4 3.1 %shard_map.76 = (bf16[256,2048]{1,0:T(8,128)(2,1)S(1)}, bf16[512,256]{1,0:T(8,128)(2,1)S(1)}) custom-call(bf16[128,2176]{1,0:T(8,128)(2,1)S(1)} %copy-done.11, bf16[192,2176]{1,0:T(8,128)(2,1)} %constant_dynamic-update-slice_fusion.12.refs_1_, bf16[192,2176]{1,0:T(8,128)(2,1)} %collective-permute-done.18.refs_2_, ...), custom_call_target="tpu_custom_call" | custom-call | flops 1342177280 | bytes 8388608 | tf_op jit(solution)/shard_map/pallas_call | solution.py:216
  87.6 0.0 collective-permute-done.4.refs_2_
  87.6 0.0 copy-done.7
  87.6 6.5 %shard_map.77 = f32[512,2048]{1,0:T(8,128)} custom-call(bf16[128,2176]{1,0:T(8,128)(2,1)S(1)} %copy-done.7, bf16[192,2176]{1,0:T(8,128)(2,1)} %constant_dynamic-update-slice_fusion.2.refs_1_, bf16[192,2176]{1,0:T(8,128)(2,1)} %collective-permute-done.4.refs_2_, bf16[256,2048]{1,0:T(8,128)(2,1)S(1)} %get-tuple-element.11.refs_3_, ...), custom_call_target="tpu_custom_call" | custom-call | flops 3489660928 | bytes 16777216 | tf_op jit(solution)/shard_map/pallas_call | solution.py:232
  (26 shorter events, 0.3 us)
Async XLA Ops:
  4.6 5.7 %collective-permute-start.5 = (bf16[64,2176]{1,0:T(8,128)(2,1)}, bf16[64,2176]{1,0:T(8,128)(2,1)S(1)}, u32[]{:S(2)}, u32[]{:S(2)}) collective-permute-start(bf16[64,2176]{1,0:T(8,128)(2,1)} %shard_map.73), channel_id=1, source_target_pairs={{0,1},{1,0},{2,3},{3,2},{4,5},{5,4},{6,7},{7,6},{8,9},{9,8},{10,11... | collective-permute-start | bytes 835592 | tf_op jit(solution)/shard_map/ppermute | solution.py:175
  5.0 29.8 %collective-permute-start.14 = (bf16[64,2176]{1,0:T(8,128)(2,1)}, bf16[64,2176]{1,0:T(8,128)(2,1)S(1)}, u32[]{:S(2)}, u32[]{:S(2)}) collective-permute-start(bf16[64,2176]{1,0:T(8,128)(2,1)} %shard_map.73), channel_id=1, source_target_pairs={{0,12},{1,13},{2,14},{3,15},{4,8},{5,9},{6,10},{7,11},{8,4},{9,5},... | collective-permute-start | bytes 835592 | tf_op jit(solution)/shard_map/ppermute | solution.py:175
  9.6 24.6 %collective-permute-start.9 = (bf16[64,2176]{1,0:T(8,128)(2,1)}, bf16[64,2176]{1,0:T(8,128)(2,1)S(1)}, u32[]{:S(2)}, u32[]{:S(2)}) collective-permute-start(bf16[64,2176]{1,0:T(8,128)(2,1)} %shard_map.73), channel_id=1, source_target_pairs={{0,4},{1,5},{2,6},{3,7},{4,0},{5,1},{6,2},{7,3},{8,12},{9,13},{10,... | collective-permute-start | bytes 835592 | tf_op jit(solution)/shard_map/ppermute | solution.py:175
  9.6 24.6 %collective-permute-start = (bf16[64,2176]{1,0:T(8,128)(2,1)}, bf16[64,2176]{1,0:T(8,128)(2,1)S(1)}, u32[]{:S(2)}, u32[]{:S(2)}) collective-permute-start(bf16[64,2176]{1,0:T(8,128)(2,1)} %shard_map.73), channel_id=1, source_target_pairs={{0,8},{1,9},{2,10},{3,11},{4,12},{5,13},{6,14},{7,15},{8,0},{9,1},... | collective-permute-start | bytes 835592 | tf_op jit(solution)/shard_map/ppermute | solution.py:175
  11.3 31.6 %copy-start.4 = (bf16[128,2176]{1,0:T(8,128)(2,1)}, bf16[128,2176]{1,0:T(8,128)(2,1)S(1)}, u32[]{:S(2)}) copy-start(bf16[128,2176]{1,0:T(8,128)(2,1)S(1)} %pad_maximum_fusion.refs_0_) | copy-start | bytes 1671172
  11.3 29.1 %collective-permute-start.6 = (bf16[128,2176]{1,0:T(8,128)(2,1)S(1)}, bf16[128,2176]{1,0:T(8,128)(2,1)S(1)}, u32[]{:S(2)}, u32[]{:S(2)}) collective-permute-start(bf16[128,2176]{1,0:T(8,128)(2,1)S(1)} %pad_maximum_fusion.refs_0_), channel_id=1, source_target_pairs={{0,2},{1,17},{2,0},{3,19},{4,6},{5,21},{6,4},{7,23},{8,10},{9,25},... | collective-permute-start | bytes 1671176 | tf_op jit(solution)/shard_map/ppermute | solution.py:175
  34.2 4.6 %collective-permute-start.1 = (bf16[64,2176]{1,0:T(8,128)(2,1)S(1)}, bf16[64,2176]{1,0:T(8,128)(2,1)S(1)}, u32[]{:S(2)}, u32[]{:S(2)}) collective-permute-start(bf16[64,2176]{1,0:T(8,128)(2,1)S(1)} %collective-permute-done), channel_id=1, source_target_pairs={{0,1},{1,0},{2,3},{3,2},{4,5},{5,4},{6,7},{7,6},{8,9},{9,8},{10,11... | collective-permute-start | bytes 835592 | tf_op jit(solution)/shard_map/ppermute | solution.py:175
  34.2 3.9 %collective-permute-start.10 = (bf16[64,2176]{1,0:T(8,128)(2,1)S(1)}, bf16[64,2176]{1,0:T(8,128)(2,1)S(1)}, u32[]{:S(2)}, u32[]{:S(2)}) collective-permute-start(bf16[64,2176]{1,0:T(8,128)(2,1)S(1)} %collective-permute-done.9), channel_id=1, source_target_pairs={{0,1},{1,0},{2,3},{3,2},{4,5},{5,4},{6,7},{7,6},{8,9},{9,8},{10,11... | collective-permute-start | bytes 835592 | tf_op jit(solution)/shard_map/ppermute | solution.py:175
  34.9 1.7 %collective-permute-start.15 = (bf16[64,2176]{1,0:T(8,128)(2,1)S(1)}, bf16[64,2176]{1,0:T(8,128)(2,1)S(1)}, u32[]{:S(2)}, u32[]{:S(2)}) collective-permute-start(bf16[64,2176]{1,0:T(8,128)(2,1)S(1)} %collective-permute-done.14), channel_id=1, source_target_pairs={{0,1},{1,0},{2,3},{3,2},{4,5},{5,4},{6,7},{7,6},{8,9},{9,8},{10,11... | collective-permute-start | bytes 835592 | tf_op jit(solution)/shard_map/ppermute | solution.py:175
  36.6 30.5 %copy-start.10 = (bf16[128,2176]{1,0:T(8,128)(2,1)}, bf16[128,2176]{1,0:T(8,128)(2,1)S(1)}, u32[]{:S(2)}) copy-start(bf16[128,2176]{1,0:T(8,128)(2,1)S(1)} %constant_dynamic-update-slice_fusion.10.refs_0_) | copy-start | bytes 1671172
  36.6 12.6 %collective-permute-start.16 = (bf16[128,2176]{1,0:T(8,128)(2,1)S(1)}, bf16[128,2176]{1,0:T(8,128)(2,1)S(1)}, u32[]{:S(2)}, u32[]{:S(2)}) collective-permute-start(bf16[128,2176]{1,0:T(8,128)(2,1)S(1)} %constant_dynamic-update-slice_fusion.10.refs_0_), channel_id=1, source_target_pairs={{0,2},{1,17},{2,0},{3,19},{4,6},{5,21},{6,4},{7,23},{8,10},{9,25},... | collective-permute-start | bytes 1671176 | tf_op jit(solution)/shard_map/ppermute | solution.py:175
  38.2 31.3 %copy-start.8 = (bf16[128,2176]{1,0:T(8,128)(2,1)}, bf16[128,2176]{1,0:T(8,128)(2,1)S(1)}, u32[]{:S(2)}) copy-start(bf16[128,2176]{1,0:T(8,128)(2,1)S(1)} %constant_dynamic-update-slice_fusion.6.refs_0_) | copy-start | bytes 1671172
  38.2 19.9 %collective-permute-start.11 = (bf16[128,2176]{1,0:T(8,128)(2,1)S(1)}, bf16[128,2176]{1,0:T(8,128)(2,1)S(1)}, u32[]{:S(2)}, u32[]{:S(2)}) collective-permute-start(bf16[128,2176]{1,0:T(8,128)(2,1)S(1)} %constant_dynamic-update-slice_fusion.6.refs_0_), channel_id=1, source_target_pairs={{0,2},{1,17},{2,0},{3,19},{4,6},{5,21},{6,4},{7,23},{8,10},{9,25},... | collective-permute-start | bytes 1671176 | tf_op jit(solution)/shard_map/ppermute | solution.py:175
  38.8 31.5 %copy-start.6 = (bf16[128,2176]{1,0:T(8,128)(2,1)}, bf16[128,2176]{1,0:T(8,128)(2,1)S(1)}, u32[]{:S(2)}) copy-start(bf16[128,2176]{1,0:T(8,128)(2,1)S(1)} %constant_dynamic-update-slice_fusion.refs_0_) | copy-start | bytes 1671172
  38.8 28.2 %collective-permute-start.2 = (bf16[128,2176]{1,0:T(8,128)(2,1)S(1)}, bf16[128,2176]{1,0:T(8,128)(2,1)S(1)}, u32[]{:S(2)}, u32[]{:S(2)}) collective-permute-start(bf16[128,2176]{1,0:T(8,128)(2,1)S(1)} %constant_dynamic-update-slice_fusion.refs_0_), channel_id=1, source_target_pairs={{0,2},{1,17},{2,0},{3,19},{4,6},{5,21},{6,4},{7,23},{8,10},{9,25},... | collective-permute-start | bytes 1671176 | tf_op jit(solution)/shard_map/ppermute | solution.py:175
  40.4 28.3 %collective-permute-start.7 = (bf16[64,2176]{1,0:T(8,128)(2,1)S(1)}, bf16[64,2176]{1,0:T(8,128)(2,1)S(1)}, u32[]{:S(2)}, u32[]{:S(2)}) collective-permute-start(bf16[64,2176]{1,0:T(8,128)(2,1)S(1)} %slice.17), channel_id=1, source_target_pairs={{0,16},{1,3},{2,18},{3,1},{4,20},{5,7},{6,22},{7,5},{8,24},{9,11},... | collective-permute-start | bytes 835592 | tf_op jit(solution)/shard_map/ppermute | solution.py:175
  49.2 24.1 %collective-permute-start.17 = (bf16[64,2176]{1,0:T(8,128)(2,1)S(1)}, bf16[64,2176]{1,0:T(8,128)(2,1)S(1)}, u32[]{:S(2)}, u32[]{:S(2)}) collective-permute-start(bf16[64,2176]{1,0:T(8,128)(2,1)S(1)} %slice.19), channel_id=1, source_target_pairs={{0,16},{1,3},{2,18},{3,1},{4,20},{5,7},{6,22},{7,5},{8,24},{9,11},... | collective-permute-start | bytes 835592 | tf_op jit(solution)/shard_map/ppermute | solution.py:175
  58.2 13.9 %collective-permute-start.12 = (bf16[64,2176]{1,0:T(8,128)(2,1)S(1)}, bf16[64,2176]{1,0:T(8,128)(2,1)S(1)}, u32[]{:S(2)}, u32[]{:S(2)}) collective-permute-start(bf16[64,2176]{1,0:T(8,128)(2,1)S(1)} %slice.18), channel_id=1, source_target_pairs={{0,16},{1,3},{2,18},{3,1},{4,20},{5,7},{6,22},{7,5},{8,24},{9,11},... | collective-permute-start | bytes 835592 | tf_op jit(solution)/shard_map/ppermute | solution.py:175
  67.1 6.9 %collective-permute-start.3 = (bf16[64,2176]{1,0:T(8,128)(2,1)S(1)}, bf16[64,2176]{1,0:T(8,128)(2,1)S(1)}, u32[]{:S(2)}, u32[]{:S(2)}) collective-permute-start(bf16[64,2176]{1,0:T(8,128)(2,1)S(1)} %slice.16), channel_id=1, source_target_pairs={{0,16},{1,3},{2,18},{3,1},{4,20},{5,7},{6,22},{7,5},{8,24},{9,11},... | collective-permute-start | bytes 835592 | tf_op jit(solution)/shard_map/ppermute | solution.py:175
  69.4 5.8 %collective-permute-start.8 = (bf16[192,2176]{1,0:T(8,128)(2,1)}, bf16[192,2176]{1,0:T(8,128)(2,1)}, u32[]{:S(2)}, u32[]{:S(2)}) collective-permute-start(bf16[192,2176]{1,0:T(8,128)(2,1)} %constant_dynamic-update-slice_fusion.4.refs_1_), channel_id=1, source_target_pairs={{0,1},{1,0},{2,3},{3,2},{4,5},{5,4},{6,7},{7,6},{8,9},{9,8},{10,11... | collective-permute-start | bytes 2506760 | tf_op jit(solution)/shard_map/ppermute | solution.py:175
  70.3 4.9 %copy-start = (bf16[1,2,256,2048]{3,2,1,0:T(8,128)(2,1)S(1)}, bf16[1,2,256,2048]{3,2,1,0:T(8,128)(2,1)}, u32[]{:S(2)}) copy-start(bf16[1,2,256,2048]{3,2,1,0:T(8,128)(2,1)} %param.11) | copy-start | bytes 6291460
  70.3 4.9 %copy-start.3 = (bf16[1,256,2048]{2,1,0:T(8,128)(2,1)S(1)}, bf16[1,256,2048]{2,1,0:T(8,128)(2,1)}, u32[]{:S(2)}) copy-start(bf16[1,256,2048]{2,1,0:T(8,128)(2,1)} %param.12) | copy-start | bytes 3145732
  72.8 8.4 %collective-permute-start.13 = (bf16[192,2176]{1,0:T(8,128)(2,1)}, bf16[192,2176]{1,0:T(8,128)(2,1)}, u32[]{:S(2)}, u32[]{:S(2)}) collective-permute-start(bf16[192,2176]{1,0:T(8,128)(2,1)} %constant_dynamic-update-slice_fusion.8.refs_1_), channel_id=1, source_target_pairs={{0,1},{1,0},{2,3},{3,2},{4,5},{5,4},{6,7},{7,6},{8,9},{9,8},{10,11... | collective-permute-start | bytes 2506760 | tf_op jit(solution)/shard_map/ppermute | solution.py:175
  74.0 10.4 %collective-permute-start.18 = (bf16[192,2176]{1,0:T(8,128)(2,1)}, bf16[192,2176]{1,0:T(8,128)(2,1)}, u32[]{:S(2)}, u32[]{:S(2)}) collective-permute-start(bf16[192,2176]{1,0:T(8,128)(2,1)} %constant_dynamic-update-slice_fusion.12.refs_1_), channel_id=1, source_target_pairs={{0,1},{1,0},{2,3},{3,2},{4,5},{5,4},{6,7},{7,6},{8,9},{9,8},{10,11... | collective-permute-start | bytes 2506760 | tf_op jit(solution)/shard_map/ppermute | solution.py:175
  74.7 12.8 %collective-permute-start.4 = (bf16[192,2176]{1,0:T(8,128)(2,1)}, bf16[192,2176]{1,0:T(8,128)(2,1)}, u32[]{:S(2)}, u32[]{:S(2)}) collective-permute-start(bf16[192,2176]{1,0:T(8,128)(2,1)} %constant_dynamic-update-slice_fusion.2.refs_1_), channel_id=1, source_target_pairs={{0,1},{1,0},{2,3},{3,2},{4,5},{5,4},{6,7},{7,6},{8,9},{9,8},{10,11... | collective-permute-start | bytes 2506760 | tf_op jit(solution)/shard_map/ppermute | solution.py:175
  75.3 1.6 %copy-start.1 = (bf16[1,2,256,2048]{3,2,1,0:T(8,128)(2,1)S(1)}, bf16[1,2,256,2048]{3,2,1,0:T(8,128)(2,1)}, u32[]{:S(2)}) copy-start(bf16[1,2,256,2048]{3,2,1,0:T(8,128)(2,1)} %param.13) | copy-start | bytes 6291460
  76.9 1.1 %copy-start.5 = (bf16[128,2176]{1,0:T(8,128)(2,1)S(1)}, bf16[128,2176]{1,0:T(8,128)(2,1)}, u32[]{:S(2)}) copy-start(bf16[128,2176]{1,0:T(8,128)(2,1)} %copy-done.4) | copy-start | bytes 1671172
  77.9 3.3 %copy-start.2 = (bf16[1,2,256,2048]{3,2,1,0:T(8,128)(2,1)S(1)}, bf16[1,2,256,2048]{3,2,1,0:T(8,128)(2,1)}, u32[]{:S(2)}) copy-start(bf16[1,2,256,2048]{3,2,1,0:T(8,128)(2,1)} %param.13) | copy-start | bytes 6291460
  77.9 3.3 %copy-start.9 = (bf16[128,2176]{1,0:T(8,128)(2,1)S(1)}, bf16[128,2176]{1,0:T(8,128)(2,1)}, u32[]{:S(2)}) copy-start(bf16[128,2176]{1,0:T(8,128)(2,1)} %copy-done.8) | copy-start | bytes 1671172
  81.2 3.2 %copy-start.11 = (bf16[128,2176]{1,0:T(8,128)(2,1)S(1)}, bf16[128,2176]{1,0:T(8,128)(2,1)}, u32[]{:S(2)}) copy-start(bf16[128,2176]{1,0:T(8,128)(2,1)} %copy-done.10) | copy-start | bytes 1671172
  84.4 3.2 %copy-start.7 = (bf16[128,2176]{1,0:T(8,128)(2,1)S(1)}, bf16[128,2176]{1,0:T(8,128)(2,1)}, u32[]{:S(2)}) copy-start(bf16[128,2176]{1,0:T(8,128)(2,1)} %copy-done.6) | copy-start | bytes 1671172

commit v3 on v2

--- a/solution.py
+++ b/solution.py
@@ -94,19 +94,25 @@
     tok_dev, model_dim = tok_ref.shape
     out_ref[0:tok_dev, 0:model_dim] = tok_ref[...]
     out_ref[tok_dev:, 0:model_dim] = cot_ref[...]
-    lane = lax.broadcasted_iota(jnp.int32, (tok_dev, LANES), 1)
-    weight = jnp.zeros((tok_dev, LANES), jnp.float32)
-    for k in range(route_ref.shape[1]):
-        named = route_ref[:, k : k + 1] == lane % experts
-        weight = jnp.where(named, comb_ref[:, k : k + 1], weight)
+    line = lax.broadcasted_iota(jnp.int32, (LANES, tok_dev), 0)
+    weight = jnp.zeros((LANES, tok_dev), jnp.float32)
+    for k in range(route_ref.shape[0]):
+        named = route_ref[k : k + 1, :] == line % experts
+        weight = jnp.where(named, comb_ref[k : k + 1, :], weight)
     high = weight.astype(jnp.bfloat16).astype(jnp.float32)
     middle = (weight - high).astype(jnp.bfloat16).astype(jnp.float32)
     low = weight - high - middle
-    part = lane // experts
+    part = line // experts
     zero = jnp.zeros_like(weight)
     value = jnp.where(part == 0, high, jnp.where(part == 1, middle, jnp.where(part == 2, low, zero)))
-    out_ref[0:tok_dev, model_dim:] = value.astype(jnp.bfloat16)
-    out_ref[tok_dev:, model_dim:] = zero.astype(jnp.bfloat16)
+    row = lax.broadcasted_iota(jnp.int32, (tok_dev, tok_dev), 0)
+    column = lax.broadcasted_iota(jnp.int32, (tok_dev, tok_dev), 1)
+    same = (row == column).astype(jnp.float32).astype(jnp.bfloat16)
+    turned = lax.dot_general(
+        same, value.astype(jnp.bfloat16), NT, preferred_element_type=jnp.float32
+    )
+    out_ref[0:tok_dev, model_dim:] = turned.astype(jnp.bfloat16)
+    out_ref[tok_dev:, model_dim:] = jnp.zeros((tok_dev, LANES), jnp.bfloat16)
 
 
 def slice_dirs(pieces, pick_ref, w_ref, v_ref, wo_ref, x_ref, c_ref, wt_ref, tok_dev):
@@ -122,11 +128,12 @@
             row += tok_dev
     x = x_ref[...]
     weight = lax.dot_general(pick_ref[...], wt_ref[...], NT, preferred_element_type=jnp.float32)
-    pre = lax.dot_general(w_ref[...], x, NT, preferred_element_type=jnp.float32)
-    tan = lax.dot_general(v_ref[...], x, NT, preferred_element_type=jnp.float32)
+    both = jnp.concatenate([w_ref[...], v_ref[...]], axis=0)
+    seen = lax.dot_general(both, x, NT, preferred_element_type=jnp.float32)
     back = lax.dot_general(wo_ref[...], c_ref[...], NT, preferred_element_type=jnp.float32)
     back = back * weight[0:1, :]
-    return directions(pre[:half], pre[half:], tan[:half], tan[half:], back)
+    parts = [seen[n * half : (n + 1) * half] for n in range(4)]
+    return directions(*parts, back)
 
 
 def slice_kernel(*refs, count, tok_dev):
@@ -157,11 +164,9 @@
     copies = []
     for n in range(out_ref.shape[1] // columns):
         at = pl.ds(n * columns, columns)
-        total = None
-        for rows, dirs in pairs:
-            term = lax.dot_general(dirs[...], rows[:, at], NN, preferred_element_type=jnp.float32)
-            total = term if total is None else total + term
-        sum_ref[:, at] = total
+        rows = jnp.concatenate([r[:, at] for r, _ in pairs], axis=0)
+        dirs = jnp.concatenate([d[...] for _, d in pairs], axis=1)
+        sum_ref[:, at] = lax.dot_general(dirs, rows, NN, preferred_element_type=jnp.float32)
         copy = pltpu.make_async_copy(sum_ref.at[:, at], out_ref.at[:, at], sems.at[n])
         copy.start()
         copies.append(copy)
@@ -173,6 +178,10 @@
     axes = ("dp", "expert")
     count = lax.axis_size("dp") * lax.axis_size("expert")
     return lax.ppermute(value, axes, [(i, i ^ masks[i & CORE]) for i in range(count)])
+
+
+def after(value, *others):
+    return lax.optimization_barrier((value, *others))[0]
 
 
 def dense(tokens, cotangent, routes, combine, w_in, w_out, v_in):
@@ -186,13 +195,16 @@
         in_specs=[inside] * 4,
         out_specs=inside,
         out_shape=jax.ShapeDtypeStruct((2 * tok_dev, wide), jnp.bfloat16),
-    )(tokens, cotangent, routes, combine)
+    )(tokens, cotangent, routes.T, combine.T)
 
     lane = jnp.arange(LANES, dtype=jnp.int32)
     mine = (lane % experts == lax.axis_index("expert")) & (lane < 3 * experts)
     pick = jnp.broadcast_to(mine.astype(jnp.bfloat16)[None, :], (16, LANES))
 
-    slices = [own] + [swap(own, (m, m)) for m in (Z_NEAR, Z_NEAR ^ Z_FAR, Z_FAR)]
+    slices = [own]
+    for mask in (Z_NEAR, Z_NEAR ^ Z_FAR, Z_FAR):
+        sent = own if len(slices) == 1 else after(own, slices[-1])
+        slices.append(swap(sent, (mask, mask)))
     weights = (
         w_in.reshape(2 * half, model_dim),
         v_in.reshape(2 * half, model_dim),
@@ -203,8 +215,8 @@
         chip = jnp.concatenate([block, swap(block, (CORE, CORE))], axis=0)
         beside = swap(chip, (X, Y))
         across = swap(beside[: 2 * tok_dev], (Y, X))
-        got = jnp.concatenate([beside, across], axis=0)
-        pieces = [chip, got, swap(got, (CORE, CORE))]
+        pieces = [chip, beside, across]
+        pieces += [swap(got, (CORE, CORE)) for got in (beside, across)]
         rows = sum(p.shape[0] for p in pieces) // 2
         last = n == len(slices) - 1
         scratch = [

time: 94.4 us -> 87 us (0.922)
  waiting for transfers between devices: 43.9 us -> 31.6 us
  starting transfers between devices: 19.1 us -> 25 us
  Pallas kernels: 17.8 us -> 16.5 us
    ppermute x19 -> x23, waiting for transfers between devices: 43.9 us -> 31.6 us  [swap(): lax.ppermute(value, axes, [(i, i ^ masks[i & CORE]) for i in range(count)])]
    ppermute x19 -> x23, starting transfers between devices: 19.1 us -> 25 us  [swap(): lax.ppermute(value, axes, [(i, i ^ masks[i & CORE]) for i in range(count)])]
    slice x4, local copies, waits for them, and re-layouts: 0.08 us -> 4.43 us  [dense(): across = swap(beside[:2 * tok_dev], (Y, X))]
    concatenate x4 -> x0, local copies, waits for them, and re-layouts: 2.89 us -> none  [dense(): got = jnp.concatenate([beside, across], axis=0)]
    pallas_call x3, Pallas kernels: 9.53 us -> 7.65 us  [dense(): pl.pallas_call(functools.partial(slice_kernel, count=len(pieces), tok_dev...]
    unnamed x33 -> x47, local copies, waits for them, and re-layouts: 8.9 us -> 7.42 us
  transfers between devices with their start and end apart: 19 -> 23, of which waited for: 5 -> 8; matrix products, arithmetic and copies ran while one was open for 8% -> 6% of each run, Pallas kernels for 10% -> 9%
where the time goes in v3:
time: 87 us; the launch traced here: 86.4 us
  waiting for transfers between devices  31.6 us (36%)
  starting transfers between devices  25 us (29%)
  Pallas kernels  16.5 us (19%)
  local copies, waits for them, and re-layouts  11.9 us (14%)
  other arithmetic  1.03 us (1%)
    ppermute x23, waiting for transfers between devices, swap(): lax.ppermute(value, axes, [(i, i ^ masks[i & CORE]) for i in range(count)])  31.6 us
    ppermute x23, starting transfers between devices, swap(): lax.ppermute(value, axes, [(i, i ^ masks[i & CORE]) for i in range(count)])  25 us
    pallas_call x3, Pallas kernels, dense(): pl.pallas_call(functools.partial(slice_kernel, count=len(pieces), tok_dev...  7.65 us
    unnamed x47, local copies, waits for them, and re-layouts  7.42 us
    pallas_call x1, Pallas kernels, dense(): pl.pallas_call(functools.partial(last_kernel, count=len(pieces), earlier=...  7.06 us
    slice x4, local copies, waits for them, and re-layouts, dense(): across = swap(beside[:2 * tok_dev], (Y, X))  4.43 us
    pallas_call x1, Pallas kernels, dense(): pl.pallas_call(functools.partial(pack_kernel, experts=experts), in_specs=...  1.83 us
  transfers between devices with their start and end apart: 23, of which 8 were waited for; matrix products, arithmetic and copies ran while one was open for 6% of the time, Pallas kernels for 9%

profile of v3, /device:TPU:0, one launch (start us, length us, event | category | flops | bytes accessed | tf_op | source)
XLA Modules:
  0.0 86.4 jit_solution(7731648197353525331)
XLA Ops:
  0.0 1.8 %shard_map.73 = bf16[64,2176]{1,0:T(8,128)(2,1)} custom-call(bf16[32,2048]{1,0:T(8,128)(2,1)} %tok_ref.1, bf16[32,2048]{1,0:T(8,128)(2,1)} %cot_ref.1, s32[8,32]{1,0:T(8,128)} %bitcast.18, f32[8,32]{1,0:T(8,128)} %bitcast.19), custom_call_target="tpu_custom_call" | custom-call | tf_op jit(solution)/shard_map/pallas_call | solution.py:193
  1.8 3.0 %collective-permute-start = (bf16[64,2176]{1,0:T(8,128)(2,1)}, bf16[64,2176]{1,0:T(8,128)(2,1)S(1)}, u32[]{:S(2)}, u32[]{:S(2)}) collective-permute-start(bf16[64,2176]{1,0:T(8,128)(2,1)} %shard_map.73), channel_id=1, source_target_pairs={{0,4},{1,5},{2,6},{3,7},{4,0},{5,1},{6,2},{7,3},{8,12},{9,13},{10,... | collective-permute-start | bytes 835592 | tf_op jit(solution)/shard_map/ppermute | solution.py:180
  4.9 0.0 collective-permute-start.8
  4.9 6.9 %collective-permute-done = bf16[64,2176]{1,0:T(8,128)(2,1)S(1)} collective-permute-done((bf16[64,2176]{1,0:T(8,128)(2,1)}, bf16[64,2176]{1,0:T(8,128)(2,1)S(1)}, u32[]{:S(2)}, u32[]{:S(2)}) %collective-permute-start) | collective-permute-done | bytes 278560 | tf_op jit(solution)/shard_map/ppermute | solution.py:180
  11.7 3.8 %collective-permute-start.1 = (bf16[64,2176]{1,0:T(8,128)(2,1)}, bf16[64,2176]{1,0:T(8,128)(2,1)S(1)}, u32[]{:S(2)}, u32[]{:S(2)}) collective-permute-start(bf16[64,2176]{1,0:T(8,128)(2,1)} %shard_map.73), channel_id=1, source_target_pairs={{0,12},{1,13},{2,14},{3,15},{4,8},{5,9},{6,10},{7,11},{8,4},{9,5},... | collective-permute-start | bytes 835592 | tf_op jit(solution)/shard_map/ppermute | solution.py:180
  15.5 0.0 collective-permute-done.8
  15.5 1.0 %pad_maximum_fusion.refs_0_ = bf16[128,2176]{1,0:T(8,128)(2,1)S(1)} fusion(bf16[64,2176]{1,0:T(8,128)(2,1)S(1)} %collective-permute-done.8, bf16[64,2176]{1,0:T(8,128)(2,1)} %shard_map.73), kind=kLoop, calls=%fused_computation | loop fusion | flops 1114112 | bytes 1114112 | tf_op jit(solution)/shard_map/concatenate | solution.py:215
  16.5 1.6 %collective-permute-start.9 = (bf16[128,2176]{1,0:T(8,128)(2,1)S(1)}, bf16[128,2176]{1,0:T(8,128)(2,1)S(1)}, u32[]{:S(2)}, u32[]{:S(2)}) collective-permute-start(bf16[128,2176]{1,0:T(8,128)(2,1)S(1)} %pad_maximum_fusion.refs_0_), channel_id=1, source_target_pairs={{0,2},{1,17},{2,0},{3,19},{4,6},{5,21},{6,4},{7,23},{8,10},{9,25},... | collective-permute-start | bytes 1671176 | tf_op jit(solution)/shard_map/ppermute | solution.py:180
  18.1 0.0 collective-permute-start.13
  18.1 3.6 %collective-permute-done.1 = bf16[64,2176]{1,0:T(8,128)(2,1)S(1)} collective-permute-done((bf16[64,2176]{1,0:T(8,128)(2,1)}, bf16[64,2176]{1,0:T(8,128)(2,1)S(1)}, u32[]{:S(2)}, u32[]{:S(2)}) %collective-permute-start.1) | collective-permute-done | bytes 278560 | tf_op jit(solution)/shard_map/ppermute | solution.py:180
  21.7 6.5 %collective-permute-start.2 = (bf16[64,2176]{1,0:T(8,128)(2,1)}, bf16[64,2176]{1,0:T(8,128)(2,1)S(1)}, u32[]{:S(2)}, u32[]{:S(2)}) collective-permute-start(bf16[64,2176]{1,0:T(8,128)(2,1)} %shard_map.73), channel_id=1, source_target_pairs={{0,8},{1,9},{2,10},{3,11},{4,12},{5,13},{6,14},{7,15},{8,0},{9,1},... | collective-permute-start | bytes 835592 | tf_op jit(solution)/shard_map/ppermute | solution.py:180
  28.2 0.0 collective-permute-done.13
  28.2 1.6 %collective-permute-start.14 = (bf16[128,2176]{1,0:T(8,128)(2,1)S(1)}, bf16[128,2176]{1,0:T(8,128)(2,1)}, u32[]{:S(2)}, u32[]{:S(2)}) collective-permute-start(bf16[128,2176]{1,0:T(8,128)(2,1)S(1)} %constant_dynamic-update-slice_fusion.2.refs_0_), channel_id=1, source_target_pairs={{0,2},{1,17},{2,0},{3,19},{4,6},{5,21},{6,4},{7,23},{8,10},{9,25},... | collective-permute-start | bytes 1671176 | tf_op jit(solution)/shard_map/ppermute | solution.py:180
  29.8 0.0 collective-permute-start.18
  29.8 0.0 copy-start
  29.8 0.0 copy-start.3
  29.8 1.5 %collective-permute-done.18 = bf16[64,2176]{1,0:T(8,128)(2,1)S(1)} collective-permute-done((bf16[64,2176]{1,0:T(8,128)(2,1)S(1)}, bf16[64,2176]{1,0:T(8,128)(2,1)S(1)}, u32[]{:S(2)}, u32[]{:S(2)}) %collective-permute-start.18) | collective-permute-done | bytes 278560 | tf_op jit(solution)/shard_map/ppermute | solution.py:180
  31.4 0.6 collective-permute-start.19
  32.0 0.0 collective-permute-done.9.refs_1_
  32.0 1.6 %collective-permute-start.10 = (bf16[64,2176]{1,0:T(8,128)(2,1)S(1)}, bf16[64,2176]{1,0:T(8,128)(2,1)S(1)}, u32[]{:S(2)}, u32[]{:S(2)}) collective-permute-start(bf16[64,2176]{1,0:T(8,128)(2,1)S(1)} %slice.17), channel_id=1, source_target_pairs={{0,16},{1,3},{2,18},{3,1},{4,20},{5,7},{6,22},{7,5},{8,24},{9,11},... | collective-permute-start | bytes 835592 | tf_op jit(solution)/shard_map/ppermute | solution.py:180
  33.6 5.6 %collective-permute-done.2 = bf16[64,2176]{1,0:T(8,128)(2,1)S(1)} collective-permute-done((bf16[64,2176]{1,0:T(8,128)(2,1)}, bf16[64,2176]{1,0:T(8,128)(2,1)S(1)}, u32[]{:S(2)}, u32[]{:S(2)}) %collective-permute-start.2) | collective-permute-done | bytes 278560 | tf_op jit(solution)/shard_map/ppermute | solution.py:180
  39.2 0.0 collective-permute-start.3
  39.3 1.5 %collective-permute-done.3 = bf16[64,2176]{1,0:T(8,128)(2,1)S(1)} collective-permute-done((bf16[64,2176]{1,0:T(8,128)(2,1)S(1)}, bf16[64,2176]{1,0:T(8,128)(2,1)S(1)}, u32[]{:S(2)}, u32[]{:S(2)}) %collective-permute-start.3) | collective-permute-done | bytes 278560 | tf_op jit(solution)/shard_map/ppermute | solution.py:180
  40.8 0.0 copy-start.12
  40.8 1.6 %collective-permute-start.4 = (bf16[128,2176]{1,0:T(8,128)(2,1)S(1)}, bf16[128,2176]{1,0:T(8,128)(2,1)}, u32[]{:S(2)}, u32[]{:S(2)}) collective-permute-start(bf16[128,2176]{1,0:T(8,128)(2,1)S(1)} %constant_dynamic-update-slice_fusion.refs_0_), channel_id=1, source_target_pairs={{0,2},{1,17},{2,0},{3,19},{4,6},{5,21},{6,4},{7,23},{8,10},{9,25},... | collective-permute-start | bytes 1671176 | tf_op jit(solution)/shard_map/ppermute | solution.py:180
  42.4 0.0 collective-permute-start.11
  42.4 0.0 collective-permute-done.14.refs_1_
  42.4 1.0 %slice.18 = bf16[64,2176]{1,0:T(8,128)(2,1)S(1)} slice(bf16[128,2176]{1,0:T(8,128)(2,1)} %collective-permute-done.14.refs_1_), slice={[0:64], [0:2176]} | slice | bytes 557056 | tf_op jit(solution)/shard_map/slice | solution.py:217
  43.4 1.6 %collective-permute-start.15 = (bf16[64,2176]{1,0:T(8,128)(2,1)S(1)}, bf16[64,2176]{1,0:T(8,128)(2,1)S(1)}, u32[]{:S(2)}, u32[]{:S(2)}) collective-permute-start(bf16[64,2176]{1,0:T(8,128)(2,1)S(1)} %slice.18), channel_id=1, source_target_pairs={{0,16},{1,3},{2,18},{3,1},{4,20},{5,7},{6,22},{7,5},{8,24},{9,11},... | collective-permute-start | bytes 835592 | tf_op jit(solution)/shard_map/ppermute | solution.py:180
  45.0 0.0 collective-permute-done.10.refs_2_
  45.0 7.6 %collective-permute-done.15.refs_2_ = bf16[64,2176]{1,0:T(8,128)(2,1)S(1)} collective-permute-done((bf16[64,2176]{1,0:T(8,128)(2,1)S(1)}, bf16[64,2176]{1,0:T(8,128)(2,1)S(1)}, u32[]{:S(2)}, u32[]{:S(2)}) %collective-permute-start.15) | collective-permute-done | bytes 278560 | tf_op jit(solution)/shard_map/ppermute | solution.py:180
  52.6 0.2 collective-permute-start.17
  52.8 0.3 collective-permute-start.16
  53.1 1.7 %slice.19 = bf16[64,2176]{1,0:T(8,128)(2,1)} slice(bf16[128,2176]{1,0:T(8,128)(2,1)} %collective-permute-done.19.refs_1_), slice={[0:64], [0:2176]} | slice | bytes 557056 | tf_op jit(solution)/shard_map/slice | solution.py:217
  54.8 1.5 %collective-permute-start.20 = (bf16[64,2176]{1,0:T(8,128)(2,1)}, bf16[64,2176]{1,0:T(8,128)(2,1)}, u32[]{:S(2)}, u32[]{:S(2)}) collective-permute-start(bf16[64,2176]{1,0:T(8,128)(2,1)} %slice.19), channel_id=1, source_target_pairs={{0,16},{1,3},{2,18},{3,1},{4,20},{5,7},{6,22},{7,5},{8,24},{9,11},... | collective-permute-start | bytes 835592 | tf_op jit(solution)/shard_map/ppermute | solution.py:180
  56.3 0.0 collective-permute-done.4.refs_1_
  56.3 0.0 collective-permute-start.21
  56.3 1.7 %slice.16 = bf16[64,2176]{1,0:T(8,128)(2,1)} slice(bf16[128,2176]{1,0:T(8,128)(2,1)} %collective-permute-done.4.refs_1_), slice={[0:64], [0:2176]} | slice | bytes 557056 | tf_op jit(solution)/shard_map/slice | solution.py:217
  58.1 0.0 collective-permute-done.11.refs_3_
  58.1 0.8 copy-done.14
  58.9 1.0 %collective-permute-start.5 = (bf16[64,2176]{1,0:T(8,128)(2,1)}, bf16[64,2176]{1,0:T(8,128)(2,1)}, u32[]{:S(2)}, u32[]{:S(2)}) collective-permute-start(bf16[64,2176]{1,0:T(8,128)(2,1)} %slice.16), channel_id=1, source_target_pairs={{0,16},{1,3},{2,18},{3,1},{4,20},{5,7},{6,22},{7,5},{8,24},{9,11},... | collective-permute-start | bytes 835592 | tf_op jit(solution)/shard_map/ppermute | solution.py:180
  59.9 0.0 collective-permute-done.17.refs_4_
  59.9 0.7 copy-done.18
  60.6 0.2 collective-permute-start.6
  60.8 0.8 collective-permute-done.20.refs_2_
  61.7 4.1 %collective-permute-done.5.refs_2_ = bf16[64,2176]{1,0:T(8,128)(2,1)} collective-permute-done((bf16[64,2176]{1,0:T(8,128)(2,1)}, bf16[64,2176]{1,0:T(8,128)(2,1)}, u32[]{:S(2)}, u32[]{:S(2)}) %collective-permute-start.5) | collective-permute-done | bytes 278560 | tf_op jit(solution)/shard_map/ppermute | solution.py:180
  65.8 0.0 collective-permute-start.7
  65.8 0.0 copy-start.1
  65.8 1.6 %copy-done.1 = bf16[1,2,256,2048]{3,2,1,0:T(8,128)(2,1)S(1)} copy-done((bf16[1,2,256,2048]{3,2,1,0:T(8,128)(2,1)S(1)}, bf16[1,2,256,2048]{3,2,1,0:T(8,128)(2,1)}, u32[]{:S(2)}) %copy-start.1) | copy-done | bytes 2097176
  67.4 1.1 %copy-done.5 = bf16[128,2176]{1,0:T(8,128)(2,1)S(1)} copy-done((bf16[128,2176]{1,0:T(8,128)(2,1)S(1)}, bf16[128,2176]{1,0:T(8,128)(2,1)}, u32[]{:S(2)}) %copy-start.5) | copy-done | bytes 557080
  68.4 1.1 %copy-done.7 = bf16[128,2176]{1,0:T(8,128)(2,1)S(1)} copy-done((bf16[128,2176]{1,0:T(8,128)(2,1)S(1)}, bf16[128,2176]{1,0:T(8,128)(2,1)}, u32[]{:S(2)}) %copy-start.7) | copy-done | bytes 557080
  69.5 1.1 %copy-done.15 = bf16[128,2176]{1,0:T(8,128)(2,1)S(1)} copy-done((bf16[128,2176]{1,0:T(8,128)(2,1)S(1)}, bf16[128,2176]{1,0:T(8,128)(2,1)}, u32[]{:S(2)}) %copy-start.15) | copy-done | bytes 557080
  70.5 1.0 %copy-done.21 = bf16[64,2176]{1,0:T(8,128)(2,1)S(1)} copy-done((bf16[64,2176]{1,0:T(8,128)(2,1)S(1)}, bf16[64,2176]{1,0:T(8,128)(2,1)}, u32[]{:S(2)}) %copy-start.21) | copy-done | bytes 278552
  71.5 1.7 %shard_map.74 = (bf16[256,2048]{1,0:T(8,128)(2,1)S(1)}, bf16[512,256]{1,0:T(8,128)(2,1)S(1)}) custom-call(bf16[128,2176]{1,0:T(8,128)(2,1)S(1)} %copy-done.5, bf16[128,2176]{1,0:T(8,128)(2,1)S(1)} %copy-done.7, bf16[64,2176]{1,0:T(8,128)(2,1)S(1)} %collective-permute-done.10.refs_2_, bf16[128,2176]{1,0:T(8,128)(2,1)S(1)} %copy-done.15, ...), custom_call_target="tpu_custom_call" | custom-call | flops 1342177280 | bytes 8388608 | tf_op jit(solution)/shard_map/pallas_call | solution.py:228
  73.2 0.0 collective-permute-done.16.refs_3_
  73.2 0.0 copy-done.17
  73.2 0.1 copy-done.19
  73.3 2.9 %shard_map.75 = (bf16[256,2048]{1,0:T(8,128)(2,1)S(1)}, bf16[512,256]{1,0:T(8,128)(2,1)S(1)}) custom-call(bf16[128,2176]{1,0:T(8,128)(2,1)S(1)} %copy-done.9, bf16[128,2176]{1,0:T(8,128)(2,1)} %collective-permute-done.14.refs_1_, bf16[64,2176]{1,0:T(8,128)(2,1)S(1)} %copy-done.17, bf16[128,2176]{1,0:T(8,128)(2,1)} %collective-permute-done.16.refs_3_, ...), custom_call_target="tpu_custom_call" | custom-call | flops 1342177280 | bytes 8388608 | tf_op jit(solution)/shard_map/pallas_call | solution.py:228
  76.3 0.0 copy-start.13
  76.3 0.0 collective-permute-done.22.refs_4_
  76.3 3.0 %shard_map.76 = (bf16[256,2048]{1,0:T(8,128)(2,1)S(1)}, bf16[512,256]{1,0:T(8,128)(2,1)S(1)}) custom-call(bf16[128,2176]{1,0:T(8,128)(2,1)S(1)} %copy-done.11, bf16[128,2176]{1,0:T(8,128)(2,1)} %collective-permute-done.19.refs_1_, bf16[64,2176]{1,0:T(8,128)(2,1)} %collective-permute-done.20.refs_2_, bf16[128,2176]{1,0:T(8,128)(2,1)} %collective-permute-done.21.refs_3_, ...), custom_call_target="tpu_custom_call" | custom-call | flops 1342177280 | bytes 8388608 | tf_op jit(solution)/shard_map/pallas_call | solution.py:228
  79.4 0.0 collective-permute-done.7.refs_4_
  79.4 0.0 collective-permute-done.6.refs_3_
  79.4 7.1 %shard_map.77 = f32[512,2048]{1,0:T(8,128)} custom-call(bf16[128,2176]{1,0:T(8,128)(2,1)S(1)} %copy-done.13, bf16[128,2176]{1,0:T(8,128)(2,1)} %collective-permute-done.4.refs_1_, bf16[64,2176]{1,0:T(8,128)(2,1)} %collective-permute-done.5.refs_2_, bf16[128,2176]{1,0:T(8,128)(2,1)} %collective-permute-done.6.refs_3_, ...), custom_call_target="tpu_custom_call" | custom-call | flops 3489660928 | bytes 16777216 | tf_op jit(solution)/shard_map/pallas_call | solution.py:244
  (44 shorter events, 0.2 us)
Async XLA Ops:
  1.8 9.9 %collective-permute-start = (bf16[64,2176]{1,0:T(8,128)(2,1)}, bf16[64,2176]{1,0:T(8,128)(2,1)S(1)}, u32[]{:S(2)}, u32[]{:S(2)}) collective-permute-start(bf16[64,2176]{1,0:T(8,128)(2,1)} %shard_map.73), channel_id=1, source_target_pairs={{0,4},{1,5},{2,6},{3,7},{4,0},{5,1},{6,2},{7,3},{8,12},{9,13},{10,... | collective-permute-start | bytes 835592 | tf_op jit(solution)/shard_map/ppermute | solution.py:180
  4.9 10.6 %collective-permute-start.8 = (bf16[64,2176]{1,0:T(8,128)(2,1)}, bf16[64,2176]{1,0:T(8,128)(2,1)S(1)}, u32[]{:S(2)}, u32[]{:S(2)}) collective-permute-start(bf16[64,2176]{1,0:T(8,128)(2,1)} %shard_map.73), channel_id=1, source_target_pairs={{0,1},{1,0},{2,3},{3,2},{4,5},{5,4},{6,7},{7,6},{8,9},{9,8},{10,11... | collective-permute-start | bytes 835592 | tf_op jit(solution)/shard_map/ppermute | solution.py:180
  11.7 10.0 %collective-permute-start.1 = (bf16[64,2176]{1,0:T(8,128)(2,1)}, bf16[64,2176]{1,0:T(8,128)(2,1)S(1)}, u32[]{:S(2)}, u32[]{:S(2)}) collective-permute-start(bf16[64,2176]{1,0:T(8,128)(2,1)} %shard_map.73), channel_id=1, source_target_pairs={{0,12},{1,13},{2,14},{3,15},{4,8},{5,9},{6,10},{7,11},{8,4},{9,5},... | collective-permute-start | bytes 835592 | tf_op jit(solution)/shard_map/ppermute | solution.py:180
  16.5 26.9 %copy-start.4 = (bf16[128,2176]{1,0:T(8,128)(2,1)}, bf16[128,2176]{1,0:T(8,128)(2,1)S(1)}, u32[]{:S(2)}) copy-start(bf16[128,2176]{1,0:T(8,128)(2,1)S(1)} %pad_maximum_fusion.refs_0_) | copy-start | bytes 1671172
  16.5 15.4 %collective-permute-start.9 = (bf16[128,2176]{1,0:T(8,128)(2,1)S(1)}, bf16[128,2176]{1,0:T(8,128)(2,1)S(1)}, u32[]{:S(2)}, u32[]{:S(2)}) collective-permute-start(bf16[128,2176]{1,0:T(8,128)(2,1)S(1)} %pad_maximum_fusion.refs_0_), channel_id=1, source_target_pairs={{0,2},{1,17},{2,0},{3,19},{4,6},{5,21},{6,4},{7,23},{8,10},{9,25},... | collective-permute-start | bytes 1671176 | tf_op jit(solution)/shard_map/ppermute | solution.py:180
  18.1 10.1 %collective-permute-start.13 = (bf16[64,2176]{1,0:T(8,128)(2,1)S(1)}, bf16[64,2176]{1,0:T(8,128)(2,1)S(1)}, u32[]{:S(2)}, u32[]{:S(2)}) collective-permute-start(bf16[64,2176]{1,0:T(8,128)(2,1)S(1)} %collective-permute-done), channel_id=1, source_target_pairs={{0,1},{1,0},{2,3},{3,2},{4,5},{5,4},{6,7},{7,6},{8,9},{9,8},{10,11... | collective-permute-start | bytes 835592 | tf_op jit(solution)/shard_map/ppermute | solution.py:180
  21.7 17.6 %collective-permute-start.2 = (bf16[64,2176]{1,0:T(8,128)(2,1)}, bf16[64,2176]{1,0:T(8,128)(2,1)S(1)}, u32[]{:S(2)}, u32[]{:S(2)}) collective-permute-start(bf16[64,2176]{1,0:T(8,128)(2,1)} %shard_map.73), channel_id=1, source_target_pairs={{0,8},{1,9},{2,10},{3,11},{4,12},{5,13},{6,14},{7,15},{8,0},{9,1},... | collective-permute-start | bytes 835592 | tf_op jit(solution)/shard_map/ppermute | solution.py:180
  28.2 29.9 %copy-start.8 = (bf16[128,2176]{1,0:T(8,128)(2,1)}, bf16[128,2176]{1,0:T(8,128)(2,1)S(1)}, u32[]{:S(2)}) copy-start(bf16[128,2176]{1,0:T(8,128)(2,1)S(1)} %constant_dynamic-update-slice_fusion.2.refs_0_) | copy-start | bytes 1671172
  28.2 14.2 %collective-permute-start.14 = (bf16[128,2176]{1,0:T(8,128)(2,1)S(1)}, bf16[128,2176]{1,0:T(8,128)(2,1)}, u32[]{:S(2)}, u32[]{:S(2)}) collective-permute-start(bf16[128,2176]{1,0:T(8,128)(2,1)S(1)} %constant_dynamic-update-slice_fusion.2.refs_0_), channel_id=1, source_target_pairs={{0,2},{1,17},{2,0},{3,19},{4,6},{5,21},{6,4},{7,23},{8,10},{9,25},... | collective-permute-start | bytes 1671176 | tf_op jit(solution)/shard_map/ppermute | solution.py:180
  29.8 1.6 %collective-permute-start.18 = (bf16[64,2176]{1,0:T(8,128)(2,1)S(1)}, bf16[64,2176]{1,0:T(8,128)(2,1)S(1)}, u32[]{:S(2)}, u32[]{:S(2)}) collective-permute-start(bf16[64,2176]{1,0:T(8,128)(2,1)S(1)} %collective-permute-done.1), channel_id=1, source_target_pairs={{0,1},{1,0},{2,3},{3,2},{4,5},{5,4},{6,7},{7,6},{8,9},{9,8},{10,11... | collective-permute-start | bytes 835592 | tf_op jit(solution)/shard_map/ppermute | solution.py:180
  29.8 36.0 %copy-start = (bf16[1,2,256,2048]{3,2,1,0:T(8,128)(2,1)S(1)}, bf16[1,2,256,2048]{3,2,1,0:T(8,128)(2,1)}, u32[]{:S(2)}) copy-start(bf16[1,2,256,2048]{3,2,1,0:T(8,128)(2,1)} %param.11) | copy-start | bytes 6291460
  29.8 36.0 %copy-start.3 = (bf16[1,256,2048]{2,1,0:T(8,128)(2,1)S(1)}, bf16[1,256,2048]{2,1,0:T(8,128)(2,1)}, u32[]{:S(2)}) copy-start(bf16[1,256,2048]{2,1,0:T(8,128)(2,1)} %param.12) | copy-start | bytes 3145732
  31.4 26.7 %copy-start.10 = (bf16[128,2176]{1,0:T(8,128)(2,1)}, bf16[128,2176]{1,0:T(8,128)(2,1)S(1)}, u32[]{:S(2)}) copy-start(bf16[128,2176]{1,0:T(8,128)(2,1)S(1)} %constant_dynamic-update-slice_fusion.4.refs_0_) | copy-start | bytes 1671172
  31.4 21.4 %collective-permute-start.19 = (bf16[128,2176]{1,0:T(8,128)(2,1)S(1)}, bf16[128,2176]{1,0:T(8,128)(2,1)}, u32[]{:S(2)}, u32[]{:S(2)}) collective-permute-start(bf16[128,2176]{1,0:T(8,128)(2,1)S(1)} %constant_dynamic-update-slice_fusion.4.refs_0_), channel_id=1, source_target_pairs={{0,2},{1,17},{2,0},{3,19},{4,6},{5,21},{6,4},{7,23},{8,10},{9,25},... | collective-permute-start | bytes 1671176 | tf_op jit(solution)/shard_map/ppermute | solution.py:180
  32.0 13.0 %copy-start.6 = (bf16[128,2176]{1,0:T(8,128)(2,1)}, bf16[128,2176]{1,0:T(8,128)(2,1)S(1)}, u32[]{:S(2)}) copy-start(bf16[128,2176]{1,0:T(8,128)(2,1)S(1)} %collective-permute-done.9.refs_1_) | copy-start | bytes 1671172
  32.0 13.0 %collective-permute-start.10 = (bf16[64,2176]{1,0:T(8,128)(2,1)S(1)}, bf16[64,2176]{1,0:T(8,128)(2,1)S(1)}, u32[]{:S(2)}, u32[]{:S(2)}) collective-permute-start(bf16[64,2176]{1,0:T(8,128)(2,1)S(1)} %slice.17), channel_id=1, source_target_pairs={{0,16},{1,3},{2,18},{3,1},{4,20},{5,7},{6,22},{7,5},{8,24},{9,11},... | collective-permute-start | bytes 835592 | tf_op jit(solution)/shard_map/ppermute | solution.py:180
  39.2 1.6 %collective-permute-start.3 = (bf16[64,2176]{1,0:T(8,128)(2,1)S(1)}, bf16[64,2176]{1,0:T(8,128)(2,1)S(1)}, u32[]{:S(2)}, u32[]{:S(2)}) collective-permute-start(bf16[64,2176]{1,0:T(8,128)(2,1)S(1)} %collective-permute-done.2), channel_id=1, source_target_pairs={{0,1},{1,0},{2,3},{3,2},{4,5},{5,4},{6,7},{7,6},{8,9},{9,8},{10,11... | collective-permute-start | bytes 835592 | tf_op jit(solution)/shard_map/ppermute | solution.py:180
  40.8 19.1 %copy-start.12 = (bf16[128,2176]{1,0:T(8,128)(2,1)}, bf16[128,2176]{1,0:T(8,128)(2,1)S(1)}, u32[]{:S(2)}) copy-start(bf16[128,2176]{1,0:T(8,128)(2,1)S(1)} %constant_dynamic-update-slice_fusion.refs_0_) | copy-start | bytes 1671172
  40.8 15.5 %collective-permute-start.4 = (bf16[128,2176]{1,0:T(8,128)(2,1)S(1)}, bf16[128,2176]{1,0:T(8,128)(2,1)}, u32[]{:S(2)}, u32[]{:S(2)}) collective-permute-start(bf16[128,2176]{1,0:T(8,128)(2,1)S(1)} %constant_dynamic-update-slice_fusion.refs_0_), channel_id=1, source_target_pairs={{0,2},{1,17},{2,0},{3,19},{4,6},{5,21},{6,4},{7,23},{8,10},{9,25},... | collective-permute-start | bytes 1671176 | tf_op jit(solution)/shard_map/ppermute | solution.py:180
  42.4 15.7 %collective-permute-start.11 = (bf16[128,2176]{1,0:T(8,128)(2,1)S(1)}, bf16[128,2176]{1,0:T(8,128)(2,1)S(1)}, u32[]{:S(2)}, u32[]{:S(2)}) collective-permute-start(bf16[128,2176]{1,0:T(8,128)(2,1)S(1)} %collective-permute-done.9.refs_1_), channel_id=1, source_target_pairs={{0,1},{1,0},{2,3},{3,2},{4,5},{5,4},{6,7},{7,6},{8,9},{9,8},{10,11... | collective-permute-start | bytes 1671176 | tf_op jit(solution)/shard_map/ppermute | solution.py:180
  43.4 9.2 %collective-permute-start.15 = (bf16[64,2176]{1,0:T(8,128)(2,1)S(1)}, bf16[64,2176]{1,0:T(8,128)(2,1)S(1)}, u32[]{:S(2)}, u32[]{:S(2)}) collective-permute-start(bf16[64,2176]{1,0:T(8,128)(2,1)S(1)} %slice.18), channel_id=1, source_target_pairs={{0,16},{1,3},{2,18},{3,1},{4,20},{5,7},{6,22},{7,5},{8,24},{9,11},... | collective-permute-start | bytes 835592 | tf_op jit(solution)/shard_map/ppermute | solution.py:180
  45.0 9.8 %collective-permute-start.12 = (bf16[64,2176]{1,0:T(8,128)(2,1)S(1)}, bf16[64,2176]{1,0:T(8,128)(2,1)S(1)}, u32[]{:S(2)}, u32[]{:S(2)}) collective-permute-start(bf16[64,2176]{1,0:T(8,128)(2,1)S(1)} %collective-permute-done.10.refs_2_), channel_id=1, source_target_pairs={{0,1},{1,0},{2,3},{3,2},{4,5},{5,4},{6,7},{7,6},{8,9},{9,8},{10,11... | collective-permute-start | bytes 835592 | tf_op jit(solution)/shard_map/ppermute | solution.py:180
  52.6 7.3 %copy-start.16 = (bf16[64,2176]{1,0:T(8,128)(2,1)}, bf16[64,2176]{1,0:T(8,128)(2,1)S(1)}, u32[]{:S(2)}) copy-start(bf16[64,2176]{1,0:T(8,128)(2,1)S(1)} %collective-permute-done.15.refs_2_) | copy-start | bytes 835588
  52.6 7.3 %collective-permute-start.17 = (bf16[64,2176]{1,0:T(8,128)(2,1)S(1)}, bf16[64,2176]{1,0:T(8,128)(2,1)S(1)}, u32[]{:S(2)}, u32[]{:S(2)}) collective-permute-start(bf16[64,2176]{1,0:T(8,128)(2,1)S(1)} %collective-permute-done.15.refs_2_), channel_id=1, source_target_pairs={{0,1},{1,0},{2,3},{3,2},{4,5},{5,4},{6,7},{7,6},{8,9},{9,8},{10,11... | collective-permute-start | bytes 835592 | tf_op jit(solution)/shard_map/ppermute | solution.py:180
  52.8 20.4 %collective-permute-start.16 = (bf16[128,2176]{1,0:T(8,128)(2,1)}, bf16[128,2176]{1,0:T(8,128)(2,1)}, u32[]{:S(2)}, u32[]{:S(2)}) collective-permute-start(bf16[128,2176]{1,0:T(8,128)(2,1)} %collective-permute-done.14.refs_1_), channel_id=1, source_target_pairs={{0,1},{1,0},{2,3},{3,2},{4,5},{5,4},{6,7},{7,6},{8,9},{9,8},{10,11... | collective-permute-start | bytes 1671176 | tf_op jit(solution)/shard_map/ppermute | solution.py:180
  54.8 6.0 %copy-start.20 = (bf16[64,2176]{1,0:T(8,128)(2,1)}, bf16[64,2176]{1,0:T(8,128)(2,1)S(1)}, u32[]{:S(2)}) copy-start(bf16[64,2176]{1,0:T(8,128)(2,1)S(1)} %collective-permute-done.12.refs_4_) | copy-start | bytes 835588
  54.8 6.9 %collective-permute-start.20 = (bf16[64,2176]{1,0:T(8,128)(2,1)}, bf16[64,2176]{1,0:T(8,128)(2,1)}, u32[]{:S(2)}, u32[]{:S(2)}) collective-permute-start(bf16[64,2176]{1,0:T(8,128)(2,1)} %slice.19), channel_id=1, source_target_pairs={{0,16},{1,3},{2,18},{3,1},{4,20},{5,7},{6,22},{7,5},{8,24},{9,11},... | collective-permute-start | bytes 835592 | tf_op jit(solution)/shard_map/ppermute | solution.py:180
  56.3 19.9 %collective-permute-start.21 = (bf16[128,2176]{1,0:T(8,128)(2,1)}, bf16[128,2176]{1,0:T(8,128)(2,1)}, u32[]{:S(2)}, u32[]{:S(2)}) collective-permute-start(bf16[128,2176]{1,0:T(8,128)(2,1)} %collective-permute-done.19.refs_1_), channel_id=1, source_target_pairs={{0,1},{1,0},{2,3},{3,2},{4,5},{5,4},{6,7},{7,6},{8,9},{9,8},{10,11... | collective-permute-start | bytes 1671176 | tf_op jit(solution)/shard_map/ppermute | solution.py:180
  58.1 0.8 copy-start.14
  58.9 6.9 %collective-permute-start.5 = (bf16[64,2176]{1,0:T(8,128)(2,1)}, bf16[64,2176]{1,0:T(8,128)(2,1)}, u32[]{:S(2)}, u32[]{:S(2)}) collective-permute-start(bf16[64,2176]{1,0:T(8,128)(2,1)} %slice.16), channel_id=1, source_target_pairs={{0,16},{1,3},{2,18},{3,1},{4,20},{5,7},{6,22},{7,5},{8,24},{9,11},... | collective-permute-start | bytes 835592 | tf_op jit(solution)/shard_map/ppermute | solution.py:180
  59.9 0.7 copy-start.18
  60.6 18.7 %collective-permute-start.6 = (bf16[128,2176]{1,0:T(8,128)(2,1)}, bf16[128,2176]{1,0:T(8,128)(2,1)}, u32[]{:S(2)}, u32[]{:S(2)}) collective-permute-start(bf16[128,2176]{1,0:T(8,128)(2,1)} %collective-permute-done.4.refs_1_), channel_id=1, source_target_pairs={{0,1},{1,0},{2,3},{3,2},{4,5},{5,4},{6,7},{7,6},{8,9},{9,8},{10,11... | collective-permute-start | bytes 1671176 | tf_op jit(solution)/shard_map/ppermute | solution.py:180
  61.7 14.6 %collective-permute-start.22 = (bf16[64,2176]{1,0:T(8,128)(2,1)}, bf16[64,2176]{1,0:T(8,128)(2,1)S(1)}, u32[]{:S(2)}, u32[]{:S(2)}) collective-permute-start(bf16[64,2176]{1,0:T(8,128)(2,1)} %collective-permute-done.20.refs_2_), channel_id=1, source_target_pairs={{0,1},{1,0},{2,3},{3,2},{4,5},{5,4},{6,7},{7,6},{8,9},{9,8},{10,11... | collective-permute-start | bytes 835592 | tf_op jit(solution)/shard_map/ppermute | solution.py:180
  65.8 13.6 %collective-permute-start.7 = (bf16[64,2176]{1,0:T(8,128)(2,1)}, bf16[64,2176]{1,0:T(8,128)(2,1)S(1)}, u32[]{:S(2)}, u32[]{:S(2)}) collective-permute-start(bf16[64,2176]{1,0:T(8,128)(2,1)} %collective-permute-done.5.refs_2_), channel_id=1, source_target_pairs={{0,1},{1,0},{2,3},{3,2},{4,5},{5,4},{6,7},{7,6},{8,9},{9,8},{10,11... | collective-permute-start | bytes 835592 | tf_op jit(solution)/shard_map/ppermute | solution.py:180
  65.8 1.6 %copy-start.1 = (bf16[1,2,256,2048]{3,2,1,0:T(8,128)(2,1)S(1)}, bf16[1,2,256,2048]{3,2,1,0:T(8,128)(2,1)}, u32[]{:S(2)}) copy-start(bf16[1,2,256,2048]{3,2,1,0:T(8,128)(2,1)} %param.13) | copy-start | bytes 6291460
  67.4 1.1 %copy-start.5 = (bf16[128,2176]{1,0:T(8,128)(2,1)S(1)}, bf16[128,2176]{1,0:T(8,128)(2,1)}, u32[]{:S(2)}) copy-start(bf16[128,2176]{1,0:T(8,128)(2,1)} %copy-done.4) | copy-start | bytes 1671172
  68.4 1.1 %copy-start.7 = (bf16[128,2176]{1,0:T(8,128)(2,1)S(1)}, bf16[128,2176]{1,0:T(8,128)(2,1)}, u32[]{:S(2)}) copy-start(bf16[128,2176]{1,0:T(8,128)(2,1)} %copy-done.6) | copy-start | bytes 1671172
  69.5 1.1 %copy-start.15 = (bf16[128,2176]{1,0:T(8,128)(2,1)S(1)}, bf16[128,2176]{1,0:T(8,128)(2,1)}, u32[]{:S(2)}) copy-start(bf16[128,2176]{1,0:T(8,128)(2,1)} %copy-done.14) | copy-start | bytes 1671172
  70.5 1.0 %copy-start.21 = (bf16[64,2176]{1,0:T(8,128)(2,1)S(1)}, bf16[64,2176]{1,0:T(8,128)(2,1)}, u32[]{:S(2)}) copy-start(bf16[64,2176]{1,0:T(8,128)(2,1)} %copy-done.20) | copy-start | bytes 835588
  71.5 1.7 %copy-start.2 = (bf16[1,2,256,2048]{3,2,1,0:T(8,128)(2,1)S(1)}, bf16[1,2,256,2048]{3,2,1,0:T(8,128)(2,1)}, u32[]{:S(2)}) copy-start(bf16[1,2,256,2048]{3,2,1,0:T(8,128)(2,1)} %param.13) | copy-start | bytes 6291460
  71.5 1.7 %copy-start.9 = (bf16[128,2176]{1,0:T(8,128)(2,1)S(1)}, bf16[128,2176]{1,0:T(8,128)(2,1)}, u32[]{:S(2)}) copy-start(bf16[128,2176]{1,0:T(8,128)(2,1)} %copy-done.8) | copy-start | bytes 1671172
  71.5 1.7 %copy-start.17 = (bf16[64,2176]{1,0:T(8,128)(2,1)S(1)}, bf16[64,2176]{1,0:T(8,128)(2,1)}, u32[]{:S(2)}) copy-start(bf16[64,2176]{1,0:T(8,128)(2,1)} %copy-done.16) | copy-start | bytes 835588
  71.5 1.8 %copy-start.19 = (bf16[64,2176]{1,0:T(8,128)(2,1)S(1)}, bf16[64,2176]{1,0:T(8,128)(2,1)}, u32[]{:S(2)}) copy-start(bf16[64,2176]{1,0:T(8,128)(2,1)} %copy-done.18) | copy-start | bytes 835588
  73.2 3.1 %copy-start.11 = (bf16[128,2176]{1,0:T(8,128)(2,1)S(1)}, bf16[128,2176]{1,0:T(8,128)(2,1)}, u32[]{:S(2)}) copy-start(bf16[128,2176]{1,0:T(8,128)(2,1)} %copy-done.10) | copy-start | bytes 1671172
  76.3 3.1 %copy-start.13 = (bf16[128,2176]{1,0:T(8,128)(2,1)S(1)}, bf16[128,2176]{1,0:T(8,128)(2,1)}, u32[]{:S(2)}) copy-start(bf16[128,2176]{1,0:T(8,128)(2,1)} %copy-done.12) | copy-start | bytes 1671172

commit v4 on v3

--- a/solution.py
+++ b/solution.py
@@ -201,67 +201,82 @@
     mine = (lane % experts == lax.axis_index("expert")) & (lane < 3 * experts)
     pick = jnp.broadcast_to(mine.astype(jnp.bfloat16)[None, :], (16, LANES))
 
-    slices = [own]
-    for mask in (Z_NEAR, Z_NEAR ^ Z_FAR, Z_FAR):
-        sent = own if len(slices) == 1 else after(own, slices[-1])
-        slices.append(swap(sent, (mask, mask)))
     weights = (
         w_in.reshape(2 * half, model_dim),
         v_in.reshape(2 * half, model_dim),
         w_out.reshape(half, model_dim),
     )
-    held = []
-    for n, block in enumerate(slices):
-        chip = jnp.concatenate([block, swap(block, (CORE, CORE))], axis=0)
-        beside = swap(chip, (X, Y))
-        across = swap(beside[: 2 * tok_dev], (Y, X))
+
+    def share(blocks, *first):
+        others = [swap(b, (CORE, CORE)) for b in blocks]
+        others[0] = after(others[0], *first)
+        return jnp.concatenate(blocks + others, axis=0)
+
+    def cross(chip, *first):
+        beside = after(swap(chip, (X, Y)), *first)
+        onward = beside[: chip.shape[0] // 2]
+        across = swap(onward, (Y, X))
         pieces = [chip, beside, across]
-        pieces += [swap(got, (CORE, CORE)) for got in (beside, across)]
+        return pieces + [swap(got, (CORE, CORE)) for got in (beside, across)], onward
+
+    def call(pieces, held, last):
         rows = sum(p.shape[0] for p in pieces) // 2
-        last = n == len(slices) - 1
+        total = rows + sum(h.shape[0] for h in held[0::2])
         scratch = [
             pltpu.VMEM((rows, model_dim), jnp.bfloat16),
             pltpu.VMEM((rows, LANES), jnp.bfloat16),
         ]
-        params = pltpu.CompilerParams(vmem_limit_bytes=28 * 2**20)
+        kinds = dict(
+            in_specs=[inside] * (len(pieces) + len(held) + 4),
+            compiler_params=pltpu.CompilerParams(vmem_limit_bytes=20 * 2**20),
+            cost_estimate=pl.CostEstimate(
+                flops=2 * model_dim * half * (5 * rows + 2 * total * last),
+                bytes_accessed=8 * 2**20,
+                transcendentals=rows * half,
+            ),
+        )
         if not last:
-            held += pl.pallas_call(
+            return pl.pallas_call(
                 functools.partial(slice_kernel, count=len(pieces), tok_dev=tok_dev),
-                in_specs=[inside] * (len(pieces) + 4),
                 out_specs=[inside] * 2,
                 out_shape=[
                     jax.ShapeDtypeStruct((rows, model_dim), jnp.bfloat16),
                     jax.ShapeDtypeStruct((2 * half, rows), jnp.bfloat16),
                 ],
                 scratch_shapes=scratch,
-                compiler_params=params,
-                cost_estimate=pl.CostEstimate(
-                    flops=2 * rows * model_dim * 5 * half,
-                    bytes_accessed=8 * 2**20,
-                    transcendentals=rows * half,
-                ),
+                **kinds,
             )(*pieces, pick, *weights)
-    out = pl.pallas_call(
-        functools.partial(
-            last_kernel, count=len(pieces), earlier=len(held) // 2, tok_dev=tok_dev
-        ),
-        in_specs=[inside] * (len(pieces) + len(held) + 4),
-        out_specs=pl.BlockSpec(memory_space=pl.ANY),
-        out_shape=jax.ShapeDtypeStruct((2 * half, model_dim), jnp.float32),
-        scratch_shapes=[pltpu.VMEM((rows, model_dim), jnp.bfloat16)]
-        + scratch
-        + [
-            pltpu.VMEM((2 * half, rows), jnp.bfloat16),
-            pltpu.VMEM((2 * half, model_dim), jnp.float32),
-            pltpu.SemaphoreType.DMA((model_dim // 512,)),
-        ],
-        compiler_params=params,
-        cost_estimate=pl.CostEstimate(
-            flops=2 * rows * model_dim * 13 * half,
-            bytes_accessed=16 * 2**20,
-            transcendentals=rows * half,
-        ),
-    )(*pieces, *held, pick, *weights)
+        return pl.pallas_call(
+            functools.partial(
+                last_kernel, count=len(pieces), earlier=len(held) // 2, tok_dev=tok_dev
+            ),
+            out_specs=pl.BlockSpec(memory_space=pl.ANY),
+            out_shape=jax.ShapeDtypeStruct((2 * half, model_dim), jnp.float32),
+            scratch_shapes=[pltpu.VMEM((rows, model_dim), jnp.bfloat16)]
+            + scratch
+            + [
+                pltpu.VMEM((2 * half, rows), jnp.bfloat16),
+                pltpu.VMEM((2 * half, model_dim), jnp.float32),
+                pltpu.SemaphoreType.DMA((model_dim // 512,)),
+            ],
+            **kinds,
+        )(*pieces, *held, pick, *weights)
+
+    near = swap(own, (Z_NEAR, Z_NEAR))
+    middle = swap(own, (Z_NEAR ^ Z_FAR, Z_NEAR ^ Z_FAR))
+    chip_a = share([own])
+    pieces_a, onward_a = cross(chip_a)
+    near, middle, _ = lax.optimization_barrier((near, middle, onward_a))
+    far = swap(after(own, near), (Z_FAR, Z_FAR))
+    chip_b = share([near, middle], pieces_a[2])
+    pieces_a[0] = after(pieces_a[0], chip_b)
+    held_a = call(pieces_a, [], False)
+    chip_c = share([after(far, held_a[1])])
+    pieces_b, onward_b = cross(chip_b, chip_c)
+    pieces_c, onward_c = cross(chip_c, onward_b)
+    pieces_b[0] = after(pieces_b[0], onward_c)
+    held_b = call(pieces_b, [], False)
+    out = call(pieces_c, [*held_a, *held_b], True)
     return out.reshape(1, 2, half, model_dim)
 
 

time: 87 us -> 88 us (1.011)
  waiting for transfers between devices: 31.6 us -> 47.4 us
  starting transfers between devices: 25 us -> 15 us
  local copies, waits for them, and re-layouts: 11.9 us -> 7.67 us
  Pallas kernels: 16.5 us -> 15.3 us
  other arithmetic: 1.03 us -> 2.09 us
    ppermute x23 -> x19, waiting for transfers between devices: 31.6 us -> 47.4 us  [swap(): lax.ppermute(value, axes, [(i, i ^ masks[i & CORE]) for i in range(count)])]
    ppermute x23 -> x19, starting transfers between devices: 25 us -> 15 us  [swap(): lax.ppermute(value, axes, [(i, i ^ masks[i & CORE]) for i in range(count)])]
    unnamed x47 -> x15, local copies, waits for them, and re-layouts: 7.42 us -> 4.84 us
    slice x4 -> x3, local copies, waits for them, and re-layouts: 4.43 us -> 2.09 us  [cross(): onward = beside[:chip.shape[0] // 2]]
    pallas_call x4 -> x3, Pallas kernels: 14.7 us -> 13.5 us  [the longest x2 7.75 us: call(): pl.pallas_call(functools.partial(slice_kernel, count=len(pieces), tok_dev...]
    concatenate x1 -> x2, other arithmetic: 1.03 us -> 2.08 us  [share(): return jnp.concatenate(blocks + others, axis=0)]
  transfers between devices with their start and end apart: 23 -> 19, of which waited for: 8 -> 9; matrix products, arithmetic and copies ran while one was open for 6% -> 5% of each run, Pallas kernels for 9% -> 9%
where the time goes in v4:
time: 88 us; the launch traced here: 87.6 us
  waiting for transfers between devices  47.4 us (54%)
  Pallas kernels  15.3 us (17%)
  starting transfers between devices  15 us (17%)
  local copies, waits for them, and re-layouts  7.67 us (9%)
  other arithmetic  2.09 us (2%)
    ppermute x19, waiting for transfers between devices, swap(): lax.ppermute(value, axes, [(i, i ^ masks[i & CORE]) for i in range(count)])  47.4 us
    ppermute x19, starting transfers between devices, swap(): lax.ppermute(value, axes, [(i, i ^ masks[i & CORE]) for i in range(count)])  15 us
    pallas_call x2, Pallas kernels, call(): pl.pallas_call(functools.partial(slice_kernel, count=len(pieces), tok_dev...  7.75 us
    pallas_call x1, Pallas kernels, call(): pl.pallas_call(functools.partial(last_kernel, count=len(pieces), earlier=...  5.75 us
    unnamed x15, local copies, waits for them, and re-layouts  4.84 us
    slice x3, local copies, waits for them, and re-layouts, cross(): onward = beside[:chip.shape[0] // 2]  2.09 us
    concatenate x2, other arithmetic, share(): return jnp.concatenate(blocks + others, axis=0)  2.08 us
    pallas_call x1, Pallas kernels, dense(): pl.pallas_call(functools.partial(pack_kernel, experts=experts), in_specs=...  1.82 us
  transfers between devices with their start and end apart: 19, of which 9 were waited for; matrix products, arithmetic and copies ran while one was open for 5% of the time, Pallas kernels for 9%

profile of v4, /device:TPU:0, one launch (start us, length us, event | category | flops | bytes accessed | tf_op | source)
XLA Modules:
  0.0 87.6 jit_solution(17607389765543048362)
XLA Ops:
  0.0 1.8 %shard_map.73 = bf16[64,2176]{1,0:T(8,128)(2,1)} custom-call(bf16[32,2048]{1,0:T(8,128)(2,1)} %tok_ref.1, bf16[32,2048]{1,0:T(8,128)(2,1)} %cot_ref.1, s32[8,32]{1,0:T(8,128)} %bitcast.15, f32[8,32]{1,0:T(8,128)} %bitcast.16), custom_call_target="tpu_custom_call" | custom-call | tf_op jit(solution)/shard_map/pallas_call | solution.py:193
  1.8 0.5 collective-permute-start.2
  2.3 1.4 %collective-permute-done.2 = bf16[64,2176]{1,0:T(8,128)(2,1)S(1)} collective-permute-done((bf16[64,2176]{1,0:T(8,128)(2,1)}, bf16[64,2176]{1,0:T(8,128)(2,1)S(1)}, u32[]{:S(2)}, u32[]{:S(2)}) %collective-permute-start.2) | collective-permute-done | bytes 278560 | tf_op jit(solution)/shard_map/ppermute | solution.py:180
  3.7 0.0 copy-start.3
  3.7 1.1 %pad_maximum_fusion.refs_0_ = bf16[128,2176]{1,0:T(8,128)(2,1)S(1)} fusion(bf16[64,2176]{1,0:T(8,128)(2,1)S(1)} %collective-permute-done.2, bf16[64,2176]{1,0:T(8,128)(2,1)} %shard_map.73), kind=kLoop, calls=%fused_computation | loop fusion | flops 1114112 | bytes 1114112 | tf_op jit(solution)/shard_map/concatenate | solution.py:213
  4.8 0.0 copy-start.4
  4.8 2.9 %collective-permute-start.3 = (bf16[128,2176]{1,0:T(8,128)(2,1)S(1)}, bf16[128,2176]{1,0:T(8,128)(2,1)}, u32[]{:S(2)}, u32[]{:S(2)}) collective-permute-start(bf16[128,2176]{1,0:T(8,128)(2,1)S(1)} %pad_maximum_fusion.refs_0_), channel_id=1, source_target_pairs={{0,2},{1,17},{2,0},{3,19},{4,6},{5,21},{6,4},{7,23},{8,10},{9,25},... | collective-permute-start | bytes 1671176 | tf_op jit(solution)/shard_map/ppermute | solution.py:180
  7.7 1.6 %collective-permute-start = (bf16[64,2176]{1,0:T(8,128)(2,1)}, bf16[64,2176]{1,0:T(8,128)(2,1)S(1)}, u32[]{:S(2)}, u32[]{:S(2)}) collective-permute-start(bf16[64,2176]{1,0:T(8,128)(2,1)} %shard_map.73), channel_id=1, source_target_pairs={{0,4},{1,5},{2,6},{3,7},{4,0},{5,1},{6,2},{7,3},{8,12},{9,13},{10,... | collective-permute-start | bytes 835592 | tf_op jit(solution)/shard_map/ppermute | solution.py:180
  9.3 2.5 %collective-permute-start.1 = (bf16[64,2176]{1,0:T(8,128)(2,1)}, bf16[64,2176]{1,0:T(8,128)(2,1)S(1)}, u32[]{:S(2)}, u32[]{:S(2)}) collective-permute-start(bf16[64,2176]{1,0:T(8,128)(2,1)} %shard_map.73), channel_id=1, source_target_pairs={{0,12},{1,13},{2,14},{3,15},{4,8},{5,9},{6,10},{7,11},{8,4},{9,5},... | collective-permute-start | bytes 835592 | tf_op jit(solution)/shard_map/ppermute | solution.py:180
  11.8 3.6 %collective-permute-done.3.refs_1_ = bf16[128,2176]{1,0:T(8,128)(2,1)} collective-permute-done((bf16[128,2176]{1,0:T(8,128)(2,1)S(1)}, bf16[128,2176]{1,0:T(8,128)(2,1)}, u32[]{:S(2)}, u32[]{:S(2)}) %collective-permute-start.3) | collective-permute-done | bytes 557088 | tf_op jit(solution)/shard_map/ppermute | solution.py:180
  15.3 1.0 %slice.12 = bf16[64,2176]{1,0:T(8,128)(2,1)S(1)} slice(bf16[128,2176]{1,0:T(8,128)(2,1)} %collective-permute-done.3.refs_1_), slice={[0:64], [0:2176]} | slice | bytes 557056 | tf_op jit(solution)/shard_map/slice | solution.py:217
  16.3 0.0 copy-start
  16.3 0.3 collective-permute-done
  16.6 7.8 %collective-permute-done.1 = bf16[64,2176]{1,0:T(8,128)(2,1)S(1)} collective-permute-done((bf16[64,2176]{1,0:T(8,128)(2,1)}, bf16[64,2176]{1,0:T(8,128)(2,1)S(1)}, u32[]{:S(2)}, u32[]{:S(2)}) %collective-permute-start.1) | collective-permute-done | bytes 278560 | tf_op jit(solution)/shard_map/ppermute | solution.py:180
  24.5 0.7 constant_dynamic-update-slice_fusion.3
  25.2 0.0 collective-permute-start.5
  25.2 0.5 collective-permute-start.6
  25.7 1.2 %collective-permute-start.8 = (bf16[128,2176]{1,0:T(8,128)(2,1)}, bf16[128,2176]{1,0:T(8,128)(2,1)}, u32[]{:S(2)}, u32[]{:S(2)}) collective-permute-start(bf16[128,2176]{1,0:T(8,128)(2,1)} %collective-permute-done.3.refs_1_), channel_id=1, source_target_pairs={{0,1},{1,0},{2,3},{3,2},{4,5},{5,4},{6,7},{7,6},{8,9},{9,8},{10,11... | collective-permute-start | bytes 1671176 | tf_op jit(solution)/shard_map/ppermute | solution.py:180
  26.9 0.0 collective-permute-start.7
  26.9 0.7 constant_dynamic-update-slice_fusion.2
  27.6 0.0 collective-permute-done.5
  27.6 4.1 %collective-permute-done.6.refs_2_ = bf16[64,2176]{1,0:T(8,128)(2,1)S(1)} collective-permute-done((bf16[64,2176]{1,0:T(8,128)(2,1)S(1)}, bf16[64,2176]{1,0:T(8,128)(2,1)S(1)}, u32[]{:S(2)}, u32[]{:S(2)}) %collective-permute-start.6) | collective-permute-done | bytes 278560 | tf_op jit(solution)/shard_map/ppermute | solution.py:180
  31.7 0.7 constant_dynamic-update-slice_fusion.1
  32.5 0.0 copy-done.4
  32.5 0.0 collective-permute-done.7
  32.5 0.7 constant_dynamic-update-slice_fusion.refs_0_
  33.2 1.5 %collective-permute-start.12 = (bf16[256,2176]{1,0:T(8,128)(2,1)}, bf16[256,2176]{1,0:T(8,128)(2,1)}, u32[]{:S(2)}, u32[]{:S(2)}) collective-permute-start(bf16[256,2176]{1,0:T(8,128)(2,1)} %constant_dynamic-update-slice_fusion.refs_0_), channel_id=1, source_target_pairs={{0,2},{1,17},{2,0},{3,19},{4,6},{5,21},{6,4},{7,23},{8,10},{9,25},... | collective-permute-start | bytes 3342344 | tf_op jit(solution)/shard_map/ppermute | solution.py:180
  34.7 0.0 collective-permute-start.9
  34.7 1.8 %collective-permute-start.4 = (bf16[64,2176]{1,0:T(8,128)(2,1)}, bf16[64,2176]{1,0:T(8,128)(2,1)}, u32[]{:S(2)}, u32[]{:S(2)}) collective-permute-start(bf16[64,2176]{1,0:T(8,128)(2,1)} %shard_map.73), channel_id=1, source_target_pairs={{0,8},{1,9},{2,10},{3,11},{4,12},{5,13},{6,14},{7,15},{8,0},{9,1},... | collective-permute-start | bytes 835592 | tf_op jit(solution)/shard_map/ppermute | solution.py:180
  36.5 0.0 collective-permute-done.9.refs_4_
  36.5 0.0 collective-permute-done.8.refs_3_
  36.5 0.0 copy-done.3
  36.5 0.0 copy-done
  36.5 0.0 copy-start.1
  36.5 1.6 %copy-done.1 = bf16[1,2,256,2048]{3,2,1,0:T(8,128)(2,1)S(1)} copy-done((bf16[1,2,256,2048]{3,2,1,0:T(8,128)(2,1)S(1)}, bf16[1,2,256,2048]{3,2,1,0:T(8,128)(2,1)}, u32[]{:S(2)}) %copy-start.1) | copy-done | bytes 2097176
  38.1 0.0 copy-start.5
  38.1 1.1 %copy-done.5 = bf16[128,2176]{1,0:T(8,128)(2,1)S(1)} copy-done((bf16[128,2176]{1,0:T(8,128)(2,1)S(1)}, bf16[128,2176]{1,0:T(8,128)(2,1)}, u32[]{:S(2)}) %copy-start.5) | copy-done | bytes 557080
  39.2 3.0 %shard_map.74 = (bf16[256,2048]{1,0:T(8,128)(2,1)S(1)}, bf16[512,256]{1,0:T(8,128)(2,1)S(1)}) custom-call(bf16[128,2176]{1,0:T(8,128)(2,1)S(1)} %copy-done.5, bf16[128,2176]{1,0:T(8,128)(2,1)} %collective-permute-done.3.refs_1_, bf16[64,2176]{1,0:T(8,128)(2,1)S(1)} %collective-permute-done.6.refs_2_, bf16[128,2176]{1,0:T(8,128)(2,1)} %collective-permute-done.8.refs_3_, ...), custom_call_target="tpu_custom_call" | custom-call | flops 1342177280 | bytes 8388608 | tf_op jit(solution)/shard_map/pallas_call | solution.py:239
  42.1 8.8 %collective-permute-done.4 = bf16[64,2176]{1,0:T(8,128)(2,1)} collective-permute-done((bf16[64,2176]{1,0:T(8,128)(2,1)}, bf16[64,2176]{1,0:T(8,128)(2,1)}, u32[]{:S(2)}, u32[]{:S(2)}) %collective-permute-start.4) | collective-permute-done | bytes 278560 | tf_op jit(solution)/shard_map/ppermute | solution.py:180
  51.0 0.0 copy-start.2
  51.0 0.0 collective-permute-start.10
  51.0 1.8 %collective-permute-done.10 = bf16[64,2176]{1,0:T(8,128)(2,1)S(1)} collective-permute-done((bf16[64,2176]{1,0:T(8,128)(2,1)}, bf16[64,2176]{1,0:T(8,128)(2,1)S(1)}, u32[]{:S(2)}, u32[]{:S(2)}) %collective-permute-start.10) | collective-permute-done | bytes 278560 | tf_op jit(solution)/shard_map/ppermute | solution.py:180
  52.7 1.0 %pad_maximum_fusion.1.refs_0_ = bf16[128,2176]{1,0:T(8,128)(2,1)S(1)} fusion(bf16[64,2176]{1,0:T(8,128)(2,1)S(1)} %collective-permute-done.10, bf16[64,2176]{1,0:T(8,128)(2,1)} %collective-permute-done.4), kind=kLoop, calls=%fused_computation.1 | loop fusion | flops 1114112 | bytes 1114112 | tf_op jit(solution)/shard_map/concatenate | solution.py:213
  53.7 0.0 collective-permute-done.12.refs_1_
  53.7 1.1 %slice.10 = bf16[128,2176]{1,0:T(8,128)(2,1)S(1)} slice(bf16[256,2176]{1,0:T(8,128)(2,1)} %collective-permute-done.12.refs_1_), slice={[0:128], [0:2176]} | slice | bytes 1114112 | tf_op jit(solution)/shard_map/slice | solution.py:217
  54.8 0.6 collective-permute-start.16
  55.4 0.0 collective-permute-start.17
  55.4 1.4 %collective-permute-start.11 = (bf16[128,2176]{1,0:T(8,128)(2,1)S(1)}, bf16[128,2176]{1,0:T(8,128)(2,1)S(1)}, u32[]{:S(2)}, u32[]{:S(2)}) collective-permute-start(bf16[128,2176]{1,0:T(8,128)(2,1)S(1)} %pad_maximum_fusion.1.refs_0_), channel_id=1, source_target_pairs={{0,2},{1,17},{2,0},{3,19},{4,6},{5,21},{6,4},{7,23},{8,10},{9,25},... | collective-permute-start | bytes 1671176 | tf_op jit(solution)/shard_map/ppermute | solution.py:180
  56.8 13.6 %collective-permute-done.16.refs_2_ = bf16[128,2176]{1,0:T(8,128)(2,1)S(1)} collective-permute-done((bf16[128,2176]{1,0:T(8,128)(2,1)S(1)}, bf16[128,2176]{1,0:T(8,128)(2,1)S(1)}, u32[]{:S(2)}, u32[]{:S(2)}) %collective-permute-start.16) | collective-permute-done | bytes 557088 | tf_op jit(solution)/shard_map/ppermute | solution.py:180
  70.3 0.0 collective-permute-start.18
  70.3 0.0 collective-permute-done.11.refs_1_
  70.4 0.1 collective-permute-start.13
  70.5 0.6 collective-permute-start.14
  71.0 6.0 %collective-permute-done.13.refs_2_ = bf16[64,2176]{1,0:T(8,128)(2,1)S(1)} collective-permute-done((bf16[64,2176]{1,0:T(8,128)(2,1)S(1)}, bf16[64,2176]{1,0:T(8,128)(2,1)S(1)}, u32[]{:S(2)}, u32[]{:S(2)}) %collective-permute-start.13) | collective-permute-done | bytes 278560 | tf_op jit(solution)/shard_map/ppermute | solution.py:180
  77.0 0.0 collective-permute-start.15
  77.0 0.0 collective-permute-done.18.refs_4_
  77.0 0.0 collective-permute-done.17.refs_3_
  77.0 0.0 copy-done.2
  77.0 4.8 %shard_map.75 = (bf16[512,2048]{1,0:T(8,128)(2,1)S(1)}, bf16[512,512]{1,0:T(8,128)(2,1)S(1)}) custom-call(bf16[256,2176]{1,0:T(8,128)(2,1)} %constant_dynamic-update-slice_fusion.refs_0_, bf16[256,2176]{1,0:T(8,128)(2,1)} %collective-permute-done.12.refs_1_, bf16[128,2176]{1,0:T(8,128)(2,1)S(1)} %collective-permute-done.16.refs_2_, ...), custom_call_target="tpu_custom_call" | custom-call | flops 2684354560 | bytes 8388608 | tf_op jit(solution)/shard_map/pallas_call | solution.py:239
  81.8 0.0 collective-permute-done.15.refs_4_
  81.8 0.0 collective-permute-done.14.refs_3_
  81.8 5.8 %shard_map.76 = f32[512,2048]{1,0:T(8,128)} custom-call(bf16[128,2176]{1,0:T(8,128)(2,1)S(1)} %pad_maximum_fusion.1.refs_0_, bf16[128,2176]{1,0:T(8,128)(2,1)S(1)} %collective-permute-done.11.refs_1_, bf16[64,2176]{1,0:T(8,128)(2,1)S(1)} %collective-permute-done.13.refs_2_, bf16[128,2176]{1,0:T(8,128)(2,1)S(1)} %collective-permute-done.14.refs_3_, ...), custom_call_target="tpu_custom_call" | custom-call | flops 3489660928 | bytes 8388608 | tf_op jit(solution)/shard_map/pallas_call | solution.py:249
  (3 shorter events, 0.0 us)
Async XLA Ops:
  1.8 1.8 %collective-permute-start.2 = (bf16[64,2176]{1,0:T(8,128)(2,1)}, bf16[64,2176]{1,0:T(8,128)(2,1)S(1)}, u32[]{:S(2)}, u32[]{:S(2)}) collective-permute-start(bf16[64,2176]{1,0:T(8,128)(2,1)} %shard_map.73), channel_id=1, source_target_pairs={{0,1},{1,0},{2,3},{3,2},{4,5},{5,4},{6,7},{7,6},{8,9},{9,8},{10,11... | collective-permute-start | bytes 835592 | tf_op jit(solution)/shard_map/ppermute | solution.py:180
  3.7 32.8 %copy-start.3 = (bf16[1,256,2048]{2,1,0:T(8,128)(2,1)S(1)}, bf16[1,256,2048]{2,1,0:T(8,128)(2,1)}, u32[]{:S(2)}) copy-start(bf16[1,256,2048]{2,1,0:T(8,128)(2,1)} %param.12) | copy-start | bytes 3145732
  4.8 27.7 %copy-start.4 = (bf16[128,2176]{1,0:T(8,128)(2,1)}, bf16[128,2176]{1,0:T(8,128)(2,1)S(1)}, u32[]{:S(2)}) copy-start(bf16[128,2176]{1,0:T(8,128)(2,1)S(1)} %pad_maximum_fusion.refs_0_) | copy-start | bytes 1671172
  4.8 10.5 %collective-permute-start.3 = (bf16[128,2176]{1,0:T(8,128)(2,1)S(1)}, bf16[128,2176]{1,0:T(8,128)(2,1)}, u32[]{:S(2)}, u32[]{:S(2)}) collective-permute-start(bf16[128,2176]{1,0:T(8,128)(2,1)S(1)} %pad_maximum_fusion.refs_0_), channel_id=1, source_target_pairs={{0,2},{1,17},{2,0},{3,19},{4,6},{5,21},{6,4},{7,23},{8,10},{9,25},... | collective-permute-start | bytes 1671176 | tf_op jit(solution)/shard_map/ppermute | solution.py:180
  7.7 8.9 %collective-permute-start = (bf16[64,2176]{1,0:T(8,128)(2,1)}, bf16[64,2176]{1,0:T(8,128)(2,1)S(1)}, u32[]{:S(2)}, u32[]{:S(2)}) collective-permute-start(bf16[64,2176]{1,0:T(8,128)(2,1)} %shard_map.73), channel_id=1, source_target_pairs={{0,4},{1,5},{2,6},{3,7},{4,0},{5,1},{6,2},{7,3},{8,12},{9,13},{10,... | collective-permute-start | bytes 835592 | tf_op jit(solution)/shard_map/ppermute | solution.py:180
  9.3 15.2 %collective-permute-start.1 = (bf16[64,2176]{1,0:T(8,128)(2,1)}, bf16[64,2176]{1,0:T(8,128)(2,1)S(1)}, u32[]{:S(2)}, u32[]{:S(2)}) collective-permute-start(bf16[64,2176]{1,0:T(8,128)(2,1)} %shard_map.73), channel_id=1, source_target_pairs={{0,12},{1,13},{2,14},{3,15},{4,8},{5,9},{6,10},{7,11},{8,4},{9,5},... | collective-permute-start | bytes 835592 | tf_op jit(solution)/shard_map/ppermute | solution.py:180
  16.3 20.2 %copy-start = (bf16[1,2,256,2048]{3,2,1,0:T(8,128)(2,1)S(1)}, bf16[1,2,256,2048]{3,2,1,0:T(8,128)(2,1)}, u32[]{:S(2)}) copy-start(bf16[1,2,256,2048]{3,2,1,0:T(8,128)(2,1)} %param.11) | copy-start | bytes 6291460
  25.2 2.5 %collective-permute-start.5 = (bf16[64,2176]{1,0:T(8,128)(2,1)S(1)}, bf16[64,2176]{1,0:T(8,128)(2,1)S(1)}, u32[]{:S(2)}, u32[]{:S(2)}) collective-permute-start(bf16[64,2176]{1,0:T(8,128)(2,1)S(1)} %collective-permute-done), channel_id=1, source_target_pairs={{0,1},{1,0},{2,3},{3,2},{4,5},{5,4},{6,7},{7,6},{8,9},{9,8},{10,11... | collective-permute-start | bytes 835592 | tf_op jit(solution)/shard_map/ppermute | solution.py:180
  25.2 6.5 %collective-permute-start.6 = (bf16[64,2176]{1,0:T(8,128)(2,1)S(1)}, bf16[64,2176]{1,0:T(8,128)(2,1)S(1)}, u32[]{:S(2)}, u32[]{:S(2)}) collective-permute-start(bf16[64,2176]{1,0:T(8,128)(2,1)S(1)} %slice.12), channel_id=1, source_target_pairs={{0,16},{1,3},{2,18},{3,1},{4,20},{5,7},{6,22},{7,5},{8,24},{9,11},... | collective-permute-start | bytes 835592 | tf_op jit(solution)/shard_map/ppermute | solution.py:180
  25.7 10.8 %collective-permute-start.8 = (bf16[128,2176]{1,0:T(8,128)(2,1)}, bf16[128,2176]{1,0:T(8,128)(2,1)}, u32[]{:S(2)}, u32[]{:S(2)}) collective-permute-start(bf16[128,2176]{1,0:T(8,128)(2,1)} %collective-permute-done.3.refs_1_), channel_id=1, source_target_pairs={{0,1},{1,0},{2,3},{3,2},{4,5},{5,4},{6,7},{7,6},{8,9},{9,8},{10,11... | collective-permute-start | bytes 1671176 | tf_op jit(solution)/shard_map/ppermute | solution.py:180
  26.9 5.6 %collective-permute-start.7 = (bf16[64,2176]{1,0:T(8,128)(2,1)S(1)}, bf16[64,2176]{1,0:T(8,128)(2,1)S(1)}, u32[]{:S(2)}, u32[]{:S(2)}) collective-permute-start(bf16[64,2176]{1,0:T(8,128)(2,1)S(1)} %collective-permute-done.1), channel_id=1, source_target_pairs={{0,1},{1,0},{2,3},{3,2},{4,5},{5,4},{6,7},{7,6},{8,9},{9,8},{10,11... | collective-permute-start | bytes 835592 | tf_op jit(solution)/shard_map/ppermute | solution.py:180
  33.2 20.5 %collective-permute-start.12 = (bf16[256,2176]{1,0:T(8,128)(2,1)}, bf16[256,2176]{1,0:T(8,128)(2,1)}, u32[]{:S(2)}, u32[]{:S(2)}) collective-permute-start(bf16[256,2176]{1,0:T(8,128)(2,1)} %constant_dynamic-update-slice_fusion.refs_0_), channel_id=1, source_target_pairs={{0,2},{1,17},{2,0},{3,19},{4,6},{5,21},{6,4},{7,23},{8,10},{9,25},... | collective-permute-start | bytes 3342344 | tf_op jit(solution)/shard_map/ppermute | solution.py:180
  34.7 1.8 %collective-permute-start.9 = (bf16[64,2176]{1,0:T(8,128)(2,1)S(1)}, bf16[64,2176]{1,0:T(8,128)(2,1)}, u32[]{:S(2)}, u32[]{:S(2)}) collective-permute-start(bf16[64,2176]{1,0:T(8,128)(2,1)S(1)} %collective-permute-done.6.refs_2_), channel_id=1, source_target_pairs={{0,1},{1,0},{2,3},{3,2},{4,5},{5,4},{6,7},{7,6},{8,9},{9,8},{10,11... | collective-permute-start | bytes 835592 | tf_op jit(solution)/shard_map/ppermute | solution.py:180
  34.7 16.3 %collective-permute-start.4 = (bf16[64,2176]{1,0:T(8,128)(2,1)}, bf16[64,2176]{1,0:T(8,128)(2,1)}, u32[]{:S(2)}, u32[]{:S(2)}) collective-permute-start(bf16[64,2176]{1,0:T(8,128)(2,1)} %shard_map.73), channel_id=1, source_target_pairs={{0,8},{1,9},{2,10},{3,11},{4,12},{5,13},{6,14},{7,15},{8,0},{9,1},... | collective-permute-start | bytes 835592 | tf_op jit(solution)/shard_map/ppermute | solution.py:180
  36.5 1.6 %copy-start.1 = (bf16[1,2,256,2048]{3,2,1,0:T(8,128)(2,1)S(1)}, bf16[1,2,256,2048]{3,2,1,0:T(8,128)(2,1)}, u32[]{:S(2)}) copy-start(bf16[1,2,256,2048]{3,2,1,0:T(8,128)(2,1)} %param.13) | copy-start | bytes 6291460
  38.1 1.1 %copy-start.5 = (bf16[128,2176]{1,0:T(8,128)(2,1)S(1)}, bf16[128,2176]{1,0:T(8,128)(2,1)}, u32[]{:S(2)}) copy-start(bf16[128,2176]{1,0:T(8,128)(2,1)} %copy-done.4) | copy-start | bytes 1671172
  51.0 26.1 %copy-start.2 = (bf16[1,2,256,2048]{3,2,1,0:T(8,128)(2,1)S(1)}, bf16[1,2,256,2048]{3,2,1,0:T(8,128)(2,1)}, u32[]{:S(2)}) copy-start(bf16[1,2,256,2048]{3,2,1,0:T(8,128)(2,1)} %param.13) | copy-start | bytes 6291460
  51.0 1.8 %collective-permute-start.10 = (bf16[64,2176]{1,0:T(8,128)(2,1)}, bf16[64,2176]{1,0:T(8,128)(2,1)S(1)}, u32[]{:S(2)}, u32[]{:S(2)}) collective-permute-start(bf16[64,2176]{1,0:T(8,128)(2,1)} %collective-permute-done.4), channel_id=1, source_target_pairs={{0,1},{1,0},{2,3},{3,2},{4,5},{5,4},{6,7},{7,6},{8,9},{9,8},{10,11... | collective-permute-start | bytes 835592 | tf_op jit(solution)/shard_map/ppermute | solution.py:180
  54.8 15.5 %collective-permute-start.16 = (bf16[128,2176]{1,0:T(8,128)(2,1)S(1)}, bf16[128,2176]{1,0:T(8,128)(2,1)S(1)}, u32[]{:S(2)}, u32[]{:S(2)}) collective-permute-start(bf16[128,2176]{1,0:T(8,128)(2,1)S(1)} %slice.10), channel_id=1, source_target_pairs={{0,16},{1,3},{2,18},{3,1},{4,20},{5,7},{6,22},{7,5},{8,24},{9,11},... | collective-permute-start | bytes 1671176 | tf_op jit(solution)/shard_map/ppermute | solution.py:180
  55.4 21.6 %collective-permute-start.17 = (bf16[256,2176]{1,0:T(8,128)(2,1)}, bf16[256,2176]{1,0:T(8,128)(2,1)S(1)}, u32[]{:S(2)}, u32[]{:S(2)}) collective-permute-start(bf16[256,2176]{1,0:T(8,128)(2,1)} %collective-permute-done.12.refs_1_), channel_id=1, source_target_pairs={{0,1},{1,0},{2,3},{3,2},{4,5},{5,4},{6,7},{7,6},{8,9},{9,8},{10,11... | collective-permute-start | bytes 3342344 | tf_op jit(solution)/shard_map/ppermute | solution.py:180
  55.4 14.9 %collective-permute-start.11 = (bf16[128,2176]{1,0:T(8,128)(2,1)S(1)}, bf16[128,2176]{1,0:T(8,128)(2,1)S(1)}, u32[]{:S(2)}, u32[]{:S(2)}) collective-permute-start(bf16[128,2176]{1,0:T(8,128)(2,1)S(1)} %pad_maximum_fusion.1.refs_0_), channel_id=1, source_target_pairs={{0,2},{1,17},{2,0},{3,19},{4,6},{5,21},{6,4},{7,23},{8,10},{9,25},... | collective-permute-start | bytes 1671176 | tf_op jit(solution)/shard_map/ppermute | solution.py:180
  70.3 6.7 %collective-permute-start.18 = (bf16[128,2176]{1,0:T(8,128)(2,1)S(1)}, bf16[128,2176]{1,0:T(8,128)(2,1)S(1)}, u32[]{:S(2)}, u32[]{:S(2)}) collective-permute-start(bf16[128,2176]{1,0:T(8,128)(2,1)S(1)} %collective-permute-done.16.refs_2_), channel_id=1, source_target_pairs={{0,1},{1,0},{2,3},{3,2},{4,5},{5,4},{6,7},{7,6},{8,9},{9,8},{10,11... | collective-permute-start | bytes 1671176 | tf_op jit(solution)/shard_map/ppermute | solution.py:180
  70.4 6.6 %collective-permute-start.13 = (bf16[64,2176]{1,0:T(8,128)(2,1)S(1)}, bf16[64,2176]{1,0:T(8,128)(2,1)S(1)}, u32[]{:S(2)}, u32[]{:S(2)}) collective-permute-start(bf16[64,2176]{1,0:T(8,128)(2,1)S(1)} %slice.11), channel_id=1, source_target_pairs={{0,16},{1,3},{2,18},{3,1},{4,20},{5,7},{6,22},{7,5},{8,24},{9,11},... | collective-permute-start | bytes 835592 | tf_op jit(solution)/shard_map/ppermute | solution.py:180
  70.5 11.4 %collective-permute-start.14 = (bf16[128,2176]{1,0:T(8,128)(2,1)S(1)}, bf16[128,2176]{1,0:T(8,128)(2,1)S(1)}, u32[]{:S(2)}, u32[]{:S(2)}) collective-permute-start(bf16[128,2176]{1,0:T(8,128)(2,1)S(1)} %collective-permute-done.11.refs_1_), channel_id=1, source_target_pairs={{0,1},{1,0},{2,3},{3,2},{4,5},{5,4},{6,7},{7,6},{8,9},{9,8},{10,11... | collective-permute-start | bytes 1671176 | tf_op jit(solution)/shard_map/ppermute | solution.py:180
  77.0 4.8 %collective-permute-start.15 = (bf16[64,2176]{1,0:T(8,128)(2,1)S(1)}, bf16[64,2176]{1,0:T(8,128)(2,1)S(1)}, u32[]{:S(2)}, u32[]{:S(2)}) collective-permute-start(bf16[64,2176]{1,0:T(8,128)(2,1)S(1)} %collective-permute-done.13.refs_2_), channel_id=1, source_target_pairs={{0,1},{1,0},{2,3},{3,2},{4,5},{5,4},{6,7},{7,6},{8,9},{9,8},{10,11... | collective-permute-start | bytes 835592 | tf_op jit(solution)/shard_map/ppermute | solution.py:180

commit v5 on v3

--- a/solution.py
+++ b/solution.py
@@ -115,9 +115,8 @@
     out_ref[tok_dev:, model_dim:] = jnp.zeros((tok_dev, LANES), jnp.bfloat16)
 
 
-def slice_dirs(pieces, pick_ref, w_ref, v_ref, wo_ref, x_ref, c_ref, wt_ref, tok_dev):
+def unpack(pieces, x_ref, c_ref, wt_ref, tok_dev):
     model_dim = x_ref.shape[1]
-    half = wo_ref.shape[0]
     row = 0
     for piece in pieces:
         for first in range(0, piece.shape[0], 2 * tok_dev):
@@ -126,47 +125,70 @@
             wt_ref[at, :] = piece[first : first + tok_dev, model_dim:]
             c_ref[at, :] = piece[first + tok_dev : first + 2 * tok_dev, 0:model_dim]
             row += tok_dev
-    x = x_ref[...]
-    weight = lax.dot_general(pick_ref[...], wt_ref[...], NT, preferred_element_type=jnp.float32)
-    both = jnp.concatenate([w_ref[...], v_ref[...]], axis=0)
-    seen = lax.dot_general(both, x, NT, preferred_element_type=jnp.float32)
-    back = lax.dot_general(wo_ref[...], c_ref[...], NT, preferred_element_type=jnp.float32)
-    back = back * weight[0:1, :]
+
+
+def gather_kernel(*refs):
+    *parts, out_ref, sems = refs
+    row, copies = 0, []
+    for n, part in enumerate(parts):
+        copies.append(
+            pltpu.make_async_copy(part, out_ref.at[pl.ds(row, part.shape[0])], sems.at[n])
+        )
+        row += part.shape[0]
+    for copy in copies:
+        copy.start()
+    for copy in copies:
+        copy.wait()
+
+
+def unit_dirs(weight, all_ref, x_ref, c_ref, dir_ref):
+    half = all_ref.shape[0] // 5
+    seen = lax.dot_general(
+        all_ref[0 : 4 * half], x_ref[...], NT, preferred_element_type=jnp.float32
+    )
+    back = lax.dot_general(
+        all_ref[4 * half :], c_ref[...], NT, preferred_element_type=jnp.float32
+    )
     parts = [seen[n * half : (n + 1) * half] for n in range(4)]
-    return directions(*parts, back)
-
-
-def slice_kernel(*refs, count, tok_dev):
-    pieces = refs[:count]
-    pick_ref, w_ref, v_ref, wo_ref, x_ref, dir_ref, c_ref, wt_ref = refs[count:]
-    half = wo_ref.shape[0]
-    gate_dir, up_dir = slice_dirs(
-        pieces, pick_ref, w_ref, v_ref, wo_ref, x_ref, c_ref, wt_ref, tok_dev
-    )
+    gate_dir, up_dir = directions(*parts, back * weight)
     dir_ref[0:half, :] = gate_dir
     dir_ref[half:, :] = up_dir
 
 
-def last_kernel(*refs, count, earlier, tok_dev):
+def route_weights(pick_ref, wt_ref):
+    return lax.dot_general(pick_ref[...], wt_ref[...], NT, preferred_element_type=jnp.float32)
+
+
+def both_kernel(*refs, count, tok_dev):
     pieces = refs[:count]
-    held = refs[count : count + 2 * earlier]
-    pick_ref, w_ref, v_ref, wo_ref, out_ref, x_ref, c_ref, wt_ref, dir_ref, sum_ref, sems = refs[
-        count + 2 * earlier :
-    ]
-    half = wo_ref.shape[0]
-    gate_dir, up_dir = slice_dirs(
-        pieces, pick_ref, w_ref, v_ref, wo_ref, x_ref, c_ref, wt_ref, tok_dev
-    )
-    dir_ref[0:half, :] = gate_dir
-    dir_ref[half:, :] = up_dir
-    pairs = [(held[2 * n], held[2 * n + 1]) for n in range(earlier)] + [(x_ref, dir_ref)]
+    pick_ref, mine, other, x_ref, dir_ref, sum_ref, c_ref, wt_ref, other_ref = refs[count:]
+    unpack(pieces, x_ref, c_ref, wt_ref, tok_dev)
+    weight = route_weights(pick_ref, wt_ref)
+    unit_dirs(weight[8:9], other, x_ref, c_ref, other_ref)
+    columns = 512
+    for n in range(x_ref.shape[1] // columns):
+        at = pl.ds(n * columns, columns)
+        sum_ref[:, at] = lax.dot_general(
+            other_ref[...], x_ref[:, at], NN, preferred_element_type=jnp.float32
+        ).astype(jnp.bfloat16)
+    unit_dirs(weight[0:1], mine, x_ref, c_ref, dir_ref)
+
+
+def last_kernel(*refs, count, tok_dev):
+    pieces = refs[:count]
+    early_x, early_dir, add_ref, pick_ref, mine, out_ref = refs[count : count + 6]
+    x_ref, c_ref, wt_ref, dir_ref, sum_ref, sems = refs[count + 6 :]
+    unpack(pieces, x_ref, c_ref, wt_ref, tok_dev)
+    weight = route_weights(pick_ref, wt_ref)
+    unit_dirs(weight[0:1], mine, x_ref, c_ref, dir_ref)
     columns = 512
     copies = []
     for n in range(out_ref.shape[1] // columns):
         at = pl.ds(n * columns, columns)
-        rows = jnp.concatenate([r[:, at] for r, _ in pairs], axis=0)
-        dirs = jnp.concatenate([d[...] for _, d in pairs], axis=1)
-        sum_ref[:, at] = lax.dot_general(dirs, rows, NN, preferred_element_type=jnp.float32)
+        rows = jnp.concatenate([early_x[:, at], x_ref[:, at]], axis=0)
+        dirs = jnp.concatenate([early_dir[...], dir_ref[...]], axis=1)
+        total = lax.dot_general(dirs, rows, NN, preferred_element_type=jnp.float32)
+        sum_ref[:, at] = total + add_ref[:, at].astype(jnp.float32)
         copy = pltpu.make_async_copy(sum_ref.at[:, at], out_ref.at[:, at], sems.at[n])
         copy.start()
         copies.append(copy)
@@ -174,14 +196,18 @@
         copy.wait()
 
 
-def swap(value, masks):
+def swap(value, mask):
     axes = ("dp", "expert")
     count = lax.axis_size("dp") * lax.axis_size("expert")
-    return lax.ppermute(value, axes, [(i, i ^ masks[i & CORE]) for i in range(count)])
+    return lax.ppermute(value, axes, [(i, i ^ mask) for i in range(count)])
 
 
 def after(value, *others):
     return lax.optimization_barrier((value, *others))[0]
+
+
+def tied(values, *others):
+    return list(lax.optimization_barrier((*values, *others)))[: len(values)]
 
 
 def dense(tokens, cotangent, routes, combine, w_in, w_out, v_in):
@@ -197,71 +223,81 @@
         out_shape=jax.ShapeDtypeStruct((2 * tok_dev, wide), jnp.bfloat16),
     )(tokens, cotangent, routes.T, combine.T)
 
-    lane = jnp.arange(LANES, dtype=jnp.int32)
-    mine = (lane % experts == lax.axis_index("expert")) & (lane < 3 * experts)
-    pick = jnp.broadcast_to(mine.astype(jnp.bfloat16)[None, :], (16, LANES))
-
-    slices = [own]
-    for mask in (Z_NEAR, Z_NEAR ^ Z_FAR, Z_FAR):
-        sent = own if len(slices) == 1 else after(own, slices[-1])
-        slices.append(swap(sent, (mask, mask)))
-    weights = (
+    lane = jnp.arange(LANES, dtype=jnp.int32)[None, :]
+    line = jnp.arange(16, dtype=jnp.int32)[:, None]
+    expert = lax.axis_index("expert")
+    wanted = jnp.where(line < 8, expert, expert ^ CORE)
+    pick = ((lane % experts == wanted) & (lane < 3 * experts)).astype(jnp.bfloat16)
+    shards = (
         w_in.reshape(2 * half, model_dim),
         v_in.reshape(2 * half, model_dim),
         w_out.reshape(half, model_dim),
     )
-    held = []
-    for n, block in enumerate(slices):
-        chip = jnp.concatenate([block, swap(block, (CORE, CORE))], axis=0)
-        beside = swap(chip, (X, Y))
-        across = swap(beside[: 2 * tok_dev], (Y, X))
-        pieces = [chip, beside, across]
-        pieces += [swap(got, (CORE, CORE)) for got in (beside, across)]
-        rows = sum(p.shape[0] for p in pieces) // 2
-        last = n == len(slices) - 1
-        scratch = [
+    outside = pl.BlockSpec(memory_space=pl.ANY)
+    mine = pl.pallas_call(
+        gather_kernel,
+        in_specs=[outside] * 3,
+        out_specs=outside,
+        out_shape=jax.ShapeDtypeStruct((5 * half, model_dim), jnp.bfloat16),
+        scratch_shapes=[pltpu.SemaphoreType.DMA((3,))],
+        cost_estimate=pl.CostEstimate(flops=0, bytes_accessed=10 * 2**20, transcendentals=0),
+    )(*shards)
+
+    first = [swap(own, m) for m in (Z_NEAR, X, Y, Z_NEAR ^ Z_FAR, X ^ Y)]
+    near, beside_x, beside_y, middle, across, again, mine = tied([*first, own, mine])
+
+    pair = jnp.concatenate([near, middle], axis=0)
+    second = [swap(again, Z_FAR), swap(pair, X), swap(pair, Y), swap(across, Z_NEAR)]
+    far, pair_x, pair_y, near_across, other = tied([*second, swap(mine, CORE)])
+
+    third = [swap(far, m) for m in (X, Y, X ^ Y)] + [swap(after(across, far), Z_NEAR ^ Z_FAR)]
+    pieces = [own, beside_x, beside_y, across, pair, pair_x, pair_y, near_across, far]
+    rows = sum(p.shape[0] for p in pieces) // 2
+    early_x, early_dir, partial = pl.pallas_call(
+        functools.partial(both_kernel, count=len(pieces), tok_dev=tok_dev),
+        in_specs=[inside] * (len(pieces) + 3),
+        out_specs=[inside] * 3,
+        out_shape=[
+            jax.ShapeDtypeStruct((rows, model_dim), jnp.bfloat16),
+            jax.ShapeDtypeStruct((2 * half, rows), jnp.bfloat16),
+            jax.ShapeDtypeStruct((2 * half, model_dim), jnp.bfloat16),
+        ],
+        scratch_shapes=[
             pltpu.VMEM((rows, model_dim), jnp.bfloat16),
             pltpu.VMEM((rows, LANES), jnp.bfloat16),
-        ]
-        params = pltpu.CompilerParams(vmem_limit_bytes=28 * 2**20)
-        if not last:
-            held += pl.pallas_call(
-                functools.partial(slice_kernel, count=len(pieces), tok_dev=tok_dev),
-                in_specs=[inside] * (len(pieces) + 4),
-                out_specs=[inside] * 2,
-                out_shape=[
-                    jax.ShapeDtypeStruct((rows, model_dim), jnp.bfloat16),
-                    jax.ShapeDtypeStruct((2 * half, rows), jnp.bfloat16),
-                ],
-                scratch_shapes=scratch,
-                compiler_params=params,
-                cost_estimate=pl.CostEstimate(
-                    flops=2 * rows * model_dim * 5 * half,
-                    bytes_accessed=8 * 2**20,
-                    transcendentals=rows * half,
-                ),
-            )(*pieces, pick, *weights)
+            pltpu.VMEM((2 * half, rows), jnp.bfloat16),
+        ],
+        compiler_params=pltpu.CompilerParams(vmem_limit_bytes=14 * 2**20),
+        cost_estimate=pl.CostEstimate(
+            flops=2 * rows * model_dim * 12 * half,
+            bytes_accessed=16 * 2**20,
+            transcendentals=2 * rows * half,
+        ),
+    )(*pieces, pick, mine, other)
+    partial = swap(after(partial, *third), CORE)
+
+    blocks = third + [swap(after(block, early_dir), CORE) for block in third]
+    rows = sum(p.shape[0] for p in blocks) // 2
     out = pl.pallas_call(
-        functools.partial(
-            last_kernel, count=len(pieces), earlier=len(held) // 2, tok_dev=tok_dev
-        ),
-        in_specs=[inside] * (len(pieces) + len(held) + 4),
+        functools.partial(last_kernel, count=len(blocks), tok_dev=tok_dev),
+        in_specs=[inside] * (len(blocks) + 5),
         out_specs=pl.BlockSpec(memory_space=pl.ANY),
         out_shape=jax.ShapeDtypeStruct((2 * half, model_dim), jnp.float32),
-        scratch_shapes=[pltpu.VMEM((rows, model_dim), jnp.bfloat16)]
-        + scratch
-        + [
+        scratch_shapes=[
+            pltpu.VMEM((rows, model_dim), jnp.bfloat16),
+            pltpu.VMEM((rows, model_dim), jnp.bfloat16),
+            pltpu.VMEM((rows, LANES), jnp.bfloat16),
             pltpu.VMEM((2 * half, rows), jnp.bfloat16),
             pltpu.VMEM((2 * half, model_dim), jnp.float32),
             pltpu.SemaphoreType.DMA((model_dim // 512,)),
         ],
-        compiler_params=params,
+        compiler_params=pltpu.CompilerParams(vmem_limit_bytes=14 * 2**20),
         cost_estimate=pl.CostEstimate(
-            flops=2 * rows * model_dim * 13 * half,
+            flops=2 * rows * model_dim * 10 * half,
             bytes_accessed=16 * 2**20,
             transcendentals=rows * half,
         ),
-    )(*pieces, *held, pick, *weights)
+    )(*blocks, early_x, early_dir, partial, pick, mine)
     return out.reshape(1, 2, half, model_dim)
 
 

time: 87 us -> 220 us (2.53)
  Pallas kernels: 16.5 us -> 177 us
  waiting for transfers between devices: 31.6 us -> 17.9 us
  local copies, waits for them, and re-layouts: 11.9 us -> 2.54 us
  starting transfers between devices: 25 us -> 21.6 us
    pallas_call x4 -> x3, Pallas kernels: 14.7 us -> 175 us  [the longest x1 160 us: dense(): pl.pallas_call(gather_kernel, in_specs=[outside] * 3, out_specs=outside,...]
    ppermute x23 -> x19, waiting for transfers between devices: 31.6 us -> 17.9 us  [swap(): return lax.ppermute(value, axes, [(i, i ^ mask) for i in range(count)])]
    unnamed x47 -> x7, local copies, waits for them, and re-layouts: 7.42 us -> 2.51 us
    slice x4 -> x0, local copies, waits for them, and re-layouts: 4.43 us -> none  [dense(): across = swap(beside[:2 * tok_dev], (Y, X))]
    ppermute x23 -> x19, starting transfers between devices: 25 us -> 21.6 us  [swap(): return lax.ppermute(value, axes, [(i, i ^ mask) for i in range(count)])]
  transfers between devices with their start and end apart: 23 -> 19, of which waited for: 8 -> 5; matrix products, arithmetic and copies ran while one was open for 6% -> 0% of each run, Pallas kernels for 9% -> 77%
where the time goes in v5:
time: 220 us; the launch traced here: 219 us
  Pallas kernels  177 us (80%)
  starting transfers between devices  21.6 us (10%)
  waiting for transfers between devices  17.9 us (8%)
  local copies, waits for them, and re-layouts  2.54 us (1%)
    pallas_call x1, Pallas kernels, dense(): pl.pallas_call(gather_kernel, in_specs=[outside] * 3, out_specs=outside,...  160 us
    ppermute x19, starting transfers between devices, swap(): return lax.ppermute(value, axes, [(i, i ^ mask) for i in range(count)])  21.6 us
    ppermute x19, waiting for transfers between devices, swap(): return lax.ppermute(value, axes, [(i, i ^ mask) for i in range(count)])  17.9 us
    pallas_call x1, Pallas kernels, dense(): pl.pallas_call(functools.partial(both_kernel, count=len(pieces), tok_dev=...  9.54 us
    pallas_call x1, Pallas kernels, dense(): pl.pallas_call(functools.partial(last_kernel, count=len(blocks), tok_dev=...  5.85 us
  transfers between devices with their start and end apart: 19, of which 5 were waited for; matrix products, arithmetic and copies ran while one was open for 0% of the time, Pallas kernels for 77%

profile of v5, /device:TPU:0, one launch (start us, length us, event | category | flops | bytes accessed | tf_op | source)
XLA Modules:
  0.0 219.5 jit_solution(11922150248545184962)
XLA Ops:
  0.0 1.8 shard_map.73.refs_0_
  1.8 3.9 %collective-permute-start.4 = (bf16[64,2176]{1,0:T(8,128)(2,1)}, bf16[64,2176]{1,0:T(8,128)(2,1)S(1)}, u32[]{:S(2)}, u32[]{:S(2)}) collective-permute-start(bf16[64,2176]{1,0:T(8,128)(2,1)} %shard_map.73.refs_0_), channel_id=1, source_target_pairs={{0,18},{1,19},{2,16},{3,17},{4,22},{5,23},{6,20},{7,21},{8,26},{9,... | collective-permute-start | bytes 835592 | tf_op jit(solution)/shard_map/ppermute | solution.py:202
  5.7 3.6 %collective-permute-start.3 = (bf16[64,2176]{1,0:T(8,128)(2,1)}, bf16[64,2176]{1,0:T(8,128)(2,1)S(1)}, u32[]{:S(2)}, u32[]{:S(2)}) collective-permute-start(bf16[64,2176]{1,0:T(8,128)(2,1)} %shard_map.73.refs_0_), channel_id=1, source_target_pairs={{0,12},{1,13},{2,14},{3,15},{4,8},{5,9},{6,10},{7,11},{8,4},{9,5},... | collective-permute-start | bytes 835592 | tf_op jit(solution)/shard_map/ppermute | solution.py:202
  9.3 0.5 collective-permute-start.2
  9.8 0.5 collective-permute-start.1
  10.4 0.0 collective-permute-start
  10.4 0.0 copy-start.2
  10.4 159.9 %shard_map.74.refs_10_.refs_12_ = bf16[1280,2048]{1,0:T(8,128)(2,1)} custom-call(bf16[512,2048]{1,0:T(8,128)(2,1)} %bitcast.6, bf16[512,2048]{1,0:T(8,128)(2,1)} %bitcast.7, bf16[256,2048]{1,0:T(8,128)(2,1)} %bitcast.8), custom_call_target="tpu_custom_call" | custom-call | bytes 10485760 | tf_op jit(solution)/shard_map/pallas_call | solution.py:237
  170.3 0.0 collective-permute-done.4.refs_3_
  170.3 0.0 collective-permute-done.3
  170.3 0.0 collective-permute-done.2.refs_2_
  170.4 0.0 collective-permute-done.1.refs_1_
  170.4 0.0 collective-permute-done
  170.4 0.1 collective-permute-start.9
  170.5 1.6 collective-permute-start.7
  172.1 1.5 collective-permute-start.6
  173.6 0.0 copy-done.2
  173.6 0.8 collective-permute-start.5
  174.5 1.3 collective-permute-start.8
  175.8 0.1 and_convert_fusion.refs_9_.refs_11_
  175.9 13.2 %collective-permute-done.5.refs_8_ = bf16[64,2176]{1,0:T(8,128)(2,1)S(1)} collective-permute-done((bf16[64,2176]{1,0:T(8,128)(2,1)S(1)}, bf16[64,2176]{1,0:T(8,128)(2,1)S(1)}, u32[]{:S(2)}, u32[]{:S(2)}) %collective-permute-start.5) | collective-permute-done | bytes 278560 | tf_op jit(solution)/shard_map/ppermute | solution.py:202
  189.1 0.0 collective-permute-done.8.refs_7_
  189.1 0.0 collective-permute-done.7.refs_6_
  189.1 0.0 collective-permute-done.6.refs_5_
  189.1 0.0 collective-permute-done.9.refs_11_
  189.1 0.5 collective-permute-start.12
  189.6 1.5 collective-permute-start.11
  191.2 1.5 collective-permute-start.10
  192.7 3.0 %collective-permute-start.13 = (bf16[64,2176]{1,0:T(8,128)(2,1)S(1)}, bf16[64,2176]{1,0:T(8,128)(2,1)S(1)}, u32[]{:S(2)}, u32[]{:S(2)}) collective-permute-start(bf16[64,2176]{1,0:T(8,128)(2,1)S(1)} %collective-permute-done.4.refs_3_), channel_id=1, source_target_pairs={{0,12},{1,13},{2,14},{3,15},{4,8},{5,9},{6,10},{7,11},{8,4},{9,5},... | collective-permute-start | bytes 835592 | tf_op jit(solution)/shard_map/ppermute | solution.py:202
  195.7 0.0 copy-start
  195.7 2.5 %copy-done = bf16[1280,2048]{1,0:T(8,128)(2,1)S(1)} copy-done((bf16[1280,2048]{1,0:T(8,128)(2,1)S(1)}, bf16[1280,2048]{1,0:T(8,128)(2,1)}, u32[]{:S(2)}) %copy-start) | copy-done | bytes 5242904
  198.2 0.0 copy-start.1
  198.2 9.5 %shard_map.75 = (bf16[384,2048]{1,0:T(8,128)(2,1)S(1)}, bf16[512,384]{1,0:T(8,128)(2,1)S(1)}, bf16[512,2048]{1,0:T(8,128)(2,1)S(1)}) custom-call(bf16[64,2176]{1,0:T(8,128)(2,1)S(1)} %copy-done.2, bf16[64,2176]{1,0:T(8,128)(2,1)S(1)} %collective-permute-done.1.refs_1_, bf16[64,2176]{1,0:T(8,128)(2,1)S(1)} %collective-permute-done.2.refs_2_, ...), custom_call_target="tpu_custom_call" | custom-call | flops 4831838208 | bytes 16777216 | tf_op jit(solution)/shard_map/pallas_call | solution.py:256
  207.7 0.0 collective-permute-done.13.refs_3_
  207.8 0.0 collective-permute-done.12.refs_2_
  207.8 0.0 collective-permute-done.11.refs_1_
  207.8 0.0 collective-permute-done.10.refs_0_
  207.8 0.1 collective-permute-start.18
  207.9 0.5 collective-permute-start.17
  208.4 0.1 collective-permute-start.16
  208.4 0.4 collective-permute-start.15
  208.9 0.1 collective-permute-start.14
  209.0 3.5 %collective-permute-done.17.refs_7_ = bf16[64,2176]{1,0:T(8,128)(2,1)S(1)} collective-permute-done((bf16[64,2176]{1,0:T(8,128)(2,1)S(1)}, bf16[64,2176]{1,0:T(8,128)(2,1)S(1)}, u32[]{:S(2)}, u32[]{:S(2)}) %collective-permute-start.17) | collective-permute-done | bytes 278560 | tf_op jit(solution)/shard_map/ppermute | solution.py:202
  212.4 0.4 collective-permute-done.16.refs_6_
  212.8 0.4 collective-permute-done.15.refs_5_
  213.2 0.4 collective-permute-done.14.refs_4_
  213.6 0.0 collective-permute-done.18.refs_10_
  213.6 0.0 copy-done.1
  213.6 5.9 %shard_map.76 = f32[512,2048]{1,0:T(8,128)} custom-call(bf16[64,2176]{1,0:T(8,128)(2,1)S(1)} %collective-permute-done.10.refs_0_, bf16[64,2176]{1,0:T(8,128)(2,1)S(1)} %collective-permute-done.11.refs_1_, bf16[64,2176]{1,0:T(8,128)(2,1)S(1)} %collective-permute-done.12.refs_2_, bf16[64,2176]{1,0:T(8,128)(2,1)S(1)} %collective-permute-done.13.refs_3_, ...), custom_call_target="tpu_custom_call" | custom-call | flops 2684354560 | bytes 16777216 | tf_op jit(solution)/shard_map/pallas_call | solution.py:281
  (5 shorter events, 0.1 us)
Async XLA Ops:
  1.8 168.5 %collective-permute-start.4 = (bf16[64,2176]{1,0:T(8,128)(2,1)}, bf16[64,2176]{1,0:T(8,128)(2,1)S(1)}, u32[]{:S(2)}, u32[]{:S(2)}) collective-permute-start(bf16[64,2176]{1,0:T(8,128)(2,1)} %shard_map.73.refs_0_), channel_id=1, source_target_pairs={{0,18},{1,19},{2,16},{3,17},{4,22},{5,23},{6,20},{7,21},{8,26},{9,... | collective-permute-start | bytes 835592 | tf_op jit(solution)/shard_map/ppermute | solution.py:202
  5.7 164.6 %collective-permute-start.3 = (bf16[64,2176]{1,0:T(8,128)(2,1)}, bf16[64,2176]{1,0:T(8,128)(2,1)S(1)}, u32[]{:S(2)}, u32[]{:S(2)}) collective-permute-start(bf16[64,2176]{1,0:T(8,128)(2,1)} %shard_map.73.refs_0_), channel_id=1, source_target_pairs={{0,12},{1,13},{2,14},{3,15},{4,8},{5,9},{6,10},{7,11},{8,4},{9,5},... | collective-permute-start | bytes 835592 | tf_op jit(solution)/shard_map/ppermute | solution.py:202
  9.3 161.0 %collective-permute-start.2 = (bf16[64,2176]{1,0:T(8,128)(2,1)}, bf16[64,2176]{1,0:T(8,128)(2,1)S(1)}, u32[]{:S(2)}, u32[]{:S(2)}) collective-permute-start(bf16[64,2176]{1,0:T(8,128)(2,1)} %shard_map.73.refs_0_), channel_id=1, source_target_pairs={{0,16},{1,17},{2,18},{3,19},{4,20},{5,21},{6,22},{7,23},{8,24},{9,... | collective-permute-start | bytes 835592 | tf_op jit(solution)/shard_map/ppermute | solution.py:202
  9.8 160.5 %collective-permute-start.1 = (bf16[64,2176]{1,0:T(8,128)(2,1)}, bf16[64,2176]{1,0:T(8,128)(2,1)S(1)}, u32[]{:S(2)}, u32[]{:S(2)}) collective-permute-start(bf16[64,2176]{1,0:T(8,128)(2,1)} %shard_map.73.refs_0_), channel_id=1, source_target_pairs={{0,2},{1,3},{2,0},{3,1},{4,6},{5,7},{6,4},{7,5},{8,10},{9,11},{10,... | collective-permute-start | bytes 835592 | tf_op jit(solution)/shard_map/ppermute | solution.py:202
  10.4 160.0 %collective-permute-start = (bf16[64,2176]{1,0:T(8,128)(2,1)}, bf16[64,2176]{1,0:T(8,128)(2,1)S(1)}, u32[]{:S(2)}, u32[]{:S(2)}) collective-permute-start(bf16[64,2176]{1,0:T(8,128)(2,1)} %shard_map.73.refs_0_), channel_id=1, source_target_pairs={{0,4},{1,5},{2,6},{3,7},{4,0},{5,1},{6,2},{7,3},{8,12},{9,13},{10,... | collective-permute-start | bytes 835592 | tf_op jit(solution)/shard_map/ppermute | solution.py:202
  10.4 163.2 %copy-start.2 = (bf16[64,2176]{1,0:T(8,128)(2,1)S(1)}, bf16[64,2176]{1,0:T(8,128)(2,1)}, u32[]{:S(2)}) copy-start(bf16[64,2176]{1,0:T(8,128)(2,1)} %shard_map.73.refs_0_) | copy-start | bytes 835588
  170.4 18.7 %collective-permute-start.9 = (bf16[1280,2048]{1,0:T(8,128)(2,1)}, bf16[1280,2048]{1,0:T(8,128)(2,1)}, u32[]{:S(2)}, u32[]{:S(2)}) collective-permute-start(bf16[1280,2048]{1,0:T(8,128)(2,1)} %shard_map.74.refs_10_.refs_12_), channel_id=1, source_target_pairs={{0,1},{1,0},{2,3},{3,2},{4,5},{5,4},{6,7},{7,6},{8,9},{9,8},{10,11... | collective-permute-start | bytes 15728648 | tf_op jit(solution)/shard_map/ppermute | solution.py:202
  170.5 18.6 %collective-permute-start.7 = (bf16[128,2176]{1,0:T(8,128)(2,1)S(1)}, bf16[128,2176]{1,0:T(8,128)(2,1)S(1)}, u32[]{:S(2)}, u32[]{:S(2)}) collective-permute-start(bf16[128,2176]{1,0:T(8,128)(2,1)S(1)} %constant_dynamic-update-slice_fusion.refs_4_), channel_id=1, source_target_pairs={{0,16},{1,17},{2,18},{3,19},{4,20},{5,21},{6,22},{7,23},{8,24},{9,... | collective-permute-start | bytes 1671176 | tf_op jit(solution)/shard_map/ppermute | solution.py:202
  172.1 17.0 %collective-permute-start.6 = (bf16[128,2176]{1,0:T(8,128)(2,1)S(1)}, bf16[128,2176]{1,0:T(8,128)(2,1)S(1)}, u32[]{:S(2)}, u32[]{:S(2)}) collective-permute-start(bf16[128,2176]{1,0:T(8,128)(2,1)S(1)} %constant_dynamic-update-slice_fusion.refs_4_), channel_id=1, source_target_pairs={{0,2},{1,3},{2,0},{3,1},{4,6},{5,7},{6,4},{7,5},{8,10},{9,11},{10,... | collective-permute-start | bytes 1671176 | tf_op jit(solution)/shard_map/ppermute | solution.py:202
  173.6 15.5 %collective-permute-start.5 = (bf16[64,2176]{1,0:T(8,128)(2,1)S(1)}, bf16[64,2176]{1,0:T(8,128)(2,1)S(1)}, u32[]{:S(2)}, u32[]{:S(2)}) collective-permute-start(bf16[64,2176]{1,0:T(8,128)(2,1)S(1)} %copy-done.2), channel_id=1, source_target_pairs={{0,8},{1,9},{2,10},{3,11},{4,12},{5,13},{6,14},{7,15},{8,0},{9,1},... | collective-permute-start | bytes 835592 | tf_op jit(solution)/shard_map/ppermute | solution.py:202
  174.5 14.6 %collective-permute-start.8 = (bf16[64,2176]{1,0:T(8,128)(2,1)S(1)}, bf16[64,2176]{1,0:T(8,128)(2,1)S(1)}, u32[]{:S(2)}, u32[]{:S(2)}) collective-permute-start(bf16[64,2176]{1,0:T(8,128)(2,1)S(1)} %collective-permute-done.4.refs_3_), channel_id=1, source_target_pairs={{0,4},{1,5},{2,6},{3,7},{4,0},{5,1},{6,2},{7,3},{8,12},{9,13},{10,... | collective-permute-start | bytes 835592 | tf_op jit(solution)/shard_map/ppermute | solution.py:202
  189.1 18.7 %collective-permute-start.12 = (bf16[64,2176]{1,0:T(8,128)(2,1)S(1)}, bf16[64,2176]{1,0:T(8,128)(2,1)S(1)}, u32[]{:S(2)}, u32[]{:S(2)}) collective-permute-start(bf16[64,2176]{1,0:T(8,128)(2,1)S(1)} %collective-permute-done.5.refs_8_), channel_id=1, source_target_pairs={{0,18},{1,19},{2,16},{3,17},{4,22},{5,23},{6,20},{7,21},{8,26},{9,... | collective-permute-start | bytes 835592 | tf_op jit(solution)/shard_map/ppermute | solution.py:202
  189.6 18.1 %collective-permute-start.11 = (bf16[64,2176]{1,0:T(8,128)(2,1)S(1)}, bf16[64,2176]{1,0:T(8,128)(2,1)S(1)}, u32[]{:S(2)}, u32[]{:S(2)}) collective-permute-start(bf16[64,2176]{1,0:T(8,128)(2,1)S(1)} %collective-permute-done.5.refs_8_), channel_id=1, source_target_pairs={{0,16},{1,17},{2,18},{3,19},{4,20},{5,21},{6,22},{7,23},{8,24},{9,... | collective-permute-start | bytes 835592 | tf_op jit(solution)/shard_map/ppermute | solution.py:202
  191.2 16.6 %collective-permute-start.10 = (bf16[64,2176]{1,0:T(8,128)(2,1)S(1)}, bf16[64,2176]{1,0:T(8,128)(2,1)S(1)}, u32[]{:S(2)}, u32[]{:S(2)}) collective-permute-start(bf16[64,2176]{1,0:T(8,128)(2,1)S(1)} %collective-permute-done.5.refs_8_), channel_id=1, source_target_pairs={{0,2},{1,3},{2,0},{3,1},{4,6},{5,7},{6,4},{7,5},{8,10},{9,11},{10,... | collective-permute-start | bytes 835592 | tf_op jit(solution)/shard_map/ppermute | solution.py:202
  192.7 15.1 %collective-permute-start.13 = (bf16[64,2176]{1,0:T(8,128)(2,1)S(1)}, bf16[64,2176]{1,0:T(8,128)(2,1)S(1)}, u32[]{:S(2)}, u32[]{:S(2)}) collective-permute-start(bf16[64,2176]{1,0:T(8,128)(2,1)S(1)} %collective-permute-done.4.refs_3_), channel_id=1, source_target_pairs={{0,12},{1,13},{2,14},{3,15},{4,8},{5,9},{6,10},{7,11},{8,4},{9,5},... | collective-permute-start | bytes 835592 | tf_op jit(solution)/shard_map/ppermute | solution.py:202
  195.7 2.5 %copy-start = (bf16[1280,2048]{1,0:T(8,128)(2,1)S(1)}, bf16[1280,2048]{1,0:T(8,128)(2,1)}, u32[]{:S(2)}) copy-start(bf16[1280,2048]{1,0:T(8,128)(2,1)} %shard_map.74.refs_10_.refs_12_) | copy-start | bytes 15728644
  198.2 15.4 %copy-start.1 = (bf16[1280,2048]{1,0:T(8,128)(2,1)S(1)}, bf16[1280,2048]{1,0:T(8,128)(2,1)}, u32[]{:S(2)}) copy-start(bf16[1280,2048]{1,0:T(8,128)(2,1)} %shard_map.74.refs_10_.refs_12_) | copy-start | bytes 15728644
  207.8 5.8 %collective-permute-start.18 = (bf16[512,2048]{1,0:T(8,128)(2,1)S(1)}, bf16[512,2048]{1,0:T(8,128)(2,1)S(1)}, u32[]{:S(2)}, u32[]{:S(2)}) collective-permute-start(bf16[512,2048]{1,0:T(8,128)(2,1)S(1)} %get-tuple-element.46), channel_id=1, source_target_pairs={{0,1},{1,0},{2,3},{3,2},{4,5},{5,4},{6,7},{7,6},{8,9},{9,8},{10,11... | collective-permute-start | bytes 6291464 | tf_op jit(solution)/shard_map/ppermute | solution.py:202
  207.9 4.5 %collective-permute-start.17 = (bf16[64,2176]{1,0:T(8,128)(2,1)S(1)}, bf16[64,2176]{1,0:T(8,128)(2,1)S(1)}, u32[]{:S(2)}, u32[]{:S(2)}) collective-permute-start(bf16[64,2176]{1,0:T(8,128)(2,1)S(1)} %collective-permute-done.13.refs_3_), channel_id=1, source_target_pairs={{0,1},{1,0},{2,3},{3,2},{4,5},{5,4},{6,7},{7,6},{8,9},{9,8},{10,11... | collective-permute-start | bytes 835592 | tf_op jit(solution)/shard_map/ppermute | solution.py:202
  208.4 4.4 %collective-permute-start.16 = (bf16[64,2176]{1,0:T(8,128)(2,1)S(1)}, bf16[64,2176]{1,0:T(8,128)(2,1)S(1)}, u32[]{:S(2)}, u32[]{:S(2)}) collective-permute-start(bf16[64,2176]{1,0:T(8,128)(2,1)S(1)} %collective-permute-done.12.refs_2_), channel_id=1, source_target_pairs={{0,1},{1,0},{2,3},{3,2},{4,5},{5,4},{6,7},{7,6},{8,9},{9,8},{10,11... | collective-permute-start | bytes 835592 | tf_op jit(solution)/shard_map/ppermute | solution.py:202
  208.4 4.8 %collective-permute-start.15 = (bf16[64,2176]{1,0:T(8,128)(2,1)S(1)}, bf16[64,2176]{1,0:T(8,128)(2,1)S(1)}, u32[]{:S(2)}, u32[]{:S(2)}) collective-permute-start(bf16[64,2176]{1,0:T(8,128)(2,1)S(1)} %collective-permute-done.11.refs_1_), channel_id=1, source_target_pairs={{0,1},{1,0},{2,3},{3,2},{4,5},{5,4},{6,7},{7,6},{8,9},{9,8},{10,11... | collective-permute-start | bytes 835592 | tf_op jit(solution)/shard_map/ppermute | solution.py:202
  208.9 4.7 %collective-permute-start.14 = (bf16[64,2176]{1,0:T(8,128)(2,1)S(1)}, bf16[64,2176]{1,0:T(8,128)(2,1)S(1)}, u32[]{:S(2)}, u32[]{:S(2)}) collective-permute-start(bf16[64,2176]{1,0:T(8,128)(2,1)S(1)} %collective-permute-done.10.refs_0_), channel_id=1, source_target_pairs={{0,1},{1,0},{2,3},{3,2},{4,5},{5,4},{6,7},{7,6},{8,9},{9,8},{10,11... | collective-permute-start | bytes 835592 | tf_op jit(solution)/shard_map/ppermute | solution.py:202
